TPU v7x, 32 devices: a whole 2x2x4 slice. The times are simulated.
32 devices in a mesh: seq: 8 (over z, core), fsdp: 4 (over y, x).
Axes of the slice: x: 2, y: 2, z: 4, core: 2. Of those that a mesh axis runs over, the one named last changes fastest.
Arguments:
- queries: bfloat16 [4, 2048, 4096], P('fsdp', 'seq'), may hold values from -60 to 60
- keys: bfloat16 [4, 2048, 4096], P('fsdp', 'seq'), may hold values from -4.8 to 4.8
- values: bfloat16 [4, 2048, 4096], P('fsdp', 'seq'), may hold values from -6 to 6
- out_weight: bfloat16 [4096, 3072], P(('seq', 'fsdp')), may hold values from -0.75 to 0.75
- block_lists: int32 [4, 32, 16, 8], P('fsdp'), may hold values from 0 to 15, as said below
- block_counts: int32 [4, 32, 16], P('fsdp'), may hold values from 1 to 8, as said below
Outputs:
- projected: bfloat16 [4, 2048, 3072], P('fsdp', 'seq')
Inputs may be any that keep to these rules, and one draw needn't show every extreme that they name: `block_lists`: entry j = 0 of every list is the query block itself; the 8 entries of a list are distinct blocks; entries at slots j >= block_counts are ignored. `block_counts`: in every sequence some head and query block has 8 live slots.
All inputs are finite; a program needn't handle non-finite values.
Results may differ from a plain program's by a relative error of at most 0.0085.
Values may be sent and summed in bfloat16 or wider, within the bound.
No kernel may reach another device: no remote copies, remote signals or barrier semaphores. Data moves between devices by JAX's collectives and lax.ppermute only.
A program may use at most 128 MiB of HBM per device.

v0:
```python
import jax
import jax.numpy as jnp
from jax import lax
from jax.sharding import PartitionSpec as P


def attend_head(query_rows, key_rows, value_rows, block_ids, live_counts):
    block_total = live_counts.shape[0]
    head_width = query_rows.shape[1]
    block_size = query_rows.shape[0] // block_total
    query_blocks = query_rows.reshape(block_total, block_size, head_width)
    key_blocks = key_rows.reshape(block_total, block_size, head_width)
    value_blocks = value_rows.reshape(block_total, block_size, head_width)
    factor = head_width ** (-0.5)

    def advance(column, carry):
        running, denom_sum, accumulated = carry
        picked = block_ids[:, column]
        key_tile = key_blocks[picked]
        value_tile = value_blocks[picked]
        scores = (
            jnp.einsum("qpd,qkd->qpk", query_blocks, key_tile, preferred_element_type=jnp.float32)
            * factor
        )
        usable = (column < live_counts)[:, None, None]
        scores = jnp.where(usable, scores, -jnp.inf)
        updated = jnp.maximum(running, jnp.max(scores, axis=2))
        rescale = jnp.exp(running - updated)
        weights = jnp.exp(scores - updated[:, :, None])
        denom_sum = denom_sum * rescale + jnp.sum(weights, axis=2)
        accumulated = accumulated * rescale[:, :, None] + jnp.einsum(
            "qpk,qkd->qpd",
            weights.astype(jnp.bfloat16),
            value_tile,
            preferred_element_type=jnp.float32,
        )
        return (updated, denom_sum, accumulated)

    initial = (
        jnp.full((block_total, block_size), -jnp.inf, jnp.float32),
        jnp.zeros((block_total, block_size), jnp.float32),
        jnp.zeros((block_total, block_size, head_width), jnp.float32),
    )
    trip_count = jnp.max(live_counts)
    running, denom_sum, accumulated = lax.fori_loop(0, trip_count, advance, initial)
    return (accumulated / denom_sum[:, :, None]).astype(jnp.bfloat16).reshape(-1, head_width)


def shards(queries, keys, values, out_weight, block_lists, block_counts):
    groups = lax.axis_size("seq")
    rank_here = lax.axis_index("seq")
    head_count = block_counts.shape[1]
    head_width = queries.shape[2] // head_count
    heads_here = head_count // groups
    local_query = queries[0]
    local_key = keys[0]
    local_value = values[0]
    lists_here = block_lists[0]
    counts_here = block_counts[0]
    chosen = jnp.arange(head_count, dtype=jnp.int32)
    head_query, head_key, head_value = (
        lax.all_to_all(local_query, "seq", split_axis=1, concat_axis=0, tiled=True),
        lax.all_to_all(local_key, "seq", split_axis=1, concat_axis=0, tiled=True),
        lax.all_to_all(local_value, "seq", split_axis=1, concat_axis=0, tiled=True),
    )
    mine = lax.dynamic_slice_in_dim(chosen, rank_here * heads_here, heads_here)
    my_lists = jnp.take(lists_here, mine, axis=0)
    my_counts = jnp.take(counts_here, mine, axis=0)
    outputs = []
    for member in range(heads_here):
        lower = member * head_width
        upper = lower + head_width
        outputs.append(
            attend_head(
                head_query[:, lower:upper],
                head_key[:, lower:upper],
                head_value[:, lower:upper],
                my_lists[member],
                my_counts[member],
            )
        )
    attended = jnp.concatenate(outputs, axis=1)
    returned = lax.all_to_all(attended, "seq", split_axis=0, concat_axis=1, tiled=True)
    result = jnp.dot(
        returned,
        lax.all_gather(out_weight, ("seq", "fsdp"), axis=0, tiled=True),
        preferred_element_type=jnp.float32,
    )
    return result.astype(jnp.bfloat16)[None]


def solution(mesh):
    return jax.shard_map(
        shards,
        mesh=mesh,
        in_specs=(
            P("fsdp", "seq", None),
            P("fsdp", "seq", None),
            P("fsdp", "seq", None),
            P(("seq", "fsdp"), None),
            P("fsdp", None, None, None),
            P("fsdp", None, None),
        ),
        out_specs=P("fsdp", "seq", None),
        check_vma=False,
    )
```

profile of v0, /device:TPU:0, one launch (start us, length us, event | category | flops | bytes accessed | tf_op | source)
XLA Modules:
  0.0 531.4 jit_solution(12296706212219712028)
XLA Ops:
  7.3 3.3 copy.47
  10.5 2.4 copy.48
  12.9 6.3 %all-to-all-start = ((bf16[256,8,512]{2,0,1:T(8,128)(2,1)}), bf16[256,8,512]{2,0,1:T(8,128)(2,1)S(1)}, u32[]{:S(2)}, u32[]{:S(2)}) async-start(bf16[256,8,512]{2,0,1:T(8,128)(2,1)} %copy.48), calls=%async_computation | async-start | bytes 4194304 | tf_op jit(solution)/shard_map/all_to_all | solution.py:63
  19.3 4.2 copy.49
  23.4 3.9 copy.50
  27.4 85.5 %all-to-all-done = bf16[256,8,512]{2,0,1:T(8,128)(2,1)S(1)} async-done(((bf16[256,8,512]{2,0,1:T(8,128)(2,1)}), bf16[256,8,512]{2,0,1:T(8,128)(2,1)S(1)}, u32[]{:S(2)}, u32[]{:S(2)}) %all-to-all-start) | async-done | bytes 2097184 | tf_op jit(solution)/shard_map/all_to_all | solution.py:63
  112.9 4.4 all-to-all-start.1
  117.2 4.1 copy.51
  121.3 3.9 copy.52
  125.3 91.7 %all-to-all-done.1 = bf16[256,8,512]{2,0,1:T(8,128)(2,1)} async-done(((bf16[256,8,512]{2,0,1:T(8,128)(2,1)}), bf16[256,8,512]{2,0,1:T(8,128)(2,1)}, u32[]{:S(2)}, u32[]{:S(2)}) %all-to-all-start.1) | async-done | bytes 2097184 | tf_op jit(solution)/shard_map/all_to_all | solution.py:62
  217.0 5.1 all-to-all-start.2
  225.9 2.9 fusion.34
  228.8 49.8 %all-to-all-done.2 = bf16[256,8,512]{2,0,1:T(8,128)(2,1)} async-done(((bf16[256,8,512]{2,0,1:T(8,128)(2,1)}), bf16[256,8,512]{2,0,1:T(8,128)(2,1)}, u32[]{:S(2)}, u32[]{:S(2)}) %all-to-all-start.2) | async-done | bytes 2097184 | tf_op jit(solution)/shard_map/all_to_all | solution.py:64
  278.6 2.9 fusion.33
  281.7 20.0 %while.56 = (s32[]{:T(128)}, f32[16,128]{1,0:T(8,128)S(1)}, f32[16,128]{1,0:T(8,128)S(1)}, f32[16,128,128]{2,1,0:T(8,128)S(1)}, s32[]{:T(128)}, /*index=5*/s32[1...) while((s32[]{:T(128)}, f32[16,128]{1,0:T(8,128)S(1)}, ...), condition=%wide.region_4.5_spmd, body=%wide.region_1.0_spmd.sunk | while | flops 136582208 | bytes 9048647 | solution.py:45
  282.3 1.7 gather_fusion
  285.7 1.7 gather_fusion.1
  288.8 1.7 gather_fusion
  290.5 1.5 fusion.83
  292.2 1.7 gather_fusion.1
  295.2 1.7 gather_fusion
  298.7 1.7 gather_fusion.1
  303.0 39.3 %while.57 = (s32[]{:T(128)}, f32[16,128]{1,0:T(8,128)S(1)}, f32[16,128]{1,0:T(8,128)S(1)}, f32[16,128,128]{2,1,0:T(8,128)S(1)}, s32[]{:T(128)}, /*index=5*/s32[1...) while((s32[]{:T(128)}, f32[16,128]{1,0:T(8,128)S(1)}, ...), condition=%wide.region_9.10_spmd, body=%wide.region_6.9_spmd.sunk | while | flops 136582208 | bytes 9048647 | solution.py:45
  303.6 1.7 gather_fusion.2
  305.3 1.5 fusion.90
  307.0 1.7 gather_fusion.3
  310.1 1.7 gather_fusion.2
  311.8 1.5 fusion.90
  313.5 1.7 gather_fusion.3
  316.5 1.7 gather_fusion.2
  320.0 1.7 gather_fusion.3
  323.0 1.7 gather_fusion.2
  326.4 1.7 gather_fusion.3
  329.4 1.7 gather_fusion.2
  331.1 1.5 fusion.90
  332.9 1.7 gather_fusion.3
  335.9 1.7 gather_fusion.2
  339.3 1.7 gather_fusion.3
  343.7 13.7 %while.58 = (s32[]{:T(128)}, f32[16,128]{1,0:T(8,128)S(1)}, f32[16,128]{1,0:T(8,128)S(1)}, f32[16,128,128]{2,1,0:T(8,128)S(1)}, s32[]{:T(128)}, /*index=5*/s32[1...) while((s32[]{:T(128)}, f32[16,128]{1,0:T(8,128)S(1)}, ...), condition=%wide.region_14.15_spmd, body=%wide.region_11.14_spmd.sunk | while | flops 136582208 | bytes 9048647 | solution.py:45
  344.3 1.7 gather_fusion.4
  347.8 1.7 gather_fusion.5
  350.9 1.7 gather_fusion.4
  354.3 1.7 gather_fusion.5
  358.7 44.6 %while.59 = (s32[]{:T(128)}, f32[16,128]{1,0:T(8,128)S(1)}, f32[16,128]{1,0:T(8,128)S(1)}, f32[16,128,128]{2,1,0:T(8,128)S(1)}, s32[]{:T(128)}, /*index=5*/s32[1...) while((s32[]{:T(128)}, f32[16,128]{1,0:T(8,128)S(1)}, ...), condition=%wide.region_19.20_spmd, body=%wide.region_16.19_spmd.sunk | while | flops 136582208 | bytes 9048647 | solution.py:45
  359.3 1.7 gather_fusion.6
  361.7 1.7 gather_fusion.7
  364.8 1.7 gather_fusion.6
  367.2 1.7 gather_fusion.7
  370.3 1.7 gather_fusion.6
  372.7 1.7 gather_fusion.7
  375.8 1.7 gather_fusion.6
  378.2 1.7 gather_fusion.7
  381.3 1.7 gather_fusion.6
  383.7 1.7 gather_fusion.7
  386.8 1.7 gather_fusion.6
  389.2 1.7 gather_fusion.7
  392.3 1.7 gather_fusion.6
  394.7 1.7 gather_fusion.7
  397.8 1.7 gather_fusion.6
  400.2 1.7 gather_fusion.7
  403.6 1.6 pad_maximum_fusion
  405.3 103.4 %all_to_all.73 = bf16[8,256,512]{2,1,0:T(8,128)(2,1)} all-to-all(bf16[8,256,512]{2,1,0:T(8,128)(2,1)S(1)} %pad_maximum_fusion), channel_id=1, replica_groups=mesh['seq'=8,'fsdp'=4] {'seq'}, dimensions={0} | all-to-all | bytes 4194304 | tf_op jit(solution)/shard_map/all_to_all | solution.py:83
  508.7 2.8 copy.53
  511.6 13.0 %fusion.28 = bf16[1,256,3072]{2,1,0:T(8,128)(2,1)} fusion(bf16[256,4096]{0,1:T(8,128)(2,1)S(1)} %bitcast.120, bf16[4096,3072]{1,0:T(8,128)(2,1)} %all-gather.2.cloned.1.call-done), kind=kOutput, calls=%fused_computation.67 | convolution fusion | flops 6443237376 | bytes 28835840 | tf_op jit(solution)/shard_map/dot_general | solution.py:84
  (202 shorter events, 40.6 us)
Async XLA Ops:
  6.5 505.0 %all-gather.2.cloned.1.call-start = ((), (), s32[]{:S(2)}) async-start(), calls=%async_computation.4 | async-start | bytes 25952256 | tf_op jit(solution)/shard_map/all_gather | solution.py:86
  12.9 99.9 %all-to-all-start = ((bf16[256,8,512]{2,0,1:T(8,128)(2,1)}), bf16[256,8,512]{2,0,1:T(8,128)(2,1)S(1)}, u32[]{:S(2)}, u32[]{:S(2)}) async-start(bf16[256,8,512]{2,0,1:T(8,128)(2,1)} %copy.48), calls=%async_computation | async-start | bytes 4194304 | tf_op jit(solution)/shard_map/all_to_all | solution.py:63
  112.9 104.1 %all-to-all-start.1 = ((bf16[256,8,512]{2,0,1:T(8,128)(2,1)}), bf16[256,8,512]{2,0,1:T(8,128)(2,1)}, u32[]{:S(2)}, u32[]{:S(2)}) async-start(bf16[256,8,512]{2,0,1:T(8,128)(2,1)} %copy.50), calls=%async_computation.1 | async-start | bytes 4194304 | tf_op jit(solution)/shard_map/all_to_all | solution.py:62
  125.3 96.9 %copy-start.1 = (s32[1,32,16]{1,2,0:T(8,128)S(1)}, s32[1,32,16]{1,2,0:T(8,128)}, u32[]{:S(2)}) copy-start(s32[1,32,16]{1,2,0:T(8,128)} %param.19) | copy-start | bytes 6148
  125.3 96.9 %copy-start = (s32[1,32,16,8]{1,3,2,0:T(8,128)S(1)}, s32[1,32,16,8]{1,3,2,0:T(8,128)}, u32[]{:S(2)}) copy-start(s32[1,32,16,8]{1,3,2,0:T(8,128)} %param.18) | copy-start | bytes 49156
  217.0 61.7 %all-to-all-start.2 = ((bf16[256,8,512]{2,0,1:T(8,128)(2,1)}), bf16[256,8,512]{2,0,1:T(8,128)(2,1)}, u32[]{:S(2)}, u32[]{:S(2)}) async-start(bf16[256,8,512]{2,0,1:T(8,128)(2,1)} %copy.52), calls=%async_computation.2 | async-start | bytes 4194304 | tf_op jit(solution)/shard_map/all_to_all | solution.py:64
Sparse Core Ops, SparseCore 0:
  10.2 256.1 all-gather.1
where the time goes:
time: 529 us; the launch traced here: 531 us
  waiting for transfers between devices  228 us (43%)
  blocking collectives  103 us (19%)
  local copies, waits for them, and re-layouts  97.9 us (19%)
  matrix products  47.1 us (9%)
  starting transfers between devices  15.8 us (3%)
  loops' own time  15.5 us (3%)
  between operations  13.6 us (3%)
  other arithmetic  10.2 us (2%)
    all_to_all x1, blocking collectives, shards(): lax.all_to_all(attended, 'seq', split_axis=0, concat_axis=1, tiled=True)  103 us
    all_to_all x1, waiting for transfers between devices, shards(): lax.all_to_all(local_query, 'seq', split_axis=1, concat_axis=0, tiled=True)  91.7 us
    all_to_all x1, waiting for transfers between devices, shards(): lax.all_to_all(local_key, 'seq', split_axis=1, concat_axis=0, tiled=True)  85.5 us
    all_to_all x1, waiting for transfers between devices, shards(): lax.all_to_all(local_value, 'seq', split_axis=1, concat_axis=0, tiled=True)  49.8 us
    gather x19, local copies, waits for them, and re-layouts, advance(): key_tile = key_blocks[picked]  32.1 us
    gather x19, local copies, waits for them, and re-layouts, advance(): value_tile = value_blocks[picked]  32.1 us
    dot_general x19, matrix products, advance(): jnp.einsum('qpd,qkd->qpk', query_blocks, key_tile, preferred_element_type...  20.7 us
    another operation x4, loops' own time, attend_head(): lax.fori_loop(0, trip_count, advance, initial)  15.5 us
  transfers between devices with their start and end apart: 4, of which 3 were waited for; matrix products, arithmetic and copies ran while one was open for 27% of the time, Pallas kernels for 0%

commit v1 on v0

v1 whole, which is shorter than its diff:
```python
import functools
import math

import jax
import jax.numpy as jnp
from jax import lax
from jax.experimental import pallas as pl
from jax.experimental.pallas import tpu as pltpu
from jax.sharding import PartitionSpec as P

BLOCK = 128


def attend_kernel(base, width, slots, lists_ref, counts_ref, qkv_ref, out_ref):
    sources, tokens, lanes = qkv_ref.shape
    heads = lanes // (3 * width)
    per = tokens // BLOCK
    blocks = sources * per
    scale = width ** (-0.5) * math.log2(math.e)

    def rows_of(block):
        return block // per, pl.ds(pl.multiple_of((block % per) * BLOCK, BLOCK), BLOCK)

    for member in range(heads):
        q_cols = slice(member * width, (member + 1) * width)
        k_cols = slice((heads + member) * width, (heads + member + 1) * width)
        v_cols = slice((2 * heads + member) * width, (2 * heads + member + 1) * width)

        def one(i, carry, member=member, q_cols=q_cols, k_cols=k_cols, v_cols=v_cols):
            live = counts_ref[base + member, i]
            src, rows = rows_of(i)

            def branch(pairs):
                picked = [rows_of(lists_ref[base + member, i * slots + j]) for j in range(2 * pairs)]
                q = qkv_ref[src, rows, q_cols]
                scores = []
                for n in range(pairs):
                    k = jnp.concatenate([qkv_ref[s, r, k_cols] for s, r in picked[2 * n : 2 * n + 2]], axis=0)
                    scores.append(lax.dot_general(q, k, (((1,), (1,)), ((), ())), preferred_element_type=jnp.float32))
                second = lax.broadcasted_iota(jnp.int32, scores[-1].shape, 1) < BLOCK * (live - 2 * (pairs - 1))
                scores[-1] = jnp.where(second, scores[-1], -jnp.inf)
                top = functools.reduce(jnp.maximum, scores)
                top = jnp.max(top, axis=1, keepdims=True) * scale
                total = None
                mixed = None
                for n in range(pairs):
                    weights = jnp.exp2(scores[n] * scale - top)
                    v = jnp.concatenate([qkv_ref[s, r, v_cols] for s, r in picked[2 * n : 2 * n + 2]], axis=0)
                    part = jnp.dot(weights.astype(jnp.bfloat16), v, preferred_element_type=jnp.float32)
                    total = weights if total is None else total + weights
                    mixed = part if mixed is None else mixed + part
                totals = jnp.sum(total, axis=1, keepdims=True)
                out_ref[src, rows, q_cols] = (mixed / totals).astype(out_ref.dtype)

            for pairs in range(1, slots // 2 + 1):
                pl.when((live + 1) // 2 == pairs)(functools.partial(branch, pairs))
            return carry

        lax.fori_loop(0, blocks, one, 0)


def attend(qkv, lists, counts, base, width):
    sources, tokens, lanes = qkv.shape
    slots = lists.shape[1] // counts.shape[1]
    smem = pl.BlockSpec(memory_space=pltpu.SMEM)
    vmem = pl.BlockSpec(memory_space=pltpu.VMEM)
    flops = 4 * (sources * tokens) * (slots * BLOCK // 2) * (lanes // 3)
    return pl.pallas_call(
        functools.partial(attend_kernel, base, width, slots),
        out_shape=jax.ShapeDtypeStruct((sources, tokens, lanes // 3), jnp.bfloat16),
        in_specs=[smem, smem, vmem],
        out_specs=vmem,
        compiler_params=pltpu.CompilerParams(vmem_limit_bytes=32 * 1024 * 1024),
        cost_estimate=pl.CostEstimate(flops=flops, bytes_accessed=qkv.size * 2, transcendentals=flops // 512),
    )(lists, counts, qkv)


def shards(queries, keys, values, out_weight, block_lists, block_counts):
    groups = lax.axis_size("seq")
    rank = lax.axis_index("seq")
    head_count = block_counts.shape[1]
    blocks = block_counts.shape[2]
    width = queries.shape[2] // head_count
    here = head_count // groups
    tokens = queries.shape[1]
    lists = lax.dynamic_slice_in_dim(block_lists[0], rank * here, here).reshape(here, -1)
    counts = lax.dynamic_slice_in_dim(block_counts[0], rank * here, here)

    fields = [x[0].reshape(tokens, groups, here, width) for x in (queries, keys, values)]
    weights = lax.all_gather(out_weight, ("fsdp", "seq"), axis=0, tiled=True)
    rows = out_weight.shape[0]
    per_head = width // rows

    result = None
    for member in range(here):
        mine = jnp.concatenate([f[:, :, member].transpose(1, 0, 2) for f in fields], axis=2)
        qkv = lax.all_to_all(mine, "seq", split_axis=0, concat_axis=0, tiled=True)
        out = attend(qkv, lists, counts, member, width)
        back = lax.all_to_all(out, "seq", split_axis=0, concat_axis=0, tiled=True)
        back = back.reshape(groups, tokens, per_head, rows).transpose(1, 2, 0, 3).reshape(tokens, groups * width)
        part = jnp.dot(
            back,
            weights[member * groups * width : (member + 1) * groups * width],
            preferred_element_type=jnp.float32,
        )
        result = part if result is None else result + part
    return result.astype(jnp.bfloat16)[None]


def solution(mesh):
    return jax.shard_map(
        shards,
        mesh=mesh,
        in_specs=(
            P("fsdp", "seq", None),
            P("fsdp", "seq", None),
            P("fsdp", "seq", None),
            P(("seq", "fsdp"), None),
            P("fsdp", None, None, None),
            P("fsdp", None, None),
        ),
        out_specs=P("fsdp", "seq", None),
        check_vma=False,
    )
```

time: 529 us -> 391 us (0.74)
  blocking collectives: 103 us -> 0 us
  local copies, waits for them, and re-layouts: 97.9 us -> 33 us
  Pallas kernels: 0 us -> 37.4 us
  matrix products: 47.1 us -> 20 us
  waiting for transfers between devices: 228 us -> 245 us
  starting transfers between devices: 15.8 us -> 32.8 us
  loops' own time: 15.5 us -> 0 us
    all_to_all x1 -> x0, blocking collectives: 103 us -> none  [shards(): lax.all_to_all(attended, 'seq', split_axis=0, concat_axis=1, tiled=True)]
    gather x40 -> x0, local copies, waits for them, and re-layouts: 65.3 us -> none  [the longest x19 32.1 us: advance(): key_tile = key_blocks[picked]]
    pallas_call x0 -> x4, Pallas kernels: none -> 37.4 us  [attend(): pl.pallas_call(functools.partial(attend_kernel, base, width, slots), out_...]
    dot_general x39 -> x4, matrix products: 47.1 us -> 20 us  [shards(): jnp.dot(back, weights[member * groups * width:(member + 1) * groups * wid...]
    all_to_all x3 -> x8, starting transfers between devices: 15.8 us -> 32.8 us  [the longest x4 18.6 us: shards(): qkv = lax.all_to_all(mine, 'seq', split_axis=0, concat_axis=0, tiled=True)]
    all_to_all x3 -> x8, waiting for transfers between devices: 227 us -> 244 us  [the longest x4 213 us: shards(): qkv = lax.all_to_all(mine, 'seq', split_axis=0, concat_axis=0, tiled=True)]
    unnamed x9 -> x27, local copies, waits for them, and re-layouts: 11.7 us -> 27.9 us
    another operation x4 -> x0, loops' own time: 15.5 us -> none  [attend_head(): lax.fori_loop(0, trip_count, advance, initial)]
  transfers between devices with their start and end apart: 4 -> 9, of which waited for: 3 -> 8; matrix products, arithmetic and copies ran while one was open for 27% -> 10% of each run, Pallas kernels for 0% -> 10%
where the time goes in v1:
time: 391 us; the launch traced here: 390 us
  waiting for transfers between devices  245 us (63%)
  Pallas kernels  37.4 us (10%)
  local copies, waits for them, and re-layouts  33 us (8%)
  starting transfers between devices  32.8 us (8%)
  matrix products  20 us (5%)
  between operations  13.6 us (3%)
  other arithmetic  8.31 us (2%)
    all_to_all x4, waiting for transfers between devices, shards(): qkv = lax.all_to_all(mine, 'seq', split_axis=0, concat_axis=0, tiled=True)  213 us
    pallas_call x4, Pallas kernels, attend(): pl.pallas_call(functools.partial(attend_kernel, base, width, slots), out_...  37.4 us
    all_to_all x4, waiting for transfers between devices, shards(): back = lax.all_to_all(out, 'seq', split_axis=0, concat_axis=0, tiled=True)  31.3 us
    unnamed x27, local copies, waits for them, and re-layouts  27.9 us
    dot_general x4, matrix products, shards(): jnp.dot(back, weights[member * groups * width:(member + 1) * groups * wid...  20 us
    all_to_all x4, starting transfers between devices, shards(): qkv = lax.all_to_all(mine, 'seq', split_axis=0, concat_axis=0, tiled=True)  18.6 us
    all_to_all x4, starting transfers between devices, shards(): back = lax.all_to_all(out, 'seq', split_axis=0, concat_axis=0, tiled=True)  14.2 us
    concatenate x4, other arithmetic, shards(): jnp.concatenate([f[:, :, member].transpose(1, 0, 2) for f in fields], axi...  8.31 us
  transfers between devices with their start and end apart: 9, of which 8 were waited for; matrix products, arithmetic and copies ran while one was open for 10% of the time, Pallas kernels for 10%

profile of v1, /device:TPU:0, one launch (start us, length us, event | category | flops | bytes accessed | tf_op | source)
XLA Modules:
  0.0 389.6 jit_solution(2653674605035392095)
XLA Ops:
  6.5 0.0 copy-start
  6.5 0.0 all-gather.2.cloned.1.call-start
  6.5 0.7 all-gather.2.cloned.1.call-update
  7.3 3.3 copy.11
  10.5 1.2 fusion.23
  11.8 0.3 copy.40
  12.1 3.3 copy.13
  15.3 1.4 fusion.24
  16.7 1.3 copy.41
  18.0 3.3 copy.15
  21.4 1.3 fusion.25
  22.7 1.4 copy.42
  24.1 1.4 pad_maximum_fusion.3
  25.5 6.4 %all-to-all-start.6 = ((bf16[8,256,384]{2,1,0:T(8,128)(2,1)}), bf16[8,256,384]{2,1,0:T(8,128)(2,1)S(1)}, u32[]{:S(2)}, u32[]{:S(2)}) async-start(bf16[8,256,384]{2,1,0:T(8,128)(2,1)} %pad_maximum_fusion.3), calls=%async_computation.6 | async-start | bytes 3145728 | tf_op jit(solution)/shard_map/all_to_all | solution.py:97
  31.9 0.0 copy-done.3
  31.9 0.3 copy.37
  32.2 0.0 copy-done.4
  32.2 0.3 copy.38
  32.5 1.3 copy.39
  33.8 1.4 pad_maximum_fusion.2
  35.2 63.3 %all-to-all-done.6.qkv_ref = bf16[8,256,384]{2,1,0:T(8,128)(2,1)S(1)} async-done(((bf16[8,256,384]{2,1,0:T(8,128)(2,1)}), bf16[8,256,384]{2,1,0:T(8,128)(2,1)S(1)}, u32[]{:S(2)}, u32[]{:S(2)}) %all-to-all-start.6) | async-done | bytes 1572896 | tf_op jit(solution)/shard_map/all_to_all | solution.py:97
  98.5 3.6 all-to-all-start.4
  102.1 2.0 copy.34
  104.1 2.0 copy.35
  106.2 2.1 copy.36
  108.2 2.7 pad_maximum_fusion.1
  111.0 67.7 %all-to-all-done.4.qkv_ref = bf16[8,256,384]{2,1,0:T(8,128)(2,1)S(1)} async-done(((bf16[8,256,384]{2,1,0:T(8,128)(2,1)}), bf16[8,256,384]{2,1,0:T(8,128)(2,1)S(1)}, u32[]{:S(2)}, u32[]{:S(2)}) %all-to-all-start.4) | async-done | bytes 1572896 | tf_op jit(solution)/shard_map/all_to_all | solution.py:97
  178.6 4.3 %all-to-all-start.2 = ((bf16[8,256,384]{2,1,0:T(8,128)(2,1)}), bf16[8,256,384]{2,1,0:T(8,128)(2,1)}, u32[]{:S(2)}, u32[]{:S(2)}) async-start(bf16[8,256,384]{2,1,0:T(8,128)(2,1)} %pad_maximum_fusion.1), calls=%async_computation.2 | async-start | bytes 3145728 | tf_op jit(solution)/shard_map/all_to_all | solution.py:97
  182.9 2.0 copy.31
  185.0 2.1 copy.32
  187.1 2.1 copy.33
  189.1 2.8 pad_maximum_fusion
  191.9 53.3 %all-to-all-done.2.qkv_ref = bf16[8,256,384]{2,1,0:T(8,128)(2,1)} async-done(((bf16[8,256,384]{2,1,0:T(8,128)(2,1)}), bf16[8,256,384]{2,1,0:T(8,128)(2,1)}, u32[]{:S(2)}, u32[]{:S(2)}) %all-to-all-start.2) | async-done | bytes 1572896 | tf_op jit(solution)/shard_map/all_to_all | solution.py:97
  245.2 4.3 %all-to-all-start = ((bf16[8,256,384]{2,1,0:T(8,128)(2,1)}), bf16[8,256,384]{2,1,0:T(8,128)(2,1)}, u32[]{:S(2)}, u32[]{:S(2)}) async-start(bf16[8,256,384]{2,1,0:T(8,128)(2,1)} %pad_maximum_fusion), calls=%async_computation | async-start | bytes 3145728 | tf_op jit(solution)/shard_map/all_to_all | solution.py:97
  249.5 0.0 copy-done.5
  249.5 0.1 constant_dynamic-slice_fusion
  249.6 0.1 copy.10
  249.7 0.1 dynamic-slice_bitcast_fusion
  249.8 0.1 copy.30.lists_ref
  249.8 8.4 %shard_map.67 = bf16[8,256,128]{2,1,0:T(8,128)(2,1)S(1)} custom-call(s32[4,128]{1,0:T(4,128)S(1)} %copy.30.lists_ref, s32[4,16]{1,0:T(4,128)S(1)} %bitcast.64, bf16[8,256,384]{2,1,0:T(8,128)(2,1)S(1)} %all-to-all-done.6.qkv_ref), custom_call_target="tpu_custom_call" | custom-call | flops 536870912 | bytes 1572864 | tf_op jit(solution)/shard_map/pallas_call | solution.py:68
  258.2 0.0 copy-start.2
  258.2 0.8 copy-done.2
  259.0 28.3 %all-to-all-done.qkv_ref = bf16[8,256,384]{2,1,0:T(8,128)(2,1)} async-done(((bf16[8,256,384]{2,1,0:T(8,128)(2,1)}), bf16[8,256,384]{2,1,0:T(8,128)(2,1)}, u32[]{:S(2)}, u32[]{:S(2)}) %all-to-all-start) | async-done | bytes 1572896 | tf_op jit(solution)/shard_map/all_to_all | solution.py:97
  287.3 3.5 all-to-all-start.7
  290.8 9.5 %shard_map.66 = bf16[8,256,128]{2,1,0:T(8,128)(2,1)} custom-call(s32[4,128]{1,0:T(4,128)S(1)} %copy.30.lists_ref, s32[4,16]{1,0:T(4,128)S(1)} %bitcast.65, bf16[8,256,384]{2,1,0:T(8,128)(2,1)S(1)} %all-to-all-done.4.qkv_ref), custom_call_target="tpu_custom_call" | custom-call | flops 536870912 | bytes 1572864 | tf_op jit(solution)/shard_map/pallas_call | solution.py:68
  300.3 5.8 %all-to-all-done.7 = bf16[8,256,128]{2,1,0:T(8,128)(2,1)S(1)} async-done(((bf16[8,256,128]{2,1,0:T(8,128)(2,1)}), bf16[8,256,128]{2,1,0:T(8,128)(2,1)S(1)}, u32[]{:S(2)}, u32[]{:S(2)}) %all-to-all-start.7) | async-done | bytes 524320 | tf_op jit(solution)/shard_map/all_to_all | solution.py:99
  306.1 3.5 all-to-all-start.5
  309.6 10.0 %shard_map.65 = bf16[8,256,128]{2,1,0:T(8,128)(2,1)} custom-call(s32[4,128]{1,0:T(4,128)S(1)} %copy.30.lists_ref, s32[4,16]{1,0:T(4,128)S(1)} %bitcast.66, bf16[8,256,384]{2,1,0:T(8,128)(2,1)} %all-to-all-done.2.qkv_ref), custom_call_target="tpu_custom_call" | custom-call | flops 536870912 | bytes 1572864 | tf_op jit(solution)/shard_map/pallas_call | solution.py:68
  319.6 5.3 %all-to-all-done.5 = bf16[8,256,128]{2,1,0:T(8,128)(2,1)S(1)} async-done(((bf16[8,256,128]{2,1,0:T(8,128)(2,1)}), bf16[8,256,128]{2,1,0:T(8,128)(2,1)S(1)}, u32[]{:S(2)}, u32[]{:S(2)}) %all-to-all-start.5) | async-done | bytes 524320 | tf_op jit(solution)/shard_map/all_to_all | solution.py:99
  324.9 3.5 all-to-all-start.3
  328.4 9.6 %shard_map.64 = bf16[8,256,128]{2,1,0:T(8,128)(2,1)} custom-call(s32[4,128]{1,0:T(4,128)S(1)} %copy.30.lists_ref, s32[4,16]{1,0:T(4,128)S(1)} %bitcast.67, bf16[8,256,384]{2,1,0:T(8,128)(2,1)} %all-to-all-done.qkv_ref), custom_call_target="tpu_custom_call" | custom-call | flops 536870912 | bytes 1572864 | tf_op jit(solution)/shard_map/pallas_call | solution.py:68
  338.0 5.7 %all-to-all-done.3 = bf16[8,256,128]{2,1,0:T(8,128)(2,1)S(1)} async-done(((bf16[8,256,128]{2,1,0:T(8,128)(2,1)}), bf16[8,256,128]{2,1,0:T(8,128)(2,1)S(1)}, u32[]{:S(2)}, u32[]{:S(2)}) %all-to-all-start.3) | async-done | bytes 524320 | tf_op jit(solution)/shard_map/all_to_all | solution.py:99
  343.7 3.7 all-to-all-start.1
  347.4 0.2 copy.29
  347.6 0.2 copy.25
  347.8 0.2 copy.21
  348.0 14.4 %all-to-all-done.1 = bf16[8,256,128]{2,1,0:T(8,128)(2,1)S(1)} async-done(((bf16[8,256,128]{2,1,0:T(8,128)(2,1)}), bf16[8,256,128]{2,1,0:T(8,128)(2,1)S(1)}, u32[]{:S(2)}, u32[]{:S(2)}) %all-to-all-start.1) | async-done | bytes 524320 | tf_op jit(solution)/shard_map/all_to_all | solution.py:99
  362.5 0.2 copy.17
  362.7 0.0 all-gather.2.cloned.1.call-done
  362.7 4.7 %fusion.4 = f32[256,3072]{1,0:T(8,128)S(1)} fusion(bf16[256,1024]{0,1:T(8,128)(2,1)S(1)} %bitcast.90, bf16[4096,3072]{1,0:T(8,128)(2,1)} %all-gather.2.cloned.1.call-done), kind=kOutput, calls=%fused_computation.4 | convolution fusion | flops 1610612736 | bytes 9961472 | tf_op jit(solution)/shard_map/dot_general | solution.py:101
  367.4 4.7 %fusion.8 = f32[256,3072]{1,0:T(8,128)S(1)} fusion(f32[256,3072]{1,0:T(8,128)S(1)} %fusion.4, bf16[256,1024]{0,1:T(8,128)(2,1)S(1)} %bitcast.72, bf16[4096,3072]{1,0:T(8,128)(2,1)} %all-gather.2.cloned.1.call-done), kind=kOutput, calls=%fused_computation.8 | convolution fusion | flops 1611399168 | bytes 13107200 | tf_op jit(solution)/shard_map/dot_general | solution.py:101
  372.1 4.7 %fusion.11 = f32[256,3072]{1,0:T(8,128)S(1)} fusion(f32[256,3072]{1,0:T(8,128)S(1)} %fusion.8, bf16[256,1024]{0,1:T(8,128)(2,1)S(1)} %bitcast.71, bf16[4096,3072]{1,0:T(8,128)(2,1)} %all-gather.2.cloned.1.call-done), kind=kOutput, calls=%fused_computation.9 | convolution fusion | flops 1611399168 | bytes 13107200 | tf_op jit(solution)/shard_map/dot_general | solution.py:101
  376.8 0.0 copy-start.1
  376.8 5.9 %fusion.20 = bf16[1,256,3072]{2,1,0:T(8,128)(2,1)} fusion(f32[256,3072]{1,0:T(8,128)S(1)} %fusion.11, bf16[256,1024]{0,1:T(8,128)(2,1)S(1)} %bitcast.89, bf16[4096,3072]{1,0:T(8,128)(2,1)} %all-gather.2.cloned.1.call-done), kind=kOutput, calls=%fused_computation.12 | convolution fusion | flops 1612185600 | bytes 11534336 | tf_op jit(solution)/shard_map/dot_general | solution.py:101
  (5 shorter events, 0.0 us)
Async XLA Ops:
  6.5 243.2 %copy-start = (s32[1,32,16,8]{1,3,2,0:T(8,128)S(1)}, s32[1,32,16,8]{1,3,2,0:T(8,128)}, u32[]{:S(2)}) copy-start(s32[1,32,16,8]{1,3,2,0:T(8,128)} %param.10) | copy-start | bytes 49156
  6.5 356.2 %all-gather.2.cloned.1.call-start = ((), (), s32[]{:S(2)}) async-start(), calls=%async_computation.8 | async-start | bytes 25952256 | tf_op jit(solution)/shard_map/all_gather | solution.py:90
  25.5 6.4 %copy-start.3 = (bf16[256,8,1,128]{0,3,2,1:T(8,128)(2,1)S(1)}, bf16[256,8,1,128]{0,3,2,1:T(8,128)(2,1)}, u32[]{:S(2)}) copy-start(bf16[256,8,1,128]{0,3,2,1:T(8,128)(2,1)} %get-tuple-element.6) | copy-start | bytes 1572868
  25.5 6.7 %copy-start.4 = (bf16[256,8,1,128]{0,3,2,1:T(8,128)(2,1)S(1)}, bf16[256,8,1,128]{0,3,2,1:T(8,128)(2,1)}, u32[]{:S(2)}) copy-start(bf16[256,8,1,128]{0,3,2,1:T(8,128)(2,1)} %get-tuple-element.10) | copy-start | bytes 1572868
  25.5 73.0 %all-to-all-start.6 = ((bf16[8,256,384]{2,1,0:T(8,128)(2,1)}), bf16[8,256,384]{2,1,0:T(8,128)(2,1)S(1)}, u32[]{:S(2)}, u32[]{:S(2)}) async-start(bf16[8,256,384]{2,1,0:T(8,128)(2,1)} %pad_maximum_fusion.3), calls=%async_computation.6 | async-start | bytes 3145728 | tf_op jit(solution)/shard_map/all_to_all | solution.py:97
  98.5 80.1 %all-to-all-start.4 = ((bf16[8,256,384]{2,1,0:T(8,128)(2,1)}), bf16[8,256,384]{2,1,0:T(8,128)(2,1)S(1)}, u32[]{:S(2)}, u32[]{:S(2)}) async-start(bf16[8,256,384]{2,1,0:T(8,128)(2,1)} %pad_maximum_fusion.2), calls=%async_computation.4 | async-start | bytes 3145728 | tf_op jit(solution)/shard_map/all_to_all | solution.py:97
  178.6 66.6 %all-to-all-start.2 = ((bf16[8,256,384]{2,1,0:T(8,128)(2,1)}), bf16[8,256,384]{2,1,0:T(8,128)(2,1)}, u32[]{:S(2)}, u32[]{:S(2)}) async-start(bf16[8,256,384]{2,1,0:T(8,128)(2,1)} %pad_maximum_fusion.1), calls=%async_computation.2 | async-start | bytes 3145728 | tf_op jit(solution)/shard_map/all_to_all | solution.py:97
  189.1 60.4 %copy-start.5 = (s32[1,32,16]{1,2,0:T(8,128)S(1)}, s32[1,32,16]{1,2,0:T(8,128)}, u32[]{:S(2)}) copy-start(s32[1,32,16]{1,2,0:T(8,128)} %param.11) | copy-start | bytes 6148
  245.2 42.1 %all-to-all-start = ((bf16[8,256,384]{2,1,0:T(8,128)(2,1)}), bf16[8,256,384]{2,1,0:T(8,128)(2,1)}, u32[]{:S(2)}, u32[]{:S(2)}) async-start(bf16[8,256,384]{2,1,0:T(8,128)(2,1)} %pad_maximum_fusion), calls=%async_computation | async-start | bytes 3145728 | tf_op jit(solution)/shard_map/all_to_all | solution.py:97
  258.2 0.8 copy-start.2
  287.3 18.8 %all-to-all-start.7 = ((bf16[8,256,128]{2,1,0:T(8,128)(2,1)}), bf16[8,256,128]{2,1,0:T(8,128)(2,1)S(1)}, u32[]{:S(2)}, u32[]{:S(2)}) async-start(bf16[8,256,128]{2,1,0:T(8,128)(2,1)} %copy-done.2), calls=%async_computation.7 | async-start | bytes 1048576 | tf_op jit(solution)/shard_map/all_to_all | solution.py:99
  306.1 18.8 %all-to-all-start.5 = ((bf16[8,256,128]{2,1,0:T(8,128)(2,1)}), bf16[8,256,128]{2,1,0:T(8,128)(2,1)S(1)}, u32[]{:S(2)}, u32[]{:S(2)}) async-start(bf16[8,256,128]{2,1,0:T(8,128)(2,1)} %shard_map.66), calls=%async_computation.5 | async-start | bytes 1048576 | tf_op jit(solution)/shard_map/all_to_all | solution.py:99
  324.9 18.8 %all-to-all-start.3 = ((bf16[8,256,128]{2,1,0:T(8,128)(2,1)}), bf16[8,256,128]{2,1,0:T(8,128)(2,1)S(1)}, u32[]{:S(2)}, u32[]{:S(2)}) async-start(bf16[8,256,128]{2,1,0:T(8,128)(2,1)} %shard_map.65), calls=%async_computation.3 | async-start | bytes 1048576 | tf_op jit(solution)/shard_map/all_to_all | solution.py:99
  343.7 18.8 %all-to-all-start.1 = ((bf16[8,256,128]{2,1,0:T(8,128)(2,1)}), bf16[8,256,128]{2,1,0:T(8,128)(2,1)S(1)}, u32[]{:S(2)}, u32[]{:S(2)}) async-start(bf16[8,256,128]{2,1,0:T(8,128)(2,1)} %shard_map.64), calls=%async_computation.1 | async-start | bytes 1048576 | tf_op jit(solution)/shard_map/all_to_all | solution.py:99
  376.8 5.9 %copy-start.1 = (s32[1,32,16,8]{1,3,2,0:T(8,128)S(1)}, s32[1,32,16,8]{1,3,2,0:T(8,128)}, u32[]{:S(2)}) copy-start(s32[1,32,16,8]{1,3,2,0:T(8,128)} %param.10) | copy-start | bytes 49156
Sparse Core Ops, SparseCore 0:
  10.4 238.2 all-gather.1

commit v2 on v1

v2 whole, which is shorter than its diff:
```python
import functools
import math

import jax
import jax.numpy as jnp
from jax import lax
from jax.experimental import pallas as pl
from jax.experimental.pallas import tpu as pltpu
from jax.sharding import PartitionSpec as P

BLOCK = 128
VMEM = pl.BlockSpec(memory_space=pltpu.VMEM)
SMEM = pl.BlockSpec(memory_space=pltpu.SMEM)
ANY = pl.BlockSpec(memory_space=pl.ANY)
HBM = pl.BlockSpec(memory_space=pltpu.HBM)


def limit(mib):
    return pltpu.CompilerParams(vmem_limit_bytes=mib * 1024 * 1024)


def layout_kernel(members, here, width, *refs):
    fields, sem = refs[:3], refs[-1]
    out_refs = refs[-1 - len(members) : -1]
    groups = out_refs[0].shape[0]
    copies = []
    for m, member in enumerate(members):
        for g in range(groups):
            start = (g * here + member) * width
            for n, field in enumerate(fields):
                copies.append(
                    pltpu.make_async_copy(
                        field.at[:, pl.ds(start, width)],
                        out_refs[m].at[g, :, pl.ds(n * width, width)],
                        sem.at[m, g, n],
                    )
                )
    for copy in copies:
        copy.start()
    for copy in copies:
        copy.wait()


def lay_out(fields, members, groups, here, width, extra):
    tokens = fields[0].shape[0]
    count = len(members)
    return pl.pallas_call(
        functools.partial(layout_kernel, members, here, width),
        out_shape=[jax.ShapeDtypeStruct((groups, tokens, 3 * width), jnp.bfloat16)] * count,
        in_specs=[HBM] * 3 + [ANY] * len(extra),
        out_specs=[HBM] * count,
        scratch_shapes=[pltpu.SemaphoreType.DMA((count, groups, 3))],
        compiler_params=limit(16),
        cost_estimate=pl.CostEstimate(flops=1, bytes_accessed=1, transcendentals=0),
    )(*fields, *extra)


def attend_kernel(member, width, slots, rank_ref, lists_ref, counts_ref, *refs):
    qkv_ref, out_refs, held = refs[0], refs[1:-1], refs[-1]
    sources, tokens, _ = qkv_ref.shape
    per = tokens // BLOCK
    scale = width ** (-0.5) * math.log2(math.e)
    q_cols, k_cols, v_cols = (slice(n * width, (n + 1) * width) for n in range(3))

    def rows_of(block):
        return block // per, pl.ds(pl.multiple_of((block % per) * BLOCK, BLOCK), BLOCK)

    def one(at, carry):
        part = at // per
        rows = pl.ds(pl.multiple_of((at % per) * BLOCK, BLOCK), BLOCK)
        src = part ^ rank_ref[0]
        i = src * per + at % per
        live = counts_ref[member, i]

        def branch(pairs):
            picked = [rows_of(lists_ref[member, i * slots + j]) for j in range(2 * pairs)]
            q = qkv_ref[src, rows, q_cols]
            scores = []
            for n in range(pairs):
                k = jnp.concatenate([qkv_ref[s, r, k_cols] for s, r in picked[2 * n : 2 * n + 2]], axis=0)
                scores.append(lax.dot_general(q, k, (((1,), (1,)), ((), ())), preferred_element_type=jnp.float32))
            usable = lax.broadcasted_iota(jnp.int32, scores[-1].shape, 1) < BLOCK * (live - 2 * (pairs - 1))
            scores[-1] = jnp.where(usable, scores[-1], -jnp.inf)
            top = functools.reduce(jnp.maximum, scores)
            top = jnp.max(top, axis=1, keepdims=True) * scale
            total = None
            mixed = None
            for n in range(pairs):
                weights = jnp.exp2(scores[n] * scale - top)
                v = jnp.concatenate([qkv_ref[s, r, v_cols] for s, r in picked[2 * n : 2 * n + 2]], axis=0)
                product = jnp.dot(weights.astype(jnp.bfloat16), v, preferred_element_type=jnp.float32)
                total = weights if total is None else total + weights
                mixed = product if mixed is None else mixed + product
            totals = jnp.sum(total, axis=1, keepdims=True)
            held[part, rows, :] = (mixed / totals).astype(held.dtype)

        for pairs in range(1, slots // 2 + 1):
            pl.when((live + 1) // 2 == pairs)(functools.partial(branch, pairs))
        return carry

    lax.fori_loop(0, sources * per, one, 0)
    each = sources // len(out_refs)
    for n, out_ref in enumerate(out_refs):
        for m in range(each):
            out_ref[m * tokens : (m + 1) * tokens, :] = held[n * each + m]


def attend(qkv, rank, lists, counts, member, width, each):
    sources, tokens, _ = qkv.shape
    slots = lists.shape[1] // counts.shape[1]
    return pl.pallas_call(
        functools.partial(attend_kernel, member, width, slots),
        out_shape=[jax.ShapeDtypeStruct((each * tokens, width), jnp.bfloat16)] * (sources // each),
        in_specs=[SMEM, SMEM, SMEM, VMEM],
        out_specs=[VMEM] * (sources // each),
        scratch_shapes=[pltpu.VMEM((sources, tokens, width), jnp.bfloat16)],
        compiler_params=limit(32),
        cost_estimate=pl.CostEstimate(flops=1, bytes_accessed=1, transcendentals=0),
    )(rank, lists, counts, qkv)


def project_kernel(terms, n_rows, n_blocks, n_before, *refs):
    rows, blocks = refs[:n_rows], refs[n_rows : n_rows + n_blocks]
    before = refs[n_rows + n_blocks : n_rows + n_blocks + n_before]
    out_refs = refs[n_rows + n_blocks + n_before : -3]
    held, total, sem = refs[-3:]
    slots = held.shape[0]
    copies = [
        pltpu.make_async_copy(blocks[block].at[member], held.at[n % slots], sem.at[n % slots])
        for n, (block, member, _) in enumerate(terms)
    ]
    for copy in copies[:slots]:
        copy.start()
    wide = total.shape[-1]
    step = wide // 4
    for n, (_, _, picked) in enumerate(terms):
        copies[n].wait()
        left = jnp.concatenate([rows[r][...] for r in picked], axis=1)
        for at in range(0, wide, step):
            cols = slice(at, at + step)
            part = jnp.dot(left, held[n % slots, :, cols], preferred_element_type=jnp.float32)
            if n:
                part = part + total[:, cols]
            else:
                for other in before:
                    part = part + other[:, cols]
            if n < len(terms) - 1:
                total[:, cols] = part
            else:
                tall = part.shape[0] // len(out_refs)
                for m, out_ref in enumerate(out_refs):
                    out_ref[:, cols] = part[m * tall : (m + 1) * tall].astype(out_ref.dtype)
        if n + slots < len(terms):
            copies[n + slots].start()


def project(rows, blocks, terms, before, dtypes):
    tall = rows[0].shape[0]
    depth, wide = blocks[0].shape[1:]
    slots, outs = min(4, len(terms)), len(dtypes)
    return pl.pallas_call(
        functools.partial(project_kernel, terms, len(rows), len(blocks), len(before)),
        out_shape=[jax.ShapeDtypeStruct((tall // outs, wide), dtype) for dtype in dtypes],
        in_specs=[VMEM] * len(rows) + [ANY] * len(blocks) + [VMEM] * len(before),
        out_specs=[VMEM] * outs,
        scratch_shapes=[
            pltpu.VMEM((slots, depth, wide), jnp.bfloat16),
            pltpu.VMEM((tall, wide), jnp.float32),
            pltpu.SemaphoreType.DMA((slots,)),
        ],
        compiler_params=limit(48),
        cost_estimate=pl.CostEstimate(flops=1, bytes_accessed=1, transcendentals=0),
    )(*rows, *blocks, *before)


def along_z(pairs):
    return [(2 * i + c, 2 * j + c) for i, j in pairs for c in (0, 1)]


def after(value, *others):
    return lax.optimization_barrier((value, *others))[0]


def xor(p, groups):
    return [(i, i ^ p) for i in range(groups)]


UP = [(0, 1), (1, 2), (2, 3)]
DOWN = [(j, i) for i, j in UP]


def exchange(x):
    return lax.all_to_all(x, "seq", split_axis=0, concat_axis=0, tiled=True)


def shards_lines(fields, weight, rank, lists, counts, here, width):
    groups = 8
    chip = lax.axis_index("seq") // 2
    number = jnp.full((1,), rank, jnp.int32)
    swap = xor(1, groups)

    def send(value, pairs, *holds):
        return lax.ppermute(after(value, *holds) if holds else value, "seq", pairs)

    def send_back(out):
        unit = groups // len(out)
        return [out[0]] + [send(out[p], xor(p * unit, groups)) for p in range(1, len(out))]

    def attend_member(qkv, member, each):
        return attend(qkv, number, lists, counts, member, width, each)

    up = send(weight, along_z(UP))
    down = send(weight, along_z(DOWN))
    x0, x1, x2, x3 = lay_out(fields, (0, 1, 2, 3), groups, here, width, [])
    near = jnp.concatenate([weight, jnp.where(chip % 2 == 0, down, up)], axis=0)
    near, x0, x1, x2, x3 = lax.optimization_barrier((near, x0, x1, x2, x3))
    first = lax.all_gather(near, "fsdp", axis=0, tiled=False)
    qkv0 = exchange(x0)
    up2 = send(up, along_z(UP[1:]), near)
    down2 = send(down, along_z(DOWN[:2]), near)
    up2, down2, qkv0 = lax.optimization_barrier((up2, down2, qkv0))
    qkv1 = exchange(after(x1, up2))
    out0 = attend_member(qkv0, 0, 2)
    up3 = send(up2, along_z(UP[2:]), *out0)
    down3 = send(down2, along_z(DOWN[:1]), *out0)
    back0 = send_back(out0)
    up3, down3, qkv1 = lax.optimization_barrier((up3, down3, qkv1))
    inner = (chip == 1) | (chip == 2)
    low = chip < 2
    opposite = jnp.where(inner, jnp.where(low, down, up), jnp.where(low, down3, up3))
    far = jnp.concatenate([jnp.where(low, down2, up2), opposite], axis=0)
    second = lax.all_gather(far, "fsdp", axis=0, tiled=False)
    qkv2 = exchange(after(x2, qkv1, far))
    out1 = attend_member(qkv1, 1, 2)
    back1 = send_back(out1)
    qkv2, *back0 = lax.optimization_barrier((qkv2, *back0))
    qkv3 = exchange(after(x3, qkv2, first, *out1))
    out2 = attend_member(qkv2, 2, 2)
    qkv3, *rest = lax.optimization_barrier((qkv3, *back1, *out2))
    back1, out2 = rest[:4], rest[4:]
    back2 = send_back(out2)
    out3 = attend_member(qkv3, 3, 2)
    back0, back1, back2, out3 = lax.optimization_barrier((back0, back1, back2, out3))
    back3 = send_back(out3)
    blocks = [first, second]

    def terms(member, at):
        return [(h, member, (4 * at + 2 * h, 4 * at + 2 * h + 1)) for h in (0, 1)]

    (both,) = project(back0 + back1 + back2, blocks, terms(0, 0) + terms(1, 1) + terms(2, 2), [], (jnp.float32,))
    mine, theirs = project(back3, blocks, terms(3, 0), [both], (jnp.float32, jnp.bfloat16))
    return (mine + send(theirs, swap).astype(jnp.float32)).astype(jnp.bfloat16)


def shards_any(fields, weight, rank, lists, counts, here, width, groups):
    number = jnp.full((1,), rank, jnp.int32)
    rows = weight.shape[0]
    gathered = lax.all_gather(weight, ("fsdp", "seq"), axis=0, tiled=True)
    gathered = gathered.reshape(here, width // rows, groups, rows, -1).transpose(0, 2, 1, 3, 4)
    gathered = gathered.reshape(here, groups, width, -1)
    ready = lay_out(fields, tuple(range(here)), groups, here, width, [])
    result = None
    for member in range(here):
        out = attend(exchange(ready[member]), number, lists, counts, member, width, 1)
        for p in range(groups):
            part = jnp.dot(
                lax.ppermute(out[p], "seq", xor(p, groups)) if p else out[0],
                lax.dynamic_index_in_dim(gathered[member], rank ^ p, 0, keepdims=False),
                preferred_element_type=jnp.float32,
            )
            result = part if result is None else result + part
    return result.astype(jnp.bfloat16)


def shards(queries, keys, values, out_weight, block_lists, block_counts):
    groups = lax.axis_size("seq")
    rank = lax.axis_index("seq")
    head_count = block_counts.shape[1]
    width = queries.shape[2] // head_count
    here = head_count // groups
    lists = lax.dynamic_slice_in_dim(block_lists[0], rank * here, here).reshape(here, -1)
    counts = lax.dynamic_slice_in_dim(block_counts[0], rank * here, here)
    fields = [x[0] for x in (queries, keys, values)]
    if groups == 8 and here == 4 and lax.axis_size("fsdp") == 4 and out_weight.shape[0] == width:
        result = shards_lines(fields, out_weight, rank, lists, counts, here, width)
    else:
        result = shards_any(fields, out_weight, rank, lists, counts, here, width, groups)
    return result[None]


def solution(mesh):
    return jax.shard_map(
        shards,
        mesh=mesh,
        in_specs=(
            P("fsdp", "seq", None),
            P("fsdp", "seq", None),
            P("fsdp", "seq", None),
            P(("seq", "fsdp"), None),
            P("fsdp", None, None, None),
            P("fsdp", None, None),
        ),
        out_specs=P("fsdp", "seq", None),
        check_vma=False,
    )
```

time: 391 us -> 294 us (0.75)
  waiting for transfers between devices: 245 us -> 144 us
  starting transfers between devices: 32.8 us -> 55.8 us
  matrix products: 20 us -> 0 us
  Pallas kernels: 37.4 us -> 53.7 us
  local copies, waits for them, and re-layouts: 33 us -> 18.4 us
    all_to_all x8 -> x4, waiting for transfers between devices: 244 us -> 0.01 us  [exchange(): return lax.all_to_all(x, 'seq', split_axis=0, concat_axis=0, tiled=True)]
    ppermute x0 -> x19, waiting for transfers between devices: none -> 144 us  [send(): return lax.ppermute(after(value, *holds) if holds else value, 'seq', pairs)]
    ppermute x0 -> x19, starting transfers between devices: none -> 31.2 us  [send(): return lax.ppermute(after(value, *holds) if holds else value, 'seq', pairs)]
    dot_general x4 -> x0, matrix products: 20 us -> none  [shards(): jnp.dot(back, weights[member * groups * width:(member + 1) * groups * wid...]
    pallas_call x4 -> x7, Pallas kernels: 37.4 us -> 53.7 us  [the longest x4 35.3 us: attend(): pl.pallas_call(functools.partial(attend_kernel, member, width, slots), ou...]
    unnamed x27 -> x74, local copies, waits for them, and re-layouts: 27.9 us -> 18 us
    all_to_all x8 -> x4, starting transfers between devices: 32.8 us -> 24.6 us  [exchange(): return lax.all_to_all(x, 'seq', split_axis=0, concat_axis=0, tiled=True)]
    concatenate x4 -> x2, other arithmetic: 8.31 us -> 2.54 us  [the longest x1 1.3 us: shards_lines(): near = jnp.concatenate([weight, jnp.where(chip % 2 == 0, down, up)], axis=0)]
  transfers between devices with their start and end apart: 9 -> 25, of which waited for: 8 -> 10; matrix products, arithmetic and copies ran while one was open for 10% -> 2% of each run, Pallas kernels for 10% -> 16%
where the time goes in v2:
time: 294 us
  waiting for transfers between devices  144 us (49%)
  starting transfers between devices  55.8 us (19%)
  Pallas kernels  53.7 us (18%)
  local copies, waits for them, and re-layouts  18.4 us (6%)
  between operations  13.7 us (5%)
  other arithmetic  7.65 us (3%)
    ppermute x19, waiting for transfers between devices, send(): return lax.ppermute(after(value, *holds) if holds else value, 'seq', pairs)  144 us
    pallas_call x4, Pallas kernels, attend(): pl.pallas_call(functools.partial(attend_kernel, member, width, slots), ou...  35.3 us
    ppermute x19, starting transfers between devices, send(): return lax.ppermute(after(value, *holds) if holds else value, 'seq', pairs)  31.2 us
    all_to_all x4, starting transfers between devices, exchange(): return lax.all_to_all(x, 'seq', split_axis=0, concat_axis=0, tiled=True)  24.6 us
    unnamed x74, local copies, waits for them, and re-layouts  18 us
    pallas_call x2, Pallas kernels, project(): pl.pallas_call(functools.partial(project_kernel, terms, len(rows), len(bl...  16.1 us
  transfers between devices with their start and end apart: 25, of which 10 were waited for; matrix products, arithmetic and copies ran while one was open for 2% of the time, Pallas kernels for 16%

profile of v2, /device:TPU:0, one launch (start us, length us, event | category | flops | bytes accessed | tf_op | source)
XLA Modules:
  0.0 293.7 jit_solution(4440781989414082004)
XLA Ops:
  6.5 1.4 collective-permute-start
  8.0 5.6 %collective-permute-start.1 = (bf16[128,3072]{1,0:T(8,128)(2,1)}, bf16[128,3072]{1,0:T(8,128)(2,1)S(1)}, u32[]{:S(2)}, u32[]{:S(2)}) collective-permute-start(bf16[128,3072]{1,0:T(8,128)(2,1)} %param.9), channel_id=1, source_target_pairs={{0,8},{4,12},{8,16},{12,20},{16,24},{20,28},{1,9},{5,13},{9,17},{1... | collective-permute-start | bytes 2359304 | tf_op jit(solution)/shard_map/ppermute | solution.py:203
  13.6 1.6 copy-done.1
  15.2 1.6 copy-done.2
  16.8 1.6 copy-done.3
  18.4 2.3 shard_map.64
  20.7 1.1 copy-done.4
  21.8 1.1 copy-done.5
  22.9 1.2 copy-done.6
  24.2 5.2 %collective-permute-done = bf16[128,3072]{1,0:T(8,128)(2,1)S(1)} collective-permute-done((bf16[128,3072]{1,0:T(8,128)(2,1)}, bf16[128,3072]{1,0:T(8,128)(2,1)S(1)}, u32[]{:S(2)}, u32[]{:S(2)}) %collective-permute-start) | collective-permute-done | bytes 786464 | tf_op jit(solution)/shard_map/ppermute | solution.py:203
  29.3 1.3 collective-permute-done.1
  30.6 0.1 broadcast_select_fusion.1
  30.7 1.3 pad_maximum_fusion
  32.0 5.9 %all-to-all-start = ((bf16[8,256,384]{2,1,0:T(8,128)(2,1)}), bf16[8,256,384]{2,1,0:T(8,128)(2,1)S(1)}, u32[]{:S(2)}, u32[]{:S(2)}) async-start(bf16[8,256,384]{2,1,0:T(8,128)(2,1)} %get-tuple-element.83), calls=%async_computation | async-start | bytes 3145728 | tf_op jit(solution)/shard_map/all_to_all | solution.py:193
  38.0 1.6 collective-permute-start.2
  39.6 1.3 collective-permute-start.3
  40.9 42.6 %collective-permute-done.3 = bf16[128,3072]{1,0:T(8,128)(2,1)} collective-permute-done((bf16[128,3072]{1,0:T(8,128)(2,1)S(1)}, bf16[128,3072]{1,0:T(8,128)(2,1)}, u32[]{:S(2)}, u32[]{:S(2)}) %collective-permute-start.3) | collective-permute-done | bytes 786464 | tf_op jit(solution)/shard_map/ppermute | solution.py:203
  83.4 11.2 %all-to-all-start.1 = ((bf16[8,256,384]{2,1,0:T(8,128)(2,1)}), bf16[8,256,384]{2,1,0:T(8,128)(2,1)S(1)}, u32[]{:S(2)}, u32[]{:S(2)}) async-start(bf16[8,256,384]{2,1,0:T(8,128)(2,1)} %copy-done.6), calls=%async_computation.1 | async-start | bytes 3145728 | tf_op jit(solution)/shard_map/all_to_all | solution.py:193
  95.0 8.0 %shard_map.65 = (bf16[512,128]{1,0:T(8,128)(2,1)S(1)}, bf16[512,128]{1,0:T(8,128)(2,1)S(1)}, bf16[512,128]{1,0:T(8,128)(2,1)S(1)}, bf16[512,128]{1,0:T(8,128)(2,1)S(1)}) custom-call(s32[1]{0:T(128)} %bitcast.3.rank_ref, s32[4,128]{1,0:T(4,128)S(1)} %copy.11.lists_ref, s32[4,16]{1,0:T(4,128)S(1)} %bitcast.14, bf16[8,256,384]{2,1,0:T(8,128)(2,1)S(1)} %all-to-all-done.refs_0_), custom_call_target="tpu_custom_call" | custom-call | flops 1 | bytes 1 | tf_op jit(solution)/shard_map/pallas_call | solution.py:111
  103.0 0.6 copy-done.21
  103.7 0.7 copy-done.23
  104.3 1.7 collective-permute-start.4
  106.1 1.3 collective-permute-start.5
  107.4 2.1 broadcast_select_fusion
  109.5 30.6 %collective-permute-done.5 = bf16[128,3072]{1,0:T(8,128)(2,1)} collective-permute-done((bf16[128,3072]{1,0:T(8,128)(2,1)}, bf16[128,3072]{1,0:T(8,128)(2,1)}, u32[]{:S(2)}, u32[]{:S(2)}) %collective-permute-start.5) | collective-permute-done | bytes 786464 | tf_op jit(solution)/shard_map/ppermute | solution.py:203
  140.1 1.4 select_select_fusion
  141.5 1.2 pad_maximum_fusion.1
  142.8 3.7 %all-to-all-start.2 = ((bf16[8,256,384]{2,1,0:T(8,128)(2,1)}), bf16[8,256,384]{2,1,0:T(8,128)(2,1)S(1)}, u32[]{:S(2)}, u32[]{:S(2)}) async-start(bf16[8,256,384]{2,1,0:T(8,128)(2,1)} %copy-done.5), calls=%async_computation.2 | async-start | bytes 3145728 | tf_op jit(solution)/shard_map/all_to_all | solution.py:193
  146.5 2.0 collective-permute-start.6
  148.5 2.4 collective-permute-start.7
  150.9 8.6 %shard_map.66 = (bf16[512,128]{1,0:T(8,128)(2,1)S(1)}, bf16[512,128]{1,0:T(8,128)(2,1)S(1)}, bf16[512,128]{1,0:T(8,128)(2,1)S(1)}, bf16[512,128]{1,0:T(8,128)(2,1)S(1)}) custom-call(s32[1]{0:T(128)} %bitcast.3.rank_ref, s32[4,128]{1,0:T(4,128)S(1)} %copy.11.lists_ref, s32[4,16]{1,0:T(4,128)S(1)} %bitcast.15, bf16[8,256,384]{2,1,0:T(8,128)(2,1)S(1)} %all-to-all-done.1.refs_0_), custom_call_target="tpu_custom_call" | custom-call | flops 1 | bytes 1 | tf_op jit(solution)/shard_map/pallas_call | solution.py:111
  159.6 0.6 copy-done.11
  160.2 0.6 copy-done.24
  160.8 0.6 copy-done.25
  161.5 0.6 copy-done.26
  162.1 13.9 %collective-permute-done.6.refs_1_ = bf16[512,128]{1,0:T(8,128)(2,1)S(1)} collective-permute-done((bf16[512,128]{1,0:T(8,128)(2,1)}, bf16[512,128]{1,0:T(8,128)(2,1)S(1)}, u32[]{:S(2)}, u32[]{:S(2)}) %collective-permute-start.6) | collective-permute-done | bytes 131104 | tf_op jit(solution)/shard_map/ppermute | solution.py:203
  176.0 17.2 %collective-permute-done.7.refs_2_ = bf16[512,128]{1,0:T(8,128)(2,1)S(1)} collective-permute-done((bf16[512,128]{1,0:T(8,128)(2,1)}, bf16[512,128]{1,0:T(8,128)(2,1)S(1)}, u32[]{:S(2)}, u32[]{:S(2)}) %collective-permute-start.7) | collective-permute-done | bytes 131104 | tf_op jit(solution)/shard_map/ppermute | solution.py:203
  193.2 0.7 copy-done.7
  193.9 0.7 copy-done.9
  194.5 3.8 %all-to-all-start.3 = ((bf16[8,256,384]{2,1,0:T(8,128)(2,1)}), bf16[8,256,384]{2,1,0:T(8,128)(2,1)S(1)}, u32[]{:S(2)}, u32[]{:S(2)}) async-start(bf16[8,256,384]{2,1,0:T(8,128)(2,1)} %copy-done.4), calls=%async_computation.3 | async-start | bytes 3145728 | tf_op jit(solution)/shard_map/all_to_all | solution.py:193
  198.3 2.3 collective-permute-start.9
  200.5 1.9 collective-permute-start.10
  202.4 0.6 collective-permute-start.11
  203.0 8.7 %shard_map.67 = (bf16[512,128]{1,0:T(8,128)(2,1)S(1)}, bf16[512,128]{1,0:T(8,128)(2,1)S(1)}, bf16[512,128]{1,0:T(8,128)(2,1)S(1)}, bf16[512,128]{1,0:T(8,128)(2,1)S(1)}) custom-call(s32[1]{0:T(128)} %bitcast.3.rank_ref, s32[4,128]{1,0:T(4,128)S(1)} %copy.11.lists_ref, s32[4,16]{1,0:T(4,128)S(1)} %bitcast.16, bf16[8,256,384]{2,1,0:T(8,128)(2,1)S(1)} %all-to-all-done.2.refs_0_), custom_call_target="tpu_custom_call" | custom-call | flops 1 | bytes 1 | tf_op jit(solution)/shard_map/pallas_call | solution.py:111
  211.7 0.6 copy-done.19
  212.3 0.6 copy-done.27
  213.0 0.6 copy-done.28
  213.6 0.6 copy-done.29
  214.3 13.4 %collective-permute-done.9.refs_5_ = bf16[512,128]{1,0:T(8,128)(2,1)S(1)} collective-permute-done((bf16[512,128]{1,0:T(8,128)(2,1)}, bf16[512,128]{1,0:T(8,128)(2,1)S(1)}, u32[]{:S(2)}, u32[]{:S(2)}) %collective-permute-start.9) | collective-permute-done | bytes 131104 | tf_op jit(solution)/shard_map/ppermute | solution.py:203
  227.7 0.6 copy-done.13
  228.4 16.4 %collective-permute-done.10.refs_6_ = bf16[512,128]{1,0:T(8,128)(2,1)S(1)} collective-permute-done((bf16[512,128]{1,0:T(8,128)(2,1)}, bf16[512,128]{1,0:T(8,128)(2,1)S(1)}, u32[]{:S(2)}, u32[]{:S(2)}) %collective-permute-start.10) | collective-permute-done | bytes 131104 | tf_op jit(solution)/shard_map/ppermute | solution.py:203
  244.8 0.7 copy-done.15
  245.4 0.6 copy-done.17
  246.1 2.2 collective-permute-start.12
  248.3 2.4 collective-permute-start.14
  250.8 9.9 %shard_map.68 = (bf16[512,128]{1,0:T(8,128)(2,1)S(1)}, bf16[512,128]{1,0:T(8,128)(2,1)}, bf16[512,128]{1,0:T(8,128)(2,1)}, bf16[512,128]{1,0:T(8,128)(2,1)}) custom-call(s32[1]{0:T(128)} %bitcast.3.rank_ref, s32[4,128]{1,0:T(4,128)S(1)} %copy.11.lists_ref, s32[4,16]{1,0:T(4,128)S(1)} %bitcast.17, bf16[8,256,384]{2,1,0:T(8,128)(2,1)S(1)} %all-to-all-done.3.refs_0_), custom_call_target="tpu_custom_call" | custom-call | flops 1 | bytes 1 | tf_op jit(solution)/shard_map/pallas_call | solution.py:111
  260.7 0.5 collective-permute-done.13.refs_10_
  261.1 2.1 collective-permute-start.15
  263.2 0.2 collective-permute-start.16
  263.4 2.2 collective-permute-start.17
  265.6 9.9 %shard_map.69.refs_6_ = f32[512,3072]{1,0:T(8,128)} custom-call(bf16[512,128]{1,0:T(8,128)(2,1)S(1)} %get-tuple-element.131.refs_0_, bf16[512,128]{1,0:T(8,128)(2,1)S(1)} %collective-permute-done.6.refs_1_, bf16[512,128]{1,0:T(8,128)(2,1)S(1)} %copy-done.8, bf16[512,128]{1,0:T(8,128)(2,1)S(1)} %copy-done.10, bf16[512,128]{1,0:T(8,128)(2,1)S(1)} %copy-done.12, ...), custom_call_target="tpu_custom_call" | custom-call | flops 1 | bytes 1 | tf_op jit(solution)/shard_map/pallas_call | solution.py:161
  275.6 6.2 %shard_map.70 = (f32[256,3072]{1,0:T(8,128)S(1)}, bf16[256,3072]{1,0:T(8,128)(2,1)S(1)}) custom-call(bf16[512,128]{1,0:T(8,128)(2,1)S(1)} %get-tuple-element.127.refs_0_, bf16[512,128]{1,0:T(8,128)(2,1)S(1)} %collective-permute-done.15.refs_1_, bf16[512,128]{1,0:T(8,128)(2,1)S(1)} %collective-permute-done.16.refs_2_, ...), custom_call_target="tpu_custom_call" | custom-call | flops 1 | bytes 1 | tf_op jit(solution)/shard_map/pallas_call | solution.py:161
  281.9 3.4 %collective-permute-done.18 = bf16[256,3072]{1,0:T(8,128)(2,1)S(1)} collective-permute-done((bf16[256,3072]{1,0:T(8,128)(2,1)S(1)}, bf16[256,3072]{1,0:T(8,128)(2,1)S(1)}, u32[]{:S(2)}, u32[]{:S(2)}) %collective-permute-start.18) | collective-permute-done | bytes 1572896 | tf_op jit(solution)/shard_map/ppermute | solution.py:203
  285.3 1.6 fusion
  (79 shorter events, 0.6 us)
Async XLA Ops:
  6.5 88.3 %copy-start = (s32[1,32,16,8]{1,3,2,0:T(8,128)S(1)}, s32[1,32,16,8]{1,3,2,0:T(8,128)}, u32[]{:S(2)}) copy-start(s32[1,32,16,8]{1,3,2,0:T(8,128)} %param.10) | copy-start | bytes 49156
  6.5 188.0 %all-gather.5.cloned.1.call-start = ((), (), s32[]{:S(2)}) async-start(), calls=%async_computation.4 | async-start | bytes 7864320 | tf_op jit(solution)/shard_map/all_gather | solution.py:217
  6.5 22.8 %collective-permute-start = (bf16[128,3072]{1,0:T(8,128)(2,1)}, bf16[128,3072]{1,0:T(8,128)(2,1)S(1)}, u32[]{:S(2)}, u32[]{:S(2)}) collective-permute-start(bf16[128,3072]{1,0:T(8,128)(2,1)} %param.9), channel_id=1, source_target_pairs={{8,0},{12,4},{16,8},{20,12},{24,16},{28,20},{9,1},{13,5},{17,9},{2... | collective-permute-start | bytes 2359304 | tf_op jit(solution)/shard_map/ppermute | solution.py:203
  8.0 22.7 %collective-permute-start.1 = (bf16[128,3072]{1,0:T(8,128)(2,1)}, bf16[128,3072]{1,0:T(8,128)(2,1)S(1)}, u32[]{:S(2)}, u32[]{:S(2)}) collective-permute-start(bf16[128,3072]{1,0:T(8,128)(2,1)} %param.9), channel_id=1, source_target_pairs={{0,8},{4,12},{8,16},{12,20},{16,24},{20,28},{1,9},{5,13},{9,17},{1... | collective-permute-start | bytes 2359304 | tf_op jit(solution)/shard_map/ppermute | solution.py:203
  13.6 1.6 copy-start.1
  15.2 1.6 copy-start.2
  16.8 1.6 copy-start.3
  20.6 1.1 copy-start.4
  21.8 1.1 copy-start.5
  22.9 1.2 copy-start.6
  24.2 6.5 %copy-start.35 = (bf16[128,3072]{1,0:T(8,128)(2,1)S(1)}, bf16[128,3072]{1,0:T(8,128)(2,1)}, u32[]{:S(2)}) copy-start(bf16[128,3072]{1,0:T(8,128)(2,1)} %param.9) | copy-start | bytes 2359300
  29.3 10.2 %copy-start.30 = (bf16[128,3072]{1,0:T(8,128)(2,1)}, bf16[128,3072]{1,0:T(8,128)(2,1)S(1)}, u32[]{:S(2)}) copy-start(bf16[128,3072]{1,0:T(8,128)(2,1)S(1)} %collective-permute-done) | copy-start | bytes 2359300
  30.6 7.3 %copy-start.32 = (bf16[128,3072]{1,0:T(8,128)(2,1)}, bf16[128,3072]{1,0:T(8,128)(2,1)S(1)}, u32[]{:S(2)}) copy-start(bf16[128,3072]{1,0:T(8,128)(2,1)S(1)} %collective-permute-done.1) | copy-start | bytes 2359300
  32.0 51.4 %all-to-all-start = ((bf16[8,256,384]{2,1,0:T(8,128)(2,1)}), bf16[8,256,384]{2,1,0:T(8,128)(2,1)S(1)}, u32[]{:S(2)}, u32[]{:S(2)}) async-start(bf16[8,256,384]{2,1,0:T(8,128)(2,1)} %get-tuple-element.83), calls=%async_computation | async-start | bytes 3145728 | tf_op jit(solution)/shard_map/all_to_all | solution.py:193
  38.0 56.7 %copy-start.36 = (s32[1,32,16]{1,2,0:T(8,128)S(1)}, s32[1,32,16]{1,2,0:T(8,128)}, u32[]{:S(2)}) copy-start(s32[1,32,16]{1,2,0:T(8,128)} %param.11) | copy-start | bytes 6148
  38.0 2.9 collective-permute-start.2
  39.6 43.9 %collective-permute-start.3 = (bf16[128,3072]{1,0:T(8,128)(2,1)S(1)}, bf16[128,3072]{1,0:T(8,128)(2,1)}, u32[]{:S(2)}, u32[]{:S(2)}) collective-permute-start(bf16[128,3072]{1,0:T(8,128)(2,1)S(1)} %collective-permute-done), channel_id=1, source_target_pairs={{8,0},{12,4},{16,8},{20,12},{9,1},{13,5},{17,9},{21,13},{10,2},{14... | collective-permute-start | bytes 2359304 | tf_op jit(solution)/shard_map/ppermute | solution.py:203
  83.4 56.7 %all-to-all-start.1 = ((bf16[8,256,384]{2,1,0:T(8,128)(2,1)}), bf16[8,256,384]{2,1,0:T(8,128)(2,1)S(1)}, u32[]{:S(2)}, u32[]{:S(2)}) async-start(bf16[8,256,384]{2,1,0:T(8,128)(2,1)} %copy-done.6), calls=%async_computation.1 | async-start | bytes 3145728 | tf_op jit(solution)/shard_map/all_to_all | solution.py:193
  94.6 170.9 %all-gather.7.cloned.1.call-start = ((), (), s32[]{:S(2)}) async-start(), calls=%async_computation.5 | async-start | bytes 7864320 | tf_op jit(solution)/shard_map/all_gather | solution.py:232
  103.0 0.7 copy-start.21
  103.7 0.7 copy-start.23
  104.3 37.2 %copy-start.22 = (bf16[512,128]{1,0:T(8,128)(2,1)}, bf16[512,128]{1,0:T(8,128)(2,1)S(1)}, u32[]{:S(2)}) copy-start(bf16[512,128]{1,0:T(8,128)(2,1)S(1)} %get-tuple-element.88) | copy-start | bytes 393220
  104.3 35.8 %copy-start.31 = (bf16[128,3072]{1,0:T(8,128)(2,1)S(1)}, bf16[128,3072]{1,0:T(8,128)(2,1)}, u32[]{:S(2)}) copy-start(bf16[128,3072]{1,0:T(8,128)(2,1)} %copy-done.30) | copy-start | bytes 2359300
  104.3 35.8 %copy-start.33 = (bf16[128,3072]{1,0:T(8,128)(2,1)S(1)}, bf16[128,3072]{1,0:T(8,128)(2,1)}, u32[]{:S(2)}) copy-start(bf16[128,3072]{1,0:T(8,128)(2,1)} %copy-done.32) | copy-start | bytes 2359300
  104.3 5.2 %collective-permute-start.4 = (bf16[128,3072]{1,0:T(8,128)(2,1)}, bf16[128,3072]{1,0:T(8,128)(2,1)}, u32[]{:S(2)}, u32[]{:S(2)}) collective-permute-start(bf16[128,3072]{1,0:T(8,128)(2,1)} %collective-permute-done.2), channel_id=1, source_target_pairs={{16,24},{20,28},{17,25},{21,29},{18,26},{22,30},{19,27},{23,31}} | collective-permute-start | bytes 2359304 | tf_op jit(solution)/shard_map/ppermute | solution.py:203
  106.1 34.0 %collective-permute-start.5 = (bf16[128,3072]{1,0:T(8,128)(2,1)}, bf16[128,3072]{1,0:T(8,128)(2,1)}, u32[]{:S(2)}, u32[]{:S(2)}) collective-permute-start(bf16[128,3072]{1,0:T(8,128)(2,1)} %collective-permute-done.3), channel_id=1, source_target_pairs={{8,0},{12,4},{9,1},{13,5},{10,2},{14,6},{11,3},{15,7}} | collective-permute-start | bytes 2359304 | tf_op jit(solution)/shard_map/ppermute | solution.py:203
  140.1 1.4 copy-start.34
  142.8 51.7 %all-to-all-start.2 = ((bf16[8,256,384]{2,1,0:T(8,128)(2,1)}), bf16[8,256,384]{2,1,0:T(8,128)(2,1)S(1)}, u32[]{:S(2)}, u32[]{:S(2)}) async-start(bf16[8,256,384]{2,1,0:T(8,128)(2,1)} %copy-done.5), calls=%async_computation.2 | async-start | bytes 3145728 | tf_op jit(solution)/shard_map/all_to_all | solution.py:193
  146.5 29.5 %collective-permute-start.6 = (bf16[512,128]{1,0:T(8,128)(2,1)}, bf16[512,128]{1,0:T(8,128)(2,1)S(1)}, u32[]{:S(2)}, u32[]{:S(2)}) collective-permute-start(bf16[512,128]{1,0:T(8,128)(2,1)} %copy-done.23), channel_id=1, source_target_pairs={{0,8},{4,12},{8,0},{12,4},{16,24},{20,28},{24,16},{28,20},{1,9},{5... | collective-permute-start | bytes 393224 | tf_op jit(solution)/shard_map/ppermute | solution.py:203
  148.5 44.7 %collective-permute-start.7 = (bf16[512,128]{1,0:T(8,128)(2,1)}, bf16[512,128]{1,0:T(8,128)(2,1)S(1)}, u32[]{:S(2)}, u32[]{:S(2)}) collective-permute-start(bf16[512,128]{1,0:T(8,128)(2,1)} %copy-done.22), channel_id=1, source_target_pairs={{0,16},{4,20},{8,24},{12,28},{16,0},{20,4},{24,8},{28,12},{1,17},{... | collective-permute-start | bytes 393224 | tf_op jit(solution)/shard_map/ppermute | solution.py:203
  150.8 43.0 %collective-permute-start.8 = (bf16[512,128]{1,0:T(8,128)(2,1)}, bf16[512,128]{1,0:T(8,128)(2,1)S(1)}, u32[]{:S(2)}, u32[]{:S(2)}) collective-permute-start(bf16[512,128]{1,0:T(8,128)(2,1)} %copy-done.21), channel_id=1, source_target_pairs={{0,24},{4,28},{8,16},{12,20},{16,8},{20,12},{24,0},{28,4},{1,25},{... | collective-permute-start | bytes 393224 | tf_op jit(solution)/shard_map/ppermute | solution.py:203
  159.5 0.6 copy-start.11
  160.2 0.7 copy-start.24
  160.8 0.6 copy-start.25
  161.5 0.6 copy-start.26
  193.2 0.7 copy-start.7
  193.9 0.7 copy-start.9
  194.5 51.6 %all-to-all-start.3 = ((bf16[8,256,384]{2,1,0:T(8,128)(2,1)}), bf16[8,256,384]{2,1,0:T(8,128)(2,1)S(1)}, u32[]{:S(2)}, u32[]{:S(2)}) async-start(bf16[8,256,384]{2,1,0:T(8,128)(2,1)} %copy-done.4), calls=%async_computation.3 | async-start | bytes 3145728 | tf_op jit(solution)/shard_map/all_to_all | solution.py:193
  198.3 29.4 %collective-permute-start.9 = (bf16[512,128]{1,0:T(8,128)(2,1)}, bf16[512,128]{1,0:T(8,128)(2,1)S(1)}, u32[]{:S(2)}, u32[]{:S(2)}) collective-permute-start(bf16[512,128]{1,0:T(8,128)(2,1)} %copy-done.26), channel_id=1, source_target_pairs={{0,8},{4,12},{8,0},{12,4},{16,24},{20,28},{24,16},{28,20},{1,9},{5... | collective-permute-start | bytes 393224 | tf_op jit(solution)/shard_map/ppermute | solution.py:203
  200.5 44.2 %collective-permute-start.10 = (bf16[512,128]{1,0:T(8,128)(2,1)}, bf16[512,128]{1,0:T(8,128)(2,1)S(1)}, u32[]{:S(2)}, u32[]{:S(2)}) collective-permute-start(bf16[512,128]{1,0:T(8,128)(2,1)} %copy-done.25), channel_id=1, source_target_pairs={{0,16},{4,20},{8,24},{12,28},{16,0},{20,4},{24,8},{28,12},{1,17},{... | collective-permute-start | bytes 393224 | tf_op jit(solution)/shard_map/ppermute | solution.py:203
  202.4 43.0 %collective-permute-start.11 = (bf16[512,128]{1,0:T(8,128)(2,1)}, bf16[512,128]{1,0:T(8,128)(2,1)S(1)}, u32[]{:S(2)}, u32[]{:S(2)}) collective-permute-start(bf16[512,128]{1,0:T(8,128)(2,1)} %copy-done.24), channel_id=1, source_target_pairs={{0,24},{4,28},{8,16},{12,20},{16,8},{20,12},{24,0},{28,4},{1,25},{... | collective-permute-start | bytes 393224 | tf_op jit(solution)/shard_map/ppermute | solution.py:203
  211.7 0.6 copy-start.19
  212.3 0.6 copy-start.27
  213.0 0.6 copy-start.28
  213.6 0.6 copy-start.29
  214.3 51.3 %copy-start.8 = (bf16[512,128]{1,0:T(8,128)(2,1)S(1)}, bf16[512,128]{1,0:T(8,128)(2,1)}, u32[]{:S(2)}) copy-start(bf16[512,128]{1,0:T(8,128)(2,1)} %copy-done.7) | copy-start | bytes 393220
  214.3 51.3 %copy-start.10 = (bf16[512,128]{1,0:T(8,128)(2,1)S(1)}, bf16[512,128]{1,0:T(8,128)(2,1)}, u32[]{:S(2)}) copy-start(bf16[512,128]{1,0:T(8,128)(2,1)} %copy-done.9) | copy-start | bytes 393220
  214.3 51.3 %copy-start.12 = (bf16[512,128]{1,0:T(8,128)(2,1)S(1)}, bf16[512,128]{1,0:T(8,128)(2,1)}, u32[]{:S(2)}) copy-start(bf16[512,128]{1,0:T(8,128)(2,1)} %copy-done.11) | copy-start | bytes 393220
  227.7 0.6 copy-start.13
  228.4 37.2 %copy-start.20 = (bf16[512,128]{1,0:T(8,128)(2,1)S(1)}, bf16[512,128]{1,0:T(8,128)(2,1)}, u32[]{:S(2)}) copy-start(bf16[512,128]{1,0:T(8,128)(2,1)} %copy-done.19) | copy-start | bytes 393220
  244.8 0.7 copy-start.15
  245.4 20.2 %copy-start.14 = (bf16[512,128]{1,0:T(8,128)(2,1)S(1)}, bf16[512,128]{1,0:T(8,128)(2,1)}, u32[]{:S(2)}) copy-start(bf16[512,128]{1,0:T(8,128)(2,1)} %copy-done.13) | copy-start | bytes 393220
  245.4 0.7 copy-start.17
  246.1 19.5 %copy-start.16 = (bf16[512,128]{1,0:T(8,128)(2,1)S(1)}, bf16[512,128]{1,0:T(8,128)(2,1)}, u32[]{:S(2)}) copy-start(bf16[512,128]{1,0:T(8,128)(2,1)} %copy-done.15) | copy-start | bytes 393220
  246.1 19.5 %copy-start.18 = (bf16[512,128]{1,0:T(8,128)(2,1)S(1)}, bf16[512,128]{1,0:T(8,128)(2,1)}, u32[]{:S(2)}) copy-start(bf16[512,128]{1,0:T(8,128)(2,1)} %copy-done.17) | copy-start | bytes 393220
  246.1 14.6 %collective-permute-start.12 = (bf16[512,128]{1,0:T(8,128)(2,1)}, bf16[512,128]{1,0:T(8,128)(2,1)S(1)}, u32[]{:S(2)}, u32[]{:S(2)}) collective-permute-start(bf16[512,128]{1,0:T(8,128)(2,1)} %copy-done.29), channel_id=1, source_target_pairs={{0,8},{4,12},{8,0},{12,4},{16,24},{20,28},{24,16},{28,20},{1,9},{5... | collective-permute-start | bytes 393224 | tf_op jit(solution)/shard_map/ppermute | solution.py:203
  248.3 12.8 %collective-permute-start.13 = (bf16[512,128]{1,0:T(8,128)(2,1)}, bf16[512,128]{1,0:T(8,128)(2,1)S(1)}, u32[]{:S(2)}, u32[]{:S(2)}) collective-permute-start(bf16[512,128]{1,0:T(8,128)(2,1)} %copy-done.28), channel_id=1, source_target_pairs={{0,16},{4,20},{8,24},{12,28},{16,0},{20,4},{24,8},{28,12},{1,17},{... | collective-permute-start | bytes 393224 | tf_op jit(solution)/shard_map/ppermute | solution.py:203
  248.3 12.8 %collective-permute-start.14 = (bf16[512,128]{1,0:T(8,128)(2,1)}, bf16[512,128]{1,0:T(8,128)(2,1)S(1)}, u32[]{:S(2)}, u32[]{:S(2)}) collective-permute-start(bf16[512,128]{1,0:T(8,128)(2,1)} %copy-done.27), channel_id=1, source_target_pairs={{0,24},{4,28},{8,16},{12,20},{16,8},{20,12},{24,0},{28,4},{1,25},{... | collective-permute-start | bytes 393224 | tf_op jit(solution)/shard_map/ppermute | solution.py:203
  261.1 14.4 %collective-permute-start.15 = (bf16[512,128]{1,0:T(8,128)(2,1)}, bf16[512,128]{1,0:T(8,128)(2,1)S(1)}, u32[]{:S(2)}, u32[]{:S(2)}) collective-permute-start(bf16[512,128]{1,0:T(8,128)(2,1)} %get-tuple-element.128), channel_id=1, source_target_pairs={{0,8},{4,12},{8,0},{12,4},{16,24},{20,28},{24,16},{28,20},{1,9},{5... | collective-permute-start | bytes 393224 | tf_op jit(solution)/shard_map/ppermute | solution.py:203
  263.2 12.4 %collective-permute-start.16 = (bf16[512,128]{1,0:T(8,128)(2,1)}, bf16[512,128]{1,0:T(8,128)(2,1)S(1)}, u32[]{:S(2)}, u32[]{:S(2)}) collective-permute-start(bf16[512,128]{1,0:T(8,128)(2,1)} %get-tuple-element.129), channel_id=1, source_target_pairs={{0,16},{4,20},{8,24},{12,28},{16,0},{20,4},{24,8},{28,12},{1,17},{... | collective-permute-start | bytes 393224 | tf_op jit(solution)/shard_map/ppermute | solution.py:203
  263.4 12.2 %collective-permute-start.17 = (bf16[512,128]{1,0:T(8,128)(2,1)}, bf16[512,128]{1,0:T(8,128)(2,1)S(1)}, u32[]{:S(2)}, u32[]{:S(2)}) collective-permute-start(bf16[512,128]{1,0:T(8,128)(2,1)} %get-tuple-element.130), channel_id=1, source_target_pairs={{0,24},{4,28},{8,16},{12,20},{16,8},{20,12},{24,0},{28,4},{1,25},{... | collective-permute-start | bytes 393224 | tf_op jit(solution)/shard_map/ppermute | solution.py:203
  281.8 3.5 %collective-permute-start.18 = (bf16[256,3072]{1,0:T(8,128)(2,1)S(1)}, bf16[256,3072]{1,0:T(8,128)(2,1)S(1)}, u32[]{:S(2)}, u32[]{:S(2)}) collective-permute-start(bf16[256,3072]{1,0:T(8,128)(2,1)S(1)} %get-tuple-element.144), channel_id=1, source_target_pairs={{0,4},{4,0},{8,12},{12,8},{16,20},{20,16},{24,28},{28,24},{1,5},{5... | collective-permute-start | bytes 4718600 | tf_op jit(solution)/shard_map/ppermute | solution.py:203
Sparse Core Ops, SparseCore 0:
  32.2 72.3 all-gather.4
  142.9 70.2 all-gather.6

commit v3 on v2

v3 whole, which is shorter than its diff:
```python
import functools
import math

import jax
import jax.numpy as jnp
from jax import lax
from jax.experimental import pallas as pl
from jax.experimental.pallas import tpu as pltpu
from jax.sharding import PartitionSpec as P

BLOCK = 128
VMEM = pl.BlockSpec(memory_space=pltpu.VMEM)
SMEM = pl.BlockSpec(memory_space=pltpu.SMEM)
ANY = pl.BlockSpec(memory_space=pl.ANY)
FREE = pl.CostEstimate(flops=1, bytes_accessed=1, transcendentals=0)


def limit(mib):
    return pltpu.CompilerParams(vmem_limit_bytes=mib * 1024 * 1024)


def layout_kernel(steps, here, width, place_ref, *refs):
    fields, sem = refs[:3], refs[-1]
    out_refs = refs[-1 - len(steps) : -1]
    copies = []
    for m, (joined, out_ref) in enumerate(zip(steps, out_refs)):
        for k, step in enumerate(joined):
            for g in range(out_ref.shape[0]):
                start = pl.multiple_of((g * here + (place_ref[0] ^ step)) * width, width)
                for n, field in enumerate(fields):
                    copies.append(
                        pltpu.make_async_copy(
                            field.at[:, pl.ds(start, width)],
                            out_ref.at[g, :, pl.ds((3 * k + n) * width, width)],
                            sem.at[m, k, g, n],
                        )
                    )
    for copy in copies:
        copy.start()
    for copy in copies:
        copy.wait()


def lay_out(fields, place, steps, groups, here, width, extra):
    tokens = fields[0].shape[0]
    count = len(steps)
    most = max(len(joined) for joined in steps)
    return pl.pallas_call(
        functools.partial(layout_kernel, steps, here, width),
        out_shape=[jax.ShapeDtypeStruct((groups, tokens, 3 * width * len(joined)), jnp.bfloat16) for joined in steps],
        in_specs=[SMEM] + [ANY] * (3 + len(extra)),
        out_specs=[ANY] * count,
        scratch_shapes=[pltpu.SemaphoreType.DMA((count, most, groups, 3))],
        compiler_params=limit(16),
        cost_estimate=FREE,
    )(place, *fields, *extra)


def attend_kernel(step, at_lane, width, slots, place_ref, lists_ref, counts_ref, *refs):
    qkv_ref, out_refs, held = refs[0], refs[1:-1], refs[-1]
    sources, tokens, _ = qkv_ref.shape
    member = place_ref[0] ^ step
    per = tokens // BLOCK
    scale = width ** (-0.5) * math.log2(math.e)
    q_cols, k_cols, v_cols = (slice(at_lane + n * width, at_lane + (n + 1) * width) for n in range(3))

    def rows_of(block):
        return block // per, pl.ds(pl.multiple_of((block % per) * BLOCK, BLOCK), BLOCK)

    def place_of(at):
        part = at // per
        src = part ^ place_ref[1]
        return part, src, pl.ds(pl.multiple_of((at % per) * BLOCK, BLOCK), BLOCK), src * per + at % per

    def branch(blocks):
        picked = [
            [rows_of(lists_ref[member, i * slots + j]) for j in range(2 * pairs)] for _, _, _, i, pairs in blocks
        ]

        def gathered(b, n, cols):
            return jnp.concatenate([qkv_ref[s, r, cols] for s, r in picked[b][2 * n : 2 * n + 2]], axis=0)

        scores = []
        for b, (_, src, rows, i, pairs) in enumerate(blocks):
            q = qkv_ref[src, rows, q_cols]
            found = [
                lax.dot_general(
                    q, gathered(b, n, k_cols), (((1,), (1,)), ((), ())), preferred_element_type=jnp.float32
                )
                for n in range(pairs)
            ]
            usable = BLOCK * (counts_ref[member, i] - 2 * (pairs - 1))
            column = lax.broadcasted_iota(jnp.int32, found[-1].shape, 1)
            found[-1] = jnp.where(column < usable, found[-1], -jnp.inf)
            scores.append(found)
        tops = [jnp.max(functools.reduce(jnp.maximum, found), axis=1, keepdims=True) * scale for found in scores]
        weights = [[jnp.exp2(x * scale - top) for x in found] for found, top in zip(scores, tops)]
        totals = [jnp.sum(functools.reduce(jnp.add, found), axis=1, keepdims=True) for found in weights]
        for b, (part, _, rows, _, pairs) in enumerate(blocks):
            mixed = [
                jnp.dot(weights[b][n].astype(jnp.bfloat16), gathered(b, n, v_cols), preferred_element_type=jnp.float32)
                for n in range(pairs)
            ]
            held[part, rows, :] = (functools.reduce(jnp.add, mixed) / totals[b]).astype(held.dtype)

    def two(at, carry):
        here = [place_of(2 * at), place_of(2 * at + 1)]
        pairs = [(counts_ref[member, x[3]] + 1) // 2 for x in here]
        more = pairs[0] >= pairs[1]
        first = place_of(2 * at + jnp.where(more, 0, 1))
        second = place_of(2 * at + jnp.where(more, 1, 0))
        high, low = jnp.maximum(*pairs), jnp.minimum(*pairs)
        for m in range(1, slots // 2 + 1):
            for n in range(1, m + 1):
                pl.when((high == m) & (low == n))(functools.partial(branch, [first + (m,), second + (n,)]))
        return carry

    lax.fori_loop(0, sources * per // 2, two, 0)
    each = sources // len(out_refs)
    for n, out_ref in enumerate(out_refs):
        for m in range(each):
            out_ref[m * tokens : (m + 1) * tokens, :] = held[n * each + m]


def attend(qkv, place, lists, counts, step, width, each, at_lane=0):
    sources, tokens, _ = qkv.shape
    slots = lists.shape[1] // counts.shape[1]
    return pl.pallas_call(
        functools.partial(attend_kernel, step, at_lane, width, slots),
        out_shape=[jax.ShapeDtypeStruct((each * tokens, width), jnp.bfloat16)] * (sources // each),
        in_specs=[SMEM, SMEM, SMEM, VMEM],
        out_specs=[VMEM] * (sources // each),
        scratch_shapes=[pltpu.VMEM((sources, tokens, width), jnp.bfloat16)],
        compiler_params=limit(24),
        cost_estimate=FREE,
    )(place, lists, counts, qkv)


def project_kernel(terms, n_rows, n_blocks, n_before, *refs):
    rows, blocks = refs[:n_rows], refs[n_rows : n_rows + n_blocks]
    before = refs[n_rows + n_blocks : n_rows + n_blocks + n_before]
    out_refs = refs[n_rows + n_blocks + n_before : -4]
    held, lefts, sem, row_sem = refs[-4:]
    slots = held.shape[0]
    row_copies = []
    for n, (_, picked, cut) in enumerate(terms):
        for k, r in enumerate(picked):
            wide = rows[r].shape[1]
            target = lefts.at[n, :, pl.ds(k * wide, wide)]
            row_copies.append(pltpu.make_async_copy(rows[r].at[pl.ds(cut.start, cut.stop - cut.start), :], target, row_sem.at[n, k]))
    copies = []
    for n, (pieces, _, _) in enumerate(terms):
        at = 0
        copies.append([])
        for k, piece in enumerate(pieces):
            tall = blocks[piece].shape[0]
            target = held.at[n % slots, pl.ds(at, tall), :]
            copies[-1].append(pltpu.make_async_copy(blocks[piece], target, sem.at[n % slots, k]))
            at += tall
    for copy in row_copies + sum(copies[:slots], []):
        copy.start()
    for copy in row_copies:
        copy.wait()
    step = held.shape[-1] // 4
    for n in range(len(terms)):
        for copy in copies[n]:
            copy.wait()
        left = lefts[n]
        for at in range(0, held.shape[-1], step):
            cols = slice(at, at + step)
            part = jnp.dot(left, held[n % slots, :, cols], preferred_element_type=jnp.float32)
            tall = part.shape[0] // len(out_refs)
            for m, out_ref in enumerate(out_refs):
                mine = part[m * tall : (m + 1) * tall]
                if n:
                    mine = mine + out_ref[:, cols]
                elif before:
                    mine = mine + before[m][:, cols]
                out_ref[:, cols] = mine
        if n + slots < len(terms):
            for copy in copies[n + slots]:
                copy.start()


def project(rows, blocks, terms, before, outs):
    cut = terms[0][2]
    tall = cut.stop - cut.start
    wide = blocks[0].shape[1]
    depth = sum(blocks[piece].shape[0] for piece in terms[0][0])
    slots = min(4, len(terms))
    return pl.pallas_call(
        functools.partial(project_kernel, terms, len(rows), len(blocks), len(before)),
        out_shape=[jax.ShapeDtypeStruct((tall // outs, wide), jnp.float32)] * outs,
        in_specs=[ANY] * (len(rows) + len(blocks)) + [VMEM] * len(before),
        out_specs=[VMEM] * outs,
        scratch_shapes=[
            pltpu.VMEM((slots, depth, wide), jnp.bfloat16),
            pltpu.VMEM((len(terms), tall, depth), jnp.bfloat16),
            pltpu.SemaphoreType.DMA((slots, 2)),
            pltpu.SemaphoreType.DMA((len(terms), 2)),
        ],
        compiler_params=limit(28),
        cost_estimate=FREE,
    )(*rows, *blocks, *before)


def along_z(pairs):
    return [(2 * i + c, 2 * j + c) for i, j in pairs for c in (0, 1)]


def after(value, *others):
    return lax.optimization_barrier((value, *others))[0]


def xor(p, groups):
    return [(i, i ^ p) for i in range(groups)]


UP = [(0, 1), (1, 2), (2, 3)]
DOWN = [(j, i) for i, j in UP]


def exchange(x):
    return lax.all_to_all(x, "seq", split_axis=0, concat_axis=0, tiled=True)


def shards_lines(fields, weight, rank, lists, counts, here, width):
    groups = 8
    chip = lax.axis_index("seq") // 2
    place = jnp.stack([lax.axis_index("fsdp"), rank]).astype(jnp.int32)
    n, tokens = weight.shape[0], fields[0].shape[0]

    def along(value, axis, pairs):
        return lax.ppermute(value, axis, pairs)

    def send_back(out):
        return [out[0]] + [along(out[p], "seq", xor(2 * p, groups)) for p in (1, 2, 3)]

    def attend_step(qkv, step, at_lane=0):
        return attend(qkv, place, lists, counts, step, width, 2, at_lane)

    def sides(block):
        return [along(block, "fsdp", xor(1, 4)), along(block, "fsdp", xor(2, 4))]

    def corner(x, y):
        return [along(x[:n], "fsdp", xor(2, 4)), along(y[n:], "fsdp", xor(1, 4))]

    def fence(*values):
        return lax.optimization_barrier(values)

    (x0,) = lay_out(fields, place, ((0,),), groups, here, width, [])
    qkv0 = exchange(x0)
    weight = after(weight, x0)
    up, down = along(weight, "seq", along_z(UP)), along(weight, "seq", along_z(DOWN))
    x1, x2, x3 = lay_out(fields, place, ((1,), (2,), (3,)), groups, here, width, [x0])
    up, down, qkv0, x1, x2, x3 = fence(up, down, qkv0, x1, x2, x3)
    near = jnp.concatenate([weight, jnp.where(chip % 2 == 0, down, up)], axis=0)
    qkv1 = exchange(x1)
    up2, down2 = along(up, "seq", along_z(UP[1:])), along(down, "seq", along_z(DOWN[:2]))
    near_sides = sides(near)
    out0 = attend_step(qkv0, 0)
    up2, down2, qkv1, near_sides, out0 = fence(up2, down2, qkv1, near_sides, out0)
    qkv2 = exchange(after(x2, qkv1))
    last = along(jnp.where(chip == 2, up2, down2), "seq", along_z([(1, 0), (2, 3)]))
    near_corner = [along(near, "fsdp", xor(3, 4))]
    back0 = send_back(out0)
    out1 = attend_step(qkv1, 1)
    last, qkv2, back0, near_corner = fence(last, qkv2, back0, near_corner)
    inner = (chip == 1) | (chip == 2)
    low = chip < 2
    opposite = jnp.where(inner, jnp.where(low, down, up), last)
    far = jnp.concatenate([jnp.where(low, down2, up2), opposite], axis=0)
    qkv3 = exchange(after(x3, qkv2, *out1))
    far_sides = sides(far)
    back1 = send_back(out1)
    out2 = attend_step(qkv2, 2)
    qkv3, far_sides, back1, out2 = fence(qkv3, far_sides, back1, out2)
    back2 = send_back(out2)
    far_corner = corner(*far_sides)
    out3 = attend_step(qkv3, 3)
    back0, back1, back2, out3 = fence(back0, back1, back2, out3)
    back3 = send_back(out3)

    blocks = [near] + near_sides + near_corner + [far] + far_sides + far_corner
    both, own, other = slice(0, 2 * tokens), slice(0, tokens), slice(tokens, 2 * tokens)

    def terms(step, at, cut):
        last = (7, 8) if step == 3 else (4 + step,)
        return [((step,), (4 * at, 4 * at + 1), cut), (last, (4 * at + 2, 4 * at + 3), cut)]

    early = terms(0, 0, both) + terms(1, 1, both) + terms(2, 2, both)
    mine, theirs = project(back0 + back1 + back2, blocks, early, [], 2)
    (theirs,) = project(back3, blocks, terms(3, 0, other), [theirs], 1)
    given = along(theirs.astype(jnp.bfloat16), "seq", xor(1, groups))
    (mine,) = project(back3, blocks, terms(3, 0, own), [mine], 1)
    return (mine + given.astype(jnp.float32)).astype(jnp.bfloat16)


def shards_any(fields, weight, rank, lists, counts, here, width, groups):
    place = jnp.stack([0 * rank, rank]).astype(jnp.int32)
    rows = weight.shape[0]
    gathered = lax.all_gather(weight, ("fsdp", "seq"), axis=0, tiled=True)
    gathered = gathered.reshape(here, width // rows, groups, rows, -1).transpose(0, 2, 1, 3, 4)
    gathered = gathered.reshape(here, groups, width, -1)
    ready = lay_out(fields, place, tuple((m,) for m in range(here)), groups, here, width, [])
    result = None
    for member in range(here):
        out = attend(exchange(ready[member]), place, lists, counts, member, width, 1)
        for p in range(groups):
            part = jnp.dot(
                lax.ppermute(out[p], "seq", xor(p, groups)) if p else out[0],
                lax.dynamic_index_in_dim(gathered[member], rank ^ p, 0, keepdims=False),
                preferred_element_type=jnp.float32,
            )
            result = part if result is None else result + part
    return result.astype(jnp.bfloat16)


def shards(queries, keys, values, out_weight, block_lists, block_counts):
    groups = lax.axis_size("seq")
    rank = lax.axis_index("seq")
    head_count = block_counts.shape[1]
    width = queries.shape[2] // head_count
    here = head_count // groups
    lists = lax.dynamic_slice_in_dim(block_lists[0], rank * here, here).reshape(here, -1)
    counts = lax.dynamic_slice_in_dim(block_counts[0], rank * here, here)
    fields = [x[0] for x in (queries, keys, values)]
    if groups == 8 and here == 4 and lax.axis_size("fsdp") == 4 and out_weight.shape[0] == width:
        result = shards_lines(fields, out_weight, rank, lists, counts, here, width)
    else:
        result = shards_any(fields, out_weight, rank, lists, counts, here, width, groups)
    return result[None]


def solution(mesh):
    return jax.shard_map(
        shards,
        mesh=mesh,
        in_specs=(
            P("fsdp", "seq", None),
            P("fsdp", "seq", None),
            P("fsdp", "seq", None),
            P(("seq", "fsdp"), None),
            P("fsdp", None, None, None),
            P("fsdp", None, None),
        ),
        out_specs=P("fsdp", "seq", None),
        check_vma=False,
    )
```

time: 294 us -> 282 us (0.959)
  starting transfers between devices: 55.8 us -> 75.5 us
  waiting for transfers between devices: 144 us -> 126 us
  between operations: 13.7 us -> 0.42 us
  Pallas kernels: 53.7 us -> 41.1 us
  local copies, waits for them, and re-layouts: 18.4 us -> 29.5 us
    ppermute x19 -> x25, waiting for transfers between devices: 144 us -> 126 us  [along(): return lax.ppermute(value, axis, pairs)]
    ppermute x19 -> x25, starting transfers between devices: 31.2 us -> 42.6 us  [along(): return lax.ppermute(value, axis, pairs)]
    unnamed x74 -> x96, local copies, waits for them, and re-layouts: 18 us -> 27.9 us
    all_to_all x4, starting transfers between devices: 24.6 us -> 32.8 us  [exchange(): return lax.all_to_all(x, 'seq', split_axis=0, concat_axis=0, tiled=True)]
    pallas_call x5 -> x6, Pallas kernels: 37.5 us -> 31.1 us  [the longest x4 26.6 us: attend(): pl.pallas_call(functools.partial(attend_kernel, step, at_lane, width, slo...]
    pallas_call x2 -> x3, Pallas kernels: 16.1 us -> 9.98 us  [project(): pl.pallas_call(functools.partial(project_kernel, terms, len(rows), len(bl...]
  transfers between devices with their start and end apart: 25 -> 29, of which waited for: 10 -> 8; matrix products, arithmetic and copies ran while one was open for 2% -> 2% of each run, Pallas kernels for 16% -> 13%
where the time goes in v3:
time: 282 us; the launch traced here: 281 us
  waiting for transfers between devices  126 us (45%)
  starting transfers between devices  75.5 us (27%)
  Pallas kernels  41.1 us (15%)
  local copies, waits for them, and re-layouts  29.5 us (10%)
  other arithmetic  8.41 us (3%)
    ppermute x25, waiting for transfers between devices, along(): return lax.ppermute(value, axis, pairs)  126 us
    ppermute x25, starting transfers between devices, along(): return lax.ppermute(value, axis, pairs)  42.6 us
    all_to_all x4, starting transfers between devices, exchange(): return lax.all_to_all(x, 'seq', split_axis=0, concat_axis=0, tiled=True)  32.8 us
    unnamed x96, local copies, waits for them, and re-layouts  27.9 us
    pallas_call x4, Pallas kernels, attend(): pl.pallas_call(functools.partial(attend_kernel, step, at_lane, width, slo...  26.6 us
    pallas_call x3, Pallas kernels, project(): pl.pallas_call(functools.partial(project_kernel, terms, len(rows), len(bl...  9.98 us
  transfers between devices with their start and end apart: 29, of which 8 were waited for; matrix products, arithmetic and copies ran while one was open for 2% of the time, Pallas kernels for 13%

profile of v3, /device:TPU:0, one launch (start us, length us, event | category | flops | bytes accessed | tf_op | source)
XLA Modules:
  0.0 280.6 jit_solution(16721033774590705352)
XLA Ops:
  0.1 1.6 copy-done.7
  1.7 1.6 copy-done.9
  3.3 1.6 copy-done.11
  4.9 1.9 shard_map.64.refs_3_
  6.7 6.5 %all-to-all-start = ((bf16[8,256,384]{2,1,0:T(8,128)(2,1)}), bf16[8,256,384]{2,1,0:T(8,128)(2,1)}, u32[]{:S(2)}, u32[]{:S(2)}) async-start(bf16[8,256,384]{2,1,0:T(8,128)(2,1)} %shard_map.64.refs_3_), calls=%async_computation | async-start | bytes 3145728 | tf_op jit(solution)/shard_map/all_to_all | solution.py:224
  13.2 1.3 collective-permute-start.1
  14.5 4.6 %collective-permute-start = (bf16[128,3072]{1,0:T(8,128)(2,1)}, bf16[128,3072]{1,0:T(8,128)(2,1)S(1)}, u32[]{:S(2)}, u32[]{:S(2)}) collective-permute-start(bf16[128,3072]{1,0:T(8,128)(2,1)} %param.9), channel_id=1, source_target_pairs={{0,8},{4,12},{8,16},{12,20},{16,24},{20,28},{1,9},{5,13},{9,17},{1... | collective-permute-start | bytes 2359304 | tf_op jit(solution)/shard_map/ppermute | solution.py:234
  19.1 1.6 copy-done.10
  20.7 1.6 copy-done.12
  22.3 2.6 shard_map.65
  25.0 1.1 copy-done.13
  26.1 32.6 %collective-permute-done.1 = bf16[128,3072]{1,0:T(8,128)(2,1)} collective-permute-done((bf16[128,3072]{1,0:T(8,128)(2,1)}, bf16[128,3072]{1,0:T(8,128)(2,1)}, u32[]{:S(2)}, u32[]{:S(2)}) %collective-permute-start.1) | collective-permute-done | bytes 786464 | tf_op jit(solution)/shard_map/ppermute | solution.py:234
  58.7 11.2 %all-to-all-start.1 = ((bf16[8,256,384]{2,1,0:T(8,128)(2,1)}), bf16[8,256,384]{2,1,0:T(8,128)(2,1)}, u32[]{:S(2)}, u32[]{:S(2)}) async-start(bf16[8,256,384]{2,1,0:T(8,128)(2,1)} %copy-done.15), calls=%async_computation.1 | async-start | bytes 3145728 | tf_op jit(solution)/shard_map/all_to_all | solution.py:224
  69.9 1.2 broadcast_select_fusion.1
  71.2 1.2 pad_maximum_fusion.refs_12_.refs_4_
  72.4 1.6 collective-permute-start.5
  74.0 1.5 collective-permute-start.4
  75.5 1.6 collective-permute-start.2
  77.1 1.3 collective-permute-start.3
  78.7 6.1 %shard_map.66 = (bf16[512,128]{1,0:T(8,128)(2,1)S(1)}, bf16[512,128]{1,0:T(8,128)(2,1)S(1)}, bf16[512,128]{1,0:T(8,128)(2,1)S(1)}, bf16[512,128]{1,0:T(8,128)(2,1)S(1)}) custom-call(s32[2]{0:T(128)S(1)} %pad_add_fusion.place_ref, s32[4,128]{1,0:T(4,128)S(1)} %copy.11.lists_ref, s32[4,16]{1,0:T(4,128)S(1)} %bitcast.16, bf16[8,256,384]{2,1,0:T(8,128)(2,1)} %all-to-all-done.refs_0_), custom_call_target="tpu_custom_call" | custom-call | flops 1 | bytes 1 | tf_op jit(solution)/shard_map/pallas_call | solution.py:128
  86.1 29.7 %collective-permute-done.3 = bf16[128,3072]{1,0:T(8,128)(2,1)} collective-permute-done((bf16[128,3072]{1,0:T(8,128)(2,1)}, bf16[128,3072]{1,0:T(8,128)(2,1)}, u32[]{:S(2)}, u32[]{:S(2)}) %collective-permute-start.3) | collective-permute-done | bytes 786464 | tf_op jit(solution)/shard_map/ppermute | solution.py:234
  115.8 1.1 copy-done.3
  116.9 10.8 %all-to-all-start.2 = ((bf16[8,256,384]{2,1,0:T(8,128)(2,1)}), bf16[8,256,384]{2,1,0:T(8,128)(2,1)}, u32[]{:S(2)}, u32[]{:S(2)}) async-start(bf16[8,256,384]{2,1,0:T(8,128)(2,1)} %copy-done.14), calls=%async_computation.2 | async-start | bytes 3145728 | tf_op jit(solution)/shard_map/all_to_all | solution.py:224
  127.8 2.4 collective-permute-start.10
  130.2 2.4 broadcast_select_fusion
  132.7 1.5 collective-permute-start.6
  134.1 3.8 %collective-permute-start.7 = (bf16[512,128]{1,0:T(8,128)(2,1)S(1)}, bf16[512,128]{1,0:T(8,128)(2,1)S(1)}, u32[]{:S(2)}, u32[]{:S(2)}) collective-permute-start(bf16[512,128]{1,0:T(8,128)(2,1)S(1)} %copy-done.42), channel_id=1, source_target_pairs={{0,8},{4,12},{8,0},{12,4},{16,24},{20,28},{24,16},{28,20},{1,9},{5... | collective-permute-start | bytes 393224 | tf_op jit(solution)/shard_map/ppermute | solution.py:234
  137.9 2.0 collective-permute-start.8
  139.9 1.5 collective-permute-start.9
  141.4 7.1 %shard_map.67 = (bf16[512,128]{1,0:T(8,128)(2,1)S(1)}, bf16[512,128]{1,0:T(8,128)(2,1)S(1)}, bf16[512,128]{1,0:T(8,128)(2,1)S(1)}, bf16[512,128]{1,0:T(8,128)(2,1)S(1)}) custom-call(s32[2]{0:T(128)S(1)} %pad_add_fusion.place_ref, s32[4,128]{1,0:T(4,128)S(1)} %copy.11.lists_ref, s32[4,16]{1,0:T(4,128)S(1)} %bitcast.17, ...), custom_call_target="tpu_custom_call" | custom-call | flops 1 | bytes 1 | tf_op jit(solution)/shard_map/pallas_call | solution.py:128
  151.1 14.4 %collective-permute-done.10.refs_15_.refs_7_ = bf16[256,3072]{1,0:T(8,128)(2,1)S(1)} collective-permute-done((bf16[256,3072]{1,0:T(8,128)(2,1)S(1)}, bf16[256,3072]{1,0:T(8,128)(2,1)S(1)}, u32[]{:S(2)}, u32[]{:S(2)}) %collective-permute-start.10) | collective-permute-done | bytes 1572896 | tf_op jit(solution)/shard_map/ppermute | solution.py:234
  165.5 16.5 %collective-permute-done.7.refs_1_ = bf16[512,128]{1,0:T(8,128)(2,1)S(1)} collective-permute-done((bf16[512,128]{1,0:T(8,128)(2,1)S(1)}, bf16[512,128]{1,0:T(8,128)(2,1)S(1)}, u32[]{:S(2)}, u32[]{:S(2)}) %collective-permute-start.7) | collective-permute-done | bytes 131104 | tf_op jit(solution)/shard_map/ppermute | solution.py:234
  183.3 4.3 %all-to-all-start.3 = ((bf16[8,256,384]{2,1,0:T(8,128)(2,1)}), bf16[8,256,384]{2,1,0:T(8,128)(2,1)}, u32[]{:S(2)}, u32[]{:S(2)}) async-start(bf16[8,256,384]{2,1,0:T(8,128)(2,1)} %copy-done.13), calls=%async_computation.3 | async-start | bytes 3145728 | tf_op jit(solution)/shard_map/all_to_all | solution.py:224
  187.6 1.6 select_select_fusion
  189.3 1.6 collective-permute-start.12
  190.9 1.5 collective-permute-start.11
  192.4 1.6 collective-permute-start.13
  194.1 2.6 collective-permute-start.14
  196.8 7.1 %shard_map.68 = (bf16[512,128]{1,0:T(8,128)(2,1)S(1)}, bf16[512,128]{1,0:T(8,128)(2,1)S(1)}, bf16[512,128]{1,0:T(8,128)(2,1)S(1)}, bf16[512,128]{1,0:T(8,128)(2,1)S(1)}) custom-call(s32[2]{0:T(128)S(1)} %pad_add_fusion.place_ref, s32[4,128]{1,0:T(4,128)S(1)} %copy.11.lists_ref, s32[4,16]{1,0:T(4,128)S(1)} %bitcast.18, ...), custom_call_target="tpu_custom_call" | custom-call | flops 1 | bytes 1 | tf_op jit(solution)/shard_map/pallas_call | solution.py:128
  206.6 10.4 %collective-permute-done.13.refs_5_ = bf16[512,128]{1,0:T(8,128)(2,1)S(1)} collective-permute-done((bf16[512,128]{1,0:T(8,128)(2,1)S(1)}, bf16[512,128]{1,0:T(8,128)(2,1)S(1)}, u32[]{:S(2)}, u32[]{:S(2)}) %collective-permute-start.13) | collective-permute-done | bytes 131104 | tf_op jit(solution)/shard_map/ppermute | solution.py:234
  217.0 0.7 copy-done.22
  217.6 16.6 %collective-permute-done.14.refs_6_ = bf16[512,128]{1,0:T(8,128)(2,1)S(1)} collective-permute-done((bf16[512,128]{1,0:T(8,128)(2,1)S(1)}, bf16[512,128]{1,0:T(8,128)(2,1)S(1)}, u32[]{:S(2)}, u32[]{:S(2)}) %collective-permute-start.14) | collective-permute-done | bytes 131104 | tf_op jit(solution)/shard_map/ppermute | solution.py:234
  235.5 1.2 copy-done.1
  236.8 1.3 slice.6
  238.5 1.6 collective-permute-start.23
  240.0 1.5 collective-permute-start.22
  241.5 2.2 collective-permute-start.16
  243.8 2.4 collective-permute-start.18
  246.1 6.3 %shard_map.69 = (bf16[512,128]{1,0:T(8,128)(2,1)S(1)}, bf16[512,128]{1,0:T(8,128)(2,1)S(1)}, bf16[512,128]{1,0:T(8,128)(2,1)S(1)}, bf16[512,128]{1,0:T(8,128)(2,1)S(1)}) custom-call(s32[2]{0:T(128)S(1)} %pad_add_fusion.place_ref, s32[4,128]{1,0:T(4,128)S(1)} %copy.11.lists_ref, s32[4,16]{1,0:T(4,128)S(1)} %bitcast.19, ...), custom_call_target="tpu_custom_call" | custom-call | flops 1 | bytes 1 | tf_op jit(solution)/shard_map/pallas_call | solution.py:128
  252.4 3.6 %collective-permute-done.17.refs_10_ = bf16[512,128]{1,0:T(8,128)(2,1)S(1)} collective-permute-done((bf16[512,128]{1,0:T(8,128)(2,1)}, bf16[512,128]{1,0:T(8,128)(2,1)S(1)}, u32[]{:S(2)}, u32[]{:S(2)}) %collective-permute-start.17) | collective-permute-done | bytes 131104 | tf_op jit(solution)/shard_map/ppermute | solution.py:234
  256.0 2.1 collective-permute-start.19
  258.3 2.2 collective-permute-start.21
  260.5 0.9 copy-done.17
  261.4 0.9 copy-done.19
  262.3 0.9 copy-done.21
  263.2 0.9 copy-done.23
  264.1 0.9 copy-done.25
  265.0 0.9 copy-done.27
  265.9 0.9 copy-done.29
  266.8 6.9 %shard_map.70 = (f32[256,3072]{1,0:T(8,128)S(1)}, f32[256,3072]{1,0:T(8,128)S(1)}) custom-call(bf16[512,128]{1,0:T(8,128)(2,1)S(1)} %get-tuple-element.137.refs_0_, bf16[512,128]{1,0:T(8,128)(2,1)S(1)} %collective-permute-done.7.refs_1_, bf16[512,128]{1,0:T(8,128)(2,1)S(1)} %copy-done.17, bf16[512,128]{1,0:T(8,128)(2,1)S(1)} %copy-done.19, ...), custom_call_target="tpu_custom_call" | custom-call | flops 1 | bytes 1 | tf_op jit(solution)/shard_map/pallas_call | solution.py:191
  273.8 1.5 shard_map.72
  275.6 1.5 shard_map.71
  277.1 1.9 collective-permute-done.24
  279.0 1.6 fusion
  (113 shorter events, 10.7 us)
Async XLA Ops:
  0.0 78.5 %copy-start = (s32[1,32,16,8]{1,3,2,0:T(8,128)S(1)}, s32[1,32,16,8]{1,3,2,0:T(8,128)}, u32[]{:S(2)}) copy-start(s32[1,32,16,8]{1,3,2,0:T(8,128)} %param.10) | copy-start | bytes 49156
  0.1 1.6 copy-start.7
  1.7 1.6 copy-start.9
  3.3 1.6 copy-start.11
  6.7 12.4 %copy-start.8 = (bf16[1,256,4096]{2,1,0:T(8,128)(2,1)S(1)}, bf16[1,256,4096]{2,1,0:T(8,128)(2,1)}, u32[]{:S(2)}) copy-start(bf16[1,256,4096]{2,1,0:T(8,128)(2,1)} %param.6) | copy-start | bytes 6291460
  6.7 52.0 %all-to-all-start = ((bf16[8,256,384]{2,1,0:T(8,128)(2,1)}), bf16[8,256,384]{2,1,0:T(8,128)(2,1)}, u32[]{:S(2)}, u32[]{:S(2)}) async-start(bf16[8,256,384]{2,1,0:T(8,128)(2,1)} %shard_map.64.refs_3_), calls=%async_computation | async-start | bytes 3145728 | tf_op jit(solution)/shard_map/all_to_all | solution.py:224
  13.2 45.5 %collective-permute-start.1 = (bf16[128,3072]{1,0:T(8,128)(2,1)}, bf16[128,3072]{1,0:T(8,128)(2,1)}, u32[]{:S(2)}, u32[]{:S(2)}) collective-permute-start(bf16[128,3072]{1,0:T(8,128)(2,1)} %param.9), channel_id=1, source_target_pairs={{8,0},{12,4},{16,8},{20,12},{24,16},{28,20},{9,1},{13,5},{17,9},{2... | collective-permute-start | bytes 2359304 | tf_op jit(solution)/shard_map/ppermute | solution.py:234
  14.5 44.2 %collective-permute-start = (bf16[128,3072]{1,0:T(8,128)(2,1)}, bf16[128,3072]{1,0:T(8,128)(2,1)S(1)}, u32[]{:S(2)}, u32[]{:S(2)}) collective-permute-start(bf16[128,3072]{1,0:T(8,128)(2,1)} %param.9), channel_id=1, source_target_pairs={{0,8},{4,12},{8,16},{12,20},{16,24},{20,28},{1,9},{5,13},{9,17},{1... | collective-permute-start | bytes 2359304 | tf_op jit(solution)/shard_map/ppermute | solution.py:234
  19.1 1.6 copy-start.10
  20.7 1.6 copy-start.12
  24.9 1.1 copy-start.13
  26.1 32.6 %copy-start.14 = (bf16[8,256,384]{2,1,0:T(8,128)(2,1)}, bf16[8,256,384]{2,1,0:T(8,128)(2,1)S(1)}, u32[]{:S(2)}) copy-start(bf16[8,256,384]{2,1,0:T(8,128)(2,1)S(1)} %get-tuple-element.94) | copy-start | bytes 4718596
  26.1 32.6 %copy-start.15 = (bf16[8,256,384]{2,1,0:T(8,128)(2,1)}, bf16[8,256,384]{2,1,0:T(8,128)(2,1)S(1)}, u32[]{:S(2)}) copy-start(bf16[8,256,384]{2,1,0:T(8,128)(2,1)S(1)} %get-tuple-element.84) | copy-start | bytes 4718596
  58.7 12.5 %copy-start.45 = (bf16[128,3072]{1,0:T(8,128)(2,1)}, bf16[128,3072]{1,0:T(8,128)(2,1)S(1)}, u32[]{:S(2)}) copy-start(bf16[128,3072]{1,0:T(8,128)(2,1)S(1)} %collective-permute-done) | copy-start | bytes 2359300
  58.7 57.1 %all-to-all-start.1 = ((bf16[8,256,384]{2,1,0:T(8,128)(2,1)}), bf16[8,256,384]{2,1,0:T(8,128)(2,1)}, u32[]{:S(2)}, u32[]{:S(2)}) async-start(bf16[8,256,384]{2,1,0:T(8,128)(2,1)} %copy-done.15), calls=%async_computation.1 | async-start | bytes 3145728 | tf_op jit(solution)/shard_map/all_to_all | solution.py:224
  71.2 7.2 %copy-start.47 = (s32[1,32,16]{1,2,0:T(8,128)S(1)}, s32[1,32,16]{1,2,0:T(8,128)}, u32[]{:S(2)}) copy-start(s32[1,32,16]{1,2,0:T(8,128)} %param.11) | copy-start | bytes 6148
  72.4 43.4 %collective-permute-start.5 = (bf16[256,3072]{1,0:T(8,128)(2,1)S(1)}, bf16[256,3072]{1,0:T(8,128)(2,1)S(1)}, u32[]{:S(2)}, u32[]{:S(2)}) collective-permute-start(bf16[256,3072]{1,0:T(8,128)(2,1)S(1)} %pad_maximum_fusion.refs_12_.refs_4_), channel_id=1, source_target_pairs={{0,2},{1,3},{2,0},{3,1},{4,6},{5,7},{6,4},{7,5},{8,10},{9,11},{10,... | collective-permute-start | bytes 4718600 | tf_op jit(solution)/shard_map/ppermute | solution.py:234
  74.0 41.8 %collective-permute-start.4 = (bf16[256,3072]{1,0:T(8,128)(2,1)S(1)}, bf16[256,3072]{1,0:T(8,128)(2,1)}, u32[]{:S(2)}, u32[]{:S(2)}) collective-permute-start(bf16[256,3072]{1,0:T(8,128)(2,1)S(1)} %pad_maximum_fusion.refs_12_.refs_4_), channel_id=1, source_target_pairs={{0,1},{1,0},{2,3},{3,2},{4,5},{5,4},{6,7},{7,6},{8,9},{9,8},{10,11... | collective-permute-start | bytes 4718600 | tf_op jit(solution)/shard_map/ppermute | solution.py:234
  75.5 10.6 %collective-permute-start.2 = (bf16[128,3072]{1,0:T(8,128)(2,1)}, bf16[128,3072]{1,0:T(8,128)(2,1)}, u32[]{:S(2)}, u32[]{:S(2)}) collective-permute-start(bf16[128,3072]{1,0:T(8,128)(2,1)} %copy-done.45), channel_id=1, source_target_pairs={{8,16},{12,20},{16,24},{20,28},{9,17},{13,21},{17,25},{21,29},{10,... | collective-permute-start | bytes 2359304 | tf_op jit(solution)/shard_map/ppermute | solution.py:234
  77.1 38.7 %collective-permute-start.3 = (bf16[128,3072]{1,0:T(8,128)(2,1)}, bf16[128,3072]{1,0:T(8,128)(2,1)}, u32[]{:S(2)}, u32[]{:S(2)}) collective-permute-start(bf16[128,3072]{1,0:T(8,128)(2,1)} %collective-permute-done.1), channel_id=1, source_target_pairs={{8,0},{12,4},{16,8},{20,12},{9,1},{13,5},{17,9},{21,13},{10,2},{14... | collective-permute-start | bytes 2359304 | tf_op jit(solution)/shard_map/ppermute | solution.py:234
  86.1 29.7 %copy-start.38 = (bf16[512,128]{1,0:T(8,128)(2,1)}, bf16[512,128]{1,0:T(8,128)(2,1)S(1)}, u32[]{:S(2)}) copy-start(bf16[512,128]{1,0:T(8,128)(2,1)S(1)} %get-tuple-element.97) | copy-start | bytes 393220
  115.8 1.1 copy-start.3
  116.9 66.3 %all-to-all-start.2 = ((bf16[8,256,384]{2,1,0:T(8,128)(2,1)}), bf16[8,256,384]{2,1,0:T(8,128)(2,1)}, u32[]{:S(2)}, u32[]{:S(2)}) async-start(bf16[8,256,384]{2,1,0:T(8,128)(2,1)} %copy-done.14), calls=%async_computation.2 | async-start | bytes 3145728 | tf_op jit(solution)/shard_map/all_to_all | solution.py:224
  127.8 37.7 %collective-permute-start.10 = (bf16[256,3072]{1,0:T(8,128)(2,1)S(1)}, bf16[256,3072]{1,0:T(8,128)(2,1)S(1)}, u32[]{:S(2)}, u32[]{:S(2)}) collective-permute-start(bf16[256,3072]{1,0:T(8,128)(2,1)S(1)} %pad_maximum_fusion.refs_12_.refs_4_), channel_id=1, source_target_pairs={{0,3},{1,2},{2,1},{3,0},{4,7},{5,6},{6,5},{7,4},{8,11},{9,10},{10,... | collective-permute-start | bytes 4718600 | tf_op jit(solution)/shard_map/ppermute | solution.py:234
  130.2 3.9 %copy-start.42 = (bf16[512,128]{1,0:T(8,128)(2,1)S(1)}, bf16[512,128]{1,0:T(8,128)(2,1)}, u32[]{:S(2)}) copy-start(bf16[512,128]{1,0:T(8,128)(2,1)} %copy-done.41) | copy-start | bytes 393220
  130.2 7.7 %copy-start.39 = (bf16[512,128]{1,0:T(8,128)(2,1)S(1)}, bf16[512,128]{1,0:T(8,128)(2,1)}, u32[]{:S(2)}) copy-start(bf16[512,128]{1,0:T(8,128)(2,1)} %copy-done.38) | copy-start | bytes 393220
  130.2 9.7 %copy-start.37 = (bf16[512,128]{1,0:T(8,128)(2,1)S(1)}, bf16[512,128]{1,0:T(8,128)(2,1)}, u32[]{:S(2)}) copy-start(bf16[512,128]{1,0:T(8,128)(2,1)} %copy-done.36) | copy-start | bytes 393220
  132.7 50.6 %collective-permute-start.6 = (bf16[128,3072]{1,0:T(8,128)(2,1)S(1)}, bf16[128,3072]{1,0:T(8,128)(2,1)}, u32[]{:S(2)}, u32[]{:S(2)}) collective-permute-start(bf16[128,3072]{1,0:T(8,128)(2,1)S(1)} %get-tuple-element.152), channel_id=1, source_target_pairs={{8,0},{12,4},{16,24},{20,28},{9,1},{13,5},{17,25},{21,29},{10,2},{... | collective-permute-start | bytes 2359304 | tf_op jit(solution)/shard_map/ppermute | solution.py:234
  134.1 47.8 %collective-permute-start.7 = (bf16[512,128]{1,0:T(8,128)(2,1)S(1)}, bf16[512,128]{1,0:T(8,128)(2,1)S(1)}, u32[]{:S(2)}, u32[]{:S(2)}) collective-permute-start(bf16[512,128]{1,0:T(8,128)(2,1)S(1)} %copy-done.42), channel_id=1, source_target_pairs={{0,8},{4,12},{8,0},{12,4},{16,24},{20,28},{24,16},{28,20},{1,9},{5... | collective-permute-start | bytes 393224 | tf_op jit(solution)/shard_map/ppermute | solution.py:234
  137.9 44.1 %collective-permute-start.8 = (bf16[512,128]{1,0:T(8,128)(2,1)S(1)}, bf16[512,128]{1,0:T(8,128)(2,1)S(1)}, u32[]{:S(2)}, u32[]{:S(2)}) collective-permute-start(bf16[512,128]{1,0:T(8,128)(2,1)S(1)} %copy-done.39), channel_id=1, source_target_pairs={{0,16},{4,20},{8,24},{12,28},{16,0},{20,4},{24,8},{28,12},{1,17},{... | collective-permute-start | bytes 393224 | tf_op jit(solution)/shard_map/ppermute | solution.py:234
  139.9 42.7 %collective-permute-start.9 = (bf16[512,128]{1,0:T(8,128)(2,1)S(1)}, bf16[512,128]{1,0:T(8,128)(2,1)S(1)}, u32[]{:S(2)}, u32[]{:S(2)}) collective-permute-start(bf16[512,128]{1,0:T(8,128)(2,1)S(1)} %copy-done.37), channel_id=1, source_target_pairs={{0,24},{4,28},{8,16},{12,20},{16,8},{20,12},{24,0},{28,4},{1,25},{... | collective-permute-start | bytes 393224 | tf_op jit(solution)/shard_map/ppermute | solution.py:234
  165.5 17.8 %copy-start.5 = (bf16[256,3072]{1,0:T(8,128)(2,1)}, bf16[256,3072]{1,0:T(8,128)(2,1)S(1)}, u32[]{:S(2)}) copy-start(bf16[256,3072]{1,0:T(8,128)(2,1)S(1)} %collective-permute-done.10.refs_15_.refs_7_) | copy-start | bytes 4718596
  183.3 53.5 %all-to-all-start.3 = ((bf16[8,256,384]{2,1,0:T(8,128)(2,1)}), bf16[8,256,384]{2,1,0:T(8,128)(2,1)}, u32[]{:S(2)}, u32[]{:S(2)}) async-start(bf16[8,256,384]{2,1,0:T(8,128)(2,1)} %copy-done.13), calls=%async_computation.3 | async-start | bytes 3145728 | tf_op jit(solution)/shard_map/all_to_all | solution.py:224
  187.6 1.6 copy-start.46
  189.2 3.2 %copy-start.35 = (bf16[512,128]{1,0:T(8,128)(2,1)S(1)}, bf16[512,128]{1,0:T(8,128)(2,1)}, u32[]{:S(2)}) copy-start(bf16[512,128]{1,0:T(8,128)(2,1)} %copy-done.34) | copy-start | bytes 393220
  189.2 4.8 %copy-start.33 = (bf16[512,128]{1,0:T(8,128)(2,1)S(1)}, bf16[512,128]{1,0:T(8,128)(2,1)}, u32[]{:S(2)}) copy-start(bf16[512,128]{1,0:T(8,128)(2,1)} %copy-done.32) | copy-start | bytes 393220
  189.2 7.5 %copy-start.31 = (bf16[512,128]{1,0:T(8,128)(2,1)S(1)}, bf16[512,128]{1,0:T(8,128)(2,1)}, u32[]{:S(2)}) copy-start(bf16[512,128]{1,0:T(8,128)(2,1)} %copy-done.30) | copy-start | bytes 393220
  189.3 46.2 %collective-permute-start.12 = (bf16[256,3072]{1,0:T(8,128)(2,1)S(1)}, bf16[256,3072]{1,0:T(8,128)(2,1)S(1)}, u32[]{:S(2)}, u32[]{:S(2)}) collective-permute-start(bf16[256,3072]{1,0:T(8,128)(2,1)S(1)} %pad_maximum_fusion.1.refs_16_.refs_8_), channel_id=1, source_target_pairs={{0,2},{1,3},{2,0},{3,1},{4,6},{5,7},{6,4},{7,5},{8,10},{9,11},{10,... | collective-permute-start | bytes 4718600 | tf_op jit(solution)/shard_map/ppermute | solution.py:234
  190.9 45.8 %collective-permute-start.11 = (bf16[256,3072]{1,0:T(8,128)(2,1)S(1)}, bf16[256,3072]{1,0:T(8,128)(2,1)}, u32[]{:S(2)}, u32[]{:S(2)}) collective-permute-start(bf16[256,3072]{1,0:T(8,128)(2,1)S(1)} %pad_maximum_fusion.1.refs_16_.refs_8_), channel_id=1, source_target_pairs={{0,1},{1,0},{2,3},{3,2},{4,5},{5,4},{6,7},{7,6},{8,9},{9,8},{10,11... | collective-permute-start | bytes 4718600 | tf_op jit(solution)/shard_map/ppermute | solution.py:234
  192.4 24.6 %collective-permute-start.13 = (bf16[512,128]{1,0:T(8,128)(2,1)S(1)}, bf16[512,128]{1,0:T(8,128)(2,1)S(1)}, u32[]{:S(2)}, u32[]{:S(2)}) collective-permute-start(bf16[512,128]{1,0:T(8,128)(2,1)S(1)} %copy-done.35), channel_id=1, source_target_pairs={{0,8},{4,12},{8,0},{12,4},{16,24},{20,28},{24,16},{28,20},{1,9},{5... | collective-permute-start | bytes 393224 | tf_op jit(solution)/shard_map/ppermute | solution.py:234
  194.1 40.2 %collective-permute-start.14 = (bf16[512,128]{1,0:T(8,128)(2,1)S(1)}, bf16[512,128]{1,0:T(8,128)(2,1)S(1)}, u32[]{:S(2)}, u32[]{:S(2)}) collective-permute-start(bf16[512,128]{1,0:T(8,128)(2,1)S(1)} %copy-done.33), channel_id=1, source_target_pairs={{0,16},{4,20},{8,24},{12,28},{16,0},{20,4},{24,8},{28,12},{1,17},{... | collective-permute-start | bytes 393224 | tf_op jit(solution)/shard_map/ppermute | solution.py:234
  196.7 38.2 %collective-permute-start.15 = (bf16[512,128]{1,0:T(8,128)(2,1)S(1)}, bf16[512,128]{1,0:T(8,128)(2,1)S(1)}, u32[]{:S(2)}, u32[]{:S(2)}) collective-permute-start(bf16[512,128]{1,0:T(8,128)(2,1)S(1)} %copy-done.31), channel_id=1, source_target_pairs={{0,24},{4,28},{8,16},{12,20},{16,8},{20,12},{24,0},{28,4},{1,25},{... | collective-permute-start | bytes 393224 | tf_op jit(solution)/shard_map/ppermute | solution.py:234
  204.0 0.7 copy-start.28
  217.0 0.7 copy-start.22
  235.5 1.2 copy-start.1
  236.8 1.6 copy-start.2
  238.4 22.1 %copy-start.4 = (bf16[256,3072]{1,0:T(8,128)(2,1)S(1)}, bf16[256,3072]{1,0:T(8,128)(2,1)}, u32[]{:S(2)}) copy-start(bf16[256,3072]{1,0:T(8,128)(2,1)} %copy-done.3) | copy-start | bytes 4718596
  238.4 22.1 %copy-start.6 = (bf16[256,3072]{1,0:T(8,128)(2,1)S(1)}, bf16[256,3072]{1,0:T(8,128)(2,1)}, u32[]{:S(2)}) copy-start(bf16[256,3072]{1,0:T(8,128)(2,1)} %copy-done.5) | copy-start | bytes 4718596
  238.5 22.0 %collective-permute-start.23 = (bf16[128,3072]{1,0:T(8,128)(2,1)S(1)}, bf16[128,3072]{1,0:T(8,128)(2,1)S(1)}, u32[]{:S(2)}, u32[]{:S(2)}) collective-permute-start(bf16[128,3072]{1,0:T(8,128)(2,1)S(1)} %slice.7), channel_id=1, source_target_pairs={{0,1},{1,0},{2,3},{3,2},{4,5},{5,4},{6,7},{7,6},{8,9},{9,8},{10,11... | collective-permute-start | bytes 2359304 | tf_op jit(solution)/shard_map/ppermute | solution.py:234
  240.0 20.4 %collective-permute-start.22 = (bf16[128,3072]{1,0:T(8,128)(2,1)S(1)}, bf16[128,3072]{1,0:T(8,128)(2,1)S(1)}, u32[]{:S(2)}, u32[]{:S(2)}) collective-permute-start(bf16[128,3072]{1,0:T(8,128)(2,1)S(1)} %slice.6), channel_id=1, source_target_pairs={{0,2},{1,3},{2,0},{3,1},{4,6},{5,7},{6,4},{7,5},{8,10},{9,11},{10,... | collective-permute-start | bytes 2359304 | tf_op jit(solution)/shard_map/ppermute | solution.py:234
  241.5 10.9 %collective-permute-start.16 = (bf16[512,128]{1,0:T(8,128)(2,1)}, bf16[512,128]{1,0:T(8,128)(2,1)S(1)}, u32[]{:S(2)}, u32[]{:S(2)}) collective-permute-start(bf16[512,128]{1,0:T(8,128)(2,1)} %copy-done.44), channel_id=1, source_target_pairs={{0,8},{4,12},{8,0},{12,4},{16,24},{20,28},{24,16},{28,20},{1,9},{5... | collective-permute-start | bytes 393224 | tf_op jit(solution)/shard_map/ppermute | solution.py:234
  243.8 12.2 %collective-permute-start.17 = (bf16[512,128]{1,0:T(8,128)(2,1)}, bf16[512,128]{1,0:T(8,128)(2,1)S(1)}, u32[]{:S(2)}, u32[]{:S(2)}) collective-permute-start(bf16[512,128]{1,0:T(8,128)(2,1)} %copy-done.43), channel_id=1, source_target_pairs={{0,16},{4,20},{8,24},{12,28},{16,0},{20,4},{24,8},{28,12},{1,17},{... | collective-permute-start | bytes 393224 | tf_op jit(solution)/shard_map/ppermute | solution.py:234
  243.8 12.2 %collective-permute-start.18 = (bf16[512,128]{1,0:T(8,128)(2,1)}, bf16[512,128]{1,0:T(8,128)(2,1)S(1)}, u32[]{:S(2)}, u32[]{:S(2)}) collective-permute-start(bf16[512,128]{1,0:T(8,128)(2,1)} %copy-done.40), channel_id=1, source_target_pairs={{0,24},{4,28},{8,16},{12,20},{16,8},{20,12},{24,0},{28,4},{1,25},{... | collective-permute-start | bytes 393224 | tf_op jit(solution)/shard_map/ppermute | solution.py:234
  256.0 17.7 %collective-permute-start.19 = (bf16[512,128]{1,0:T(8,128)(2,1)S(1)}, bf16[512,128]{1,0:T(8,128)(2,1)S(1)}, u32[]{:S(2)}, u32[]{:S(2)}) collective-permute-start(bf16[512,128]{1,0:T(8,128)(2,1)S(1)} %get-tuple-element.129), channel_id=1, source_target_pairs={{0,8},{4,12},{8,0},{12,4},{16,24},{20,28},{24,16},{28,20},{1,9},{5... | collective-permute-start | bytes 393224 | tf_op jit(solution)/shard_map/ppermute | solution.py:234
  258.1 15.7 %collective-permute-start.20 = (bf16[512,128]{1,0:T(8,128)(2,1)S(1)}, bf16[512,128]{1,0:T(8,128)(2,1)S(1)}, u32[]{:S(2)}, u32[]{:S(2)}) collective-permute-start(bf16[512,128]{1,0:T(8,128)(2,1)S(1)} %get-tuple-element.130), channel_id=1, source_target_pairs={{0,16},{4,20},{8,24},{12,28},{16,0},{20,4},{24,8},{28,12},{1,17},{... | collective-permute-start | bytes 393224 | tf_op jit(solution)/shard_map/ppermute | solution.py:234
  258.3 15.5 %collective-permute-start.21 = (bf16[512,128]{1,0:T(8,128)(2,1)S(1)}, bf16[512,128]{1,0:T(8,128)(2,1)S(1)}, u32[]{:S(2)}, u32[]{:S(2)}) collective-permute-start(bf16[512,128]{1,0:T(8,128)(2,1)S(1)} %get-tuple-element.131), channel_id=1, source_target_pairs={{0,24},{4,28},{8,16},{12,20},{16,8},{20,12},{24,0},{28,4},{1,25},{... | collective-permute-start | bytes 393224 | tf_op jit(solution)/shard_map/ppermute | solution.py:234
  260.5 0.9 copy-start.17
  261.4 0.9 copy-start.19
  262.3 0.9 copy-start.21
  263.2 0.9 copy-start.23
  264.1 0.9 copy-start.25
  265.0 0.9 copy-start.27
  265.9 0.9 copy-start.29
  275.5 3.5 %collective-permute-start.24 = (bf16[256,3072]{1,0:T(8,128)(2,1)S(1)}, bf16[256,3072]{1,0:T(8,128)(2,1)S(1)}, u32[]{:S(2)}, u32[]{:S(2)}) collective-permute-start(bf16[256,3072]{1,0:T(8,128)(2,1)S(1)} %convert_element_type.9), channel_id=1, source_target_pairs={{0,4},{4,0},{8,12},{12,8},{16,20},{20,16},{24,28},{28,24},{1,5},{5... | collective-permute-start | bytes 4718600 | tf_op jit(solution)/shard_map/ppermute | solution.py:234
  (13 other events, 8.4 us)

commit v4 on v3

--- a/solution.py
+++ b/solution.py
@@ -49,9 +49,9 @@
         functools.partial(layout_kernel, steps, here, width),
         out_shape=[jax.ShapeDtypeStruct((groups, tokens, 3 * width * len(joined)), jnp.bfloat16) for joined in steps],
         in_specs=[SMEM] + [ANY] * (3 + len(extra)),
-        out_specs=[ANY] * count,
+        out_specs=[VMEM] * count,
         scratch_shapes=[pltpu.SemaphoreType.DMA((count, most, groups, 3))],
-        compiler_params=limit(16),
+        compiler_params=limit(56),
         cost_estimate=FREE,
     )(place, *fields, *extra)
 
@@ -131,7 +131,7 @@
         in_specs=[SMEM, SMEM, SMEM, VMEM],
         out_specs=[VMEM] * (sources // each),
         scratch_shapes=[pltpu.VMEM((sources, tokens, width), jnp.bfloat16)],
-        compiler_params=limit(24),
+        compiler_params=limit(12),
         cost_estimate=FREE,
     )(place, lists, counts, qkv)
 
@@ -144,10 +144,11 @@
     slots = held.shape[0]
     row_copies = []
     for n, (_, picked, cut) in enumerate(terms):
-        for k, r in enumerate(picked):
-            wide = rows[r].shape[1]
+        for k, (r, lane) in enumerate(picked):
+            wide = lefts.shape[2] // len(picked)
+            source = rows[r].at[pl.ds(cut.start, cut.stop - cut.start), pl.ds(lane, wide)]
             target = lefts.at[n, :, pl.ds(k * wide, wide)]
-            row_copies.append(pltpu.make_async_copy(rows[r].at[pl.ds(cut.start, cut.stop - cut.start), :], target, row_sem.at[n, k]))
+            row_copies.append(pltpu.make_async_copy(source, target, row_sem.at[n, k]))
     copies = []
     for n, (pieces, _, _) in enumerate(terms):
         at = 0
@@ -199,7 +200,7 @@
             pltpu.SemaphoreType.DMA((slots, 2)),
             pltpu.SemaphoreType.DMA((len(terms), 2)),
         ],
-        compiler_params=limit(28),
+        compiler_params=limit(36),
         cost_estimate=FREE,
     )(*rows, *blocks, *before)
 
@@ -230,6 +231,8 @@
     place = jnp.stack([lax.axis_index("fsdp"), rank]).astype(jnp.int32)
     n, tokens = weight.shape[0], fields[0].shape[0]
 
+    both = slice(0, 2 * tokens)
+
     def along(value, axis, pairs):
         return lax.ppermute(value, axis, pairs)
 
@@ -250,7 +253,6 @@
 
     (x0,) = lay_out(fields, place, ((0,),), groups, here, width, [])
     qkv0 = exchange(x0)
-    weight = after(weight, x0)
     up, down = along(weight, "seq", along_z(UP)), along(weight, "seq", along_z(DOWN))
     x1, x2, x3 = lay_out(fields, place, ((1,), (2,), (3,)), groups, here, width, [x0])
     up, down, qkv0, x1, x2, x3 = fence(up, down, qkv0, x1, x2, x3)
@@ -274,25 +276,33 @@
     far_sides = sides(far)
     back1 = send_back(out1)
     out2 = attend_step(qkv2, 2)
-    qkv3, far_sides, back1, out2 = fence(qkv3, far_sides, back1, out2)
+    joined = jnp.concatenate(back0, axis=1)
+    qkv3, far_sides, back1, out2, joined = fence(qkv3, far_sides, back1, out2, joined)
     back2 = send_back(out2)
+    out3 = attend_step(qkv3, 3)
     far_corner = corner(*far_sides)
-    out3 = attend_step(qkv3, 3)
-    back0, back1, back2, out3 = fence(back0, back1, back2, out3)
-    back3 = send_back(out3)
-
-    blocks = [near] + near_sides + near_corner + [far] + far_sides + far_corner
-    both, own, other = slice(0, 2 * tokens), slice(0, tokens), slice(tokens, 2 * tokens)
-
-    def terms(step, at, cut):
-        last = (7, 8) if step == 3 else (4 + step,)
-        return [((step,), (4 * at, 4 * at + 1), cut), (last, (4 * at + 2, 4 * at + 3), cut)]
-
-    early = terms(0, 0, both) + terms(1, 1, both) + terms(2, 2, both)
-    mine, theirs = project(back0 + back1 + back2, blocks, early, [], 2)
-    (theirs,) = project(back3, blocks, terms(3, 0, other), [theirs], 1)
+    back3 = [out3[0], None] + [along(out3[p], "seq", xor(2 * p, groups)) for p in (2, 3)]
+    back2, side = fence(back2, out3[1])
+    back3[1] = along(side, "seq", xor(2, groups))
+
+    sides_all = [near] + near_sides + [far] + far_sides
+    rows = [joined] + back1 + back2
+    early = [((0,), ((0, 0),), both), ((3,), ((0, 2 * width),), both)]
+    for m in (1, 2):
+        for h in (0, 1):
+            at = 4 * m - 3 + 2 * h
+            early.append(((m + 3 * h,), ((at, 0), (at + 1, 0)), both))
+    mine, theirs = project(rows, sides_all, early, [], 2)
+
+    def finish(cut, before):
+        near_pieces = tuple(range(len(near_corner)))
+        far_pieces = tuple(range(len(near_corner), len(near_corner + far_corner)))
+        terms = [(near_pieces, ((0, 0), (1, 0)), cut), (far_pieces, ((2, 0), (3, 0)), cut)]
+        return project(back3, near_corner + far_corner, terms, [before], 1)[0]
+
+    theirs = finish(slice(tokens, 2 * tokens), theirs)
     given = along(theirs.astype(jnp.bfloat16), "seq", xor(1, groups))
-    (mine,) = project(back3, blocks, terms(3, 0, own), [mine], 1)
+    mine = finish(slice(0, tokens), mine)
     return (mine + given.astype(jnp.float32)).astype(jnp.bfloat16)
 
 

time: 282 us -> 274 us (0.972)
  local copies, waits for them, and re-layouts: 29.5 us -> 7.55 us
  waiting for transfers between devices: 126 us -> 135 us
  Pallas kernels: 41.1 us -> 44.1 us
    unnamed x96 -> x62, local copies, waits for them, and re-layouts: 27.9 us -> 4.63 us
    ppermute x25, waiting for transfers between devices: 126 us -> 135 us  [along(): return lax.ppermute(value, axis, pairs)]
    pallas_call x2, Pallas kernels: 4.5 us -> 9.49 us  [lay_out(): pl.pallas_call(functools.partial(layout_kernel, steps, here, width), out_...]
    pallas_call x4, Pallas kernels: 26.6 us -> 23.8 us  [attend(): pl.pallas_call(functools.partial(attend_kernel, step, at_lane, width, slo...]
  transfers between devices with their start and end apart: 29 -> 29, of which waited for: 8 -> 9; matrix products, arithmetic and copies ran while one was open for 2% -> 3% of each run, Pallas kernels for 13% -> 14%
where the time goes in v4:
time: 274 us; the launch traced here: 273 us
  waiting for transfers between devices  135 us (49%)
  starting transfers between devices  75.5 us (28%)
  Pallas kernels  44.1 us (16%)
  other arithmetic  11.1 us (4%)
  local copies, waits for them, and re-layouts  7.55 us (3%)
    ppermute x25, waiting for transfers between devices, along(): return lax.ppermute(value, axis, pairs)  135 us
    ppermute x25, starting transfers between devices, along(): return lax.ppermute(value, axis, pairs)  42.9 us
    all_to_all x4, starting transfers between devices, exchange(): return lax.all_to_all(x, 'seq', split_axis=0, concat_axis=0, tiled=True)  32.7 us
    pallas_call x4, Pallas kernels, attend(): pl.pallas_call(functools.partial(attend_kernel, step, at_lane, width, slo...  23.8 us
    pallas_call x3, Pallas kernels, project(): pl.pallas_call(functools.partial(project_kernel, terms, len(rows), len(bl...  10.8 us
    pallas_call x2, Pallas kernels, lay_out(): pl.pallas_call(functools.partial(layout_kernel, steps, here, width), out_...  9.49 us
  transfers between devices with their start and end apart: 29, of which 9 were waited for; matrix products, arithmetic and copies ran while one was open for 3% of the time, Pallas kernels for 14%

profile of v4, /device:TPU:0, one launch (start us, length us, event | category | flops | bytes accessed | tf_op | source)
XLA Modules:
  0.0 273.5 jit_solution(14161815768567468505)
XLA Ops:
  0.0 0.7 pad_add_fusion.place_ref
  0.7 3.5 %shard_map.64.refs_3_ = bf16[8,256,384]{2,1,0:T(8,128)(2,1)} custom-call(s32[2]{0:T(128)} %pad_add_fusion.place_ref, bf16[256,4096]{1,0:T(8,128)(2,1)} %bitcast.14, bf16[256,4096]{1,0:T(8,128)(2,1)} %bitcast.16, bf16[256,4096]{1,0:T(8,128)(2,1)} %bitcast.18), custom_call_target="tpu_custom_call" | custom-call | flops 1 | bytes 1 | tf_op jit(solution)/shard_map/pallas_call | solution.py:48
  4.1 6.5 %all-to-all-start = ((bf16[8,256,384]{2,1,0:T(8,128)(2,1)}), bf16[8,256,384]{2,1,0:T(8,128)(2,1)S(1)}, u32[]{:S(2)}, u32[]{:S(2)}) async-start(bf16[8,256,384]{2,1,0:T(8,128)(2,1)} %shard_map.64.refs_3_), calls=%async_computation | async-start | bytes 3145728 | tf_op jit(solution)/shard_map/all_to_all | solution.py:225
  10.6 4.8 %collective-permute-start = (bf16[128,3072]{1,0:T(8,128)(2,1)S(1)}, bf16[128,3072]{1,0:T(8,128)(2,1)}, u32[]{:S(2)}, u32[]{:S(2)}) collective-permute-start(bf16[128,3072]{1,0:T(8,128)(2,1)S(1)} %copy-done.28), channel_id=1, source_target_pairs={{0,8},{4,12},{8,16},{12,20},{16,24},{20,28},{1,9},{5,13},{9,17},{1... | collective-permute-start | bytes 2359304 | tf_op jit(solution)/shard_map/ppermute | solution.py:237
  15.4 1.3 collective-permute-start.1
  16.7 6.0 %shard_map.65 = (bf16[8,256,384]{2,1,0:T(8,128)(2,1)}, bf16[8,256,384]{2,1,0:T(8,128)(2,1)}, bf16[8,256,384]{2,1,0:T(8,128)(2,1)}) custom-call(s32[2]{0:T(128)} %pad_add_fusion.place_ref, bf16[256,4096]{1,0:T(8,128)(2,1)} %bitcast.15, bf16[256,4096]{1,0:T(8,128)(2,1)} %bitcast.17, bf16[256,4096]{1,0:T(8,128)(2,1)} %bitcast.19, ...), custom_call_target="tpu_custom_call" | custom-call | flops 1 | bytes 1 | tf_op jit(solution)/shard_map/pallas_call | solution.py:48
  22.8 31.1 %collective-permute-done = bf16[128,3072]{1,0:T(8,128)(2,1)} collective-permute-done((bf16[128,3072]{1,0:T(8,128)(2,1)S(1)}, bf16[128,3072]{1,0:T(8,128)(2,1)}, u32[]{:S(2)}, u32[]{:S(2)}) %collective-permute-start) | collective-permute-done | bytes 786464 | tf_op jit(solution)/shard_map/ppermute | solution.py:237
  53.9 2.2 collective-permute-done.1
  56.1 11.2 %all-to-all-start.1 = ((bf16[8,256,384]{2,1,0:T(8,128)(2,1)}), bf16[8,256,384]{2,1,0:T(8,128)(2,1)S(1)}, u32[]{:S(2)}, u32[]{:S(2)}) async-start(bf16[8,256,384]{2,1,0:T(8,128)(2,1)} %get-tuple-element.73), calls=%async_computation.1 | async-start | bytes 3145728 | tf_op jit(solution)/shard_map/all_to_all | solution.py:225
  67.3 1.3 broadcast_select_fusion.1
  68.7 1.2 pad_maximum_fusion.refs_9_
  69.9 1.5 collective-permute-start.5
  71.4 1.5 collective-permute-start.4
  72.9 1.6 collective-permute-start.2
  74.5 1.3 collective-permute-start.3
  75.9 0.1 copy.10
  76.0 0.1 dynamic-slice_bitcast_fusion
  76.1 6.7 %shard_map.66 = (bf16[512,128]{1,0:T(8,128)(2,1)S(1)}, bf16[512,128]{1,0:T(8,128)(2,1)}, bf16[512,128]{1,0:T(8,128)(2,1)}, bf16[512,128]{1,0:T(8,128)(2,1)}) custom-call(s32[2]{0:T(128)S(1)} %copy-done.14, s32[4,128]{1,0:T(4,128)S(1)} %copy.11.lists_ref, s32[4,16]{1,0:T(4,128)S(1)} %bitcast.10, bf16[8,256,384]{2,1,0:T(8,128)(2,1)S(1)} %all-to-all-done.refs_0_), custom_call_target="tpu_custom_call" | custom-call | flops 1 | bytes 1 | tf_op jit(solution)/shard_map/pallas_call | solution.py:128
  82.9 0.7 copy-done.12
  83.5 29.2 %collective-permute-done.3 = bf16[128,3072]{1,0:T(8,128)(2,1)} collective-permute-done((bf16[128,3072]{1,0:T(8,128)(2,1)}, bf16[128,3072]{1,0:T(8,128)(2,1)}, u32[]{:S(2)}, u32[]{:S(2)}) %collective-permute-start.3) | collective-permute-done | bytes 786464 | tf_op jit(solution)/shard_map/ppermute | solution.py:237
  112.8 11.2 %all-to-all-start.2 = ((bf16[8,256,384]{2,1,0:T(8,128)(2,1)}), bf16[8,256,384]{2,1,0:T(8,128)(2,1)}, u32[]{:S(2)}, u32[]{:S(2)}) async-start(bf16[8,256,384]{2,1,0:T(8,128)(2,1)} %get-tuple-element.83), calls=%async_computation.2 | async-start | bytes 3145728 | tf_op jit(solution)/shard_map/all_to_all | solution.py:225
  124.0 2.4 collective-permute-start.10
  126.4 2.4 broadcast_select_fusion
  128.8 1.3 collective-permute-start.6
  130.1 4.0 %collective-permute-start.7 = (bf16[512,128]{1,0:T(8,128)(2,1)}, bf16[512,128]{1,0:T(8,128)(2,1)}, u32[]{:S(2)}, u32[]{:S(2)}) collective-permute-start(bf16[512,128]{1,0:T(8,128)(2,1)} %get-tuple-element.85), channel_id=1, source_target_pairs={{0,8},{4,12},{8,0},{12,4},{16,24},{20,28},{24,16},{28,20},{1,9},{5... | collective-permute-start | bytes 393224 | tf_op jit(solution)/shard_map/ppermute | solution.py:237
  134.1 2.0 collective-permute-start.8
  136.0 1.5 collective-permute-start.9
  137.5 5.4 %shard_map.67 = (bf16[512,128]{1,0:T(8,128)(2,1)S(1)}, bf16[512,128]{1,0:T(8,128)(2,1)S(1)}, bf16[512,128]{1,0:T(8,128)(2,1)S(1)}, bf16[512,128]{1,0:T(8,128)(2,1)S(1)}) custom-call(s32[2]{0:T(128)S(1)} %copy-done.14, s32[4,128]{1,0:T(4,128)S(1)} %copy.11.lists_ref, s32[4,16]{1,0:T(4,128)S(1)} %bitcast.11, bf16[8,256,384]{2,1,0:T(8,128)(2,1)S(1)} %all-to-all-done.1.refs_0_), custom_call_target="tpu_custom_call" | custom-call | flops 1 | bytes 1 | tf_op jit(solution)/shard_map/pallas_call | solution.py:128
  142.9 0.6 copy-done.15
  143.5 0.7 copy-done.19
  144.2 17.7 %collective-permute-done.10.refs_4_ = bf16[256,3072]{1,0:T(8,128)(2,1)S(1)} collective-permute-done((bf16[256,3072]{1,0:T(8,128)(2,1)}, bf16[256,3072]{1,0:T(8,128)(2,1)S(1)}, u32[]{:S(2)}, u32[]{:S(2)}) %collective-permute-start.10) | collective-permute-done | bytes 1572896 | tf_op jit(solution)/shard_map/ppermute | solution.py:237
  161.9 16.4 %collective-permute-done.7 = bf16[512,128]{1,0:T(8,128)(2,1)} collective-permute-done((bf16[512,128]{1,0:T(8,128)(2,1)}, bf16[512,128]{1,0:T(8,128)(2,1)}, u32[]{:S(2)}, u32[]{:S(2)}) %collective-permute-start.7) | collective-permute-done | bytes 131104 | tf_op jit(solution)/shard_map/ppermute | solution.py:237
  178.3 3.8 %all-to-all-start.3 = ((bf16[8,256,384]{2,1,0:T(8,128)(2,1)}), bf16[8,256,384]{2,1,0:T(8,128)(2,1)S(1)}, u32[]{:S(2)}, u32[]{:S(2)}) async-start(bf16[8,256,384]{2,1,0:T(8,128)(2,1)} %get-tuple-element.93), calls=%async_computation.3 | async-start | bytes 3145728 | tf_op jit(solution)/shard_map/all_to_all | solution.py:225
  182.1 1.6 select_select_fusion
  183.7 0.1 pad_maximum_fusion.1.refs_12_
  183.8 1.6 collective-permute-start.12
  185.4 1.5 collective-permute-start.11
  186.9 1.6 collective-permute-start.13
  188.6 2.6 collective-permute-start.14
  191.2 0.1 collective-permute-start.15
  191.3 6.0 %shard_map.68 = (bf16[512,128]{1,0:T(8,128)(2,1)S(1)}, bf16[512,128]{1,0:T(8,128)(2,1)S(1)}, bf16[512,128]{1,0:T(8,128)(2,1)S(1)}, bf16[512,128]{1,0:T(8,128)(2,1)S(1)}) custom-call(s32[2]{0:T(128)S(1)} %copy-done.14, s32[4,128]{1,0:T(4,128)S(1)} %copy.11.lists_ref, s32[4,16]{1,0:T(4,128)S(1)} %bitcast.12, bf16[8,256,384]{2,1,0:T(8,128)(2,1)} %all-to-all-done.2.refs_0_), custom_call_target="tpu_custom_call" | custom-call | flops 1 | bytes 1 | tf_op jit(solution)/shard_map/pallas_call | solution.py:128
  197.4 2.1 pad_maximum_fusion.2.refs_0_
  199.4 12.1 %collective-permute-done.13.refs_2_ = bf16[512,128]{1,0:T(8,128)(2,1)S(1)} collective-permute-done((bf16[512,128]{1,0:T(8,128)(2,1)S(1)}, bf16[512,128]{1,0:T(8,128)(2,1)S(1)}, u32[]{:S(2)}, u32[]{:S(2)}) %collective-permute-start.13) | collective-permute-done | bytes 131104 | tf_op jit(solution)/shard_map/ppermute | solution.py:237
  211.5 17.2 %collective-permute-done.14.refs_3_ = bf16[512,128]{1,0:T(8,128)(2,1)S(1)} collective-permute-done((bf16[512,128]{1,0:T(8,128)(2,1)S(1)}, bf16[512,128]{1,0:T(8,128)(2,1)S(1)}, u32[]{:S(2)}, u32[]{:S(2)}) %collective-permute-start.14) | collective-permute-done | bytes 131104 | tf_op jit(solution)/shard_map/ppermute | solution.py:237
  228.7 0.7 copy-done.6
  229.4 0.7 copy-done.8
  230.1 1.1 copy-done.3
  231.3 1.3 slice.7
  232.6 1.3 slice.6
  234.0 1.6 collective-permute-start.22
  235.5 1.5 collective-permute-start.23
  237.0 2.2 collective-permute-start.16
  239.3 2.4 collective-permute-start.18
  241.7 5.7 %shard_map.69 = (bf16[512,128]{1,0:T(8,128)(2,1)S(1)}, bf16[512,128]{1,0:T(8,128)(2,1)S(1)}, bf16[512,128]{1,0:T(8,128)(2,1)S(1)}, bf16[512,128]{1,0:T(8,128)(2,1)S(1)}) custom-call(s32[2]{0:T(128)S(1)} %copy-done.14, s32[4,128]{1,0:T(4,128)S(1)} %copy.11.lists_ref, s32[4,16]{1,0:T(4,128)S(1)} %bitcast.13, bf16[8,256,384]{2,1,0:T(8,128)(2,1)S(1)} %all-to-all-done.3.refs_0_), custom_call_target="tpu_custom_call" | custom-call | flops 1 | bytes 1 | tf_op jit(solution)/shard_map/pallas_call | solution.py:128
  247.4 1.1 collective-permute-start.20
  248.5 7.0 %collective-permute-done.17.refs_7_ = bf16[512,128]{1,0:T(8,128)(2,1)S(1)} collective-permute-done((bf16[512,128]{1,0:T(8,128)(2,1)S(1)}, bf16[512,128]{1,0:T(8,128)(2,1)S(1)}, u32[]{:S(2)}, u32[]{:S(2)}) %collective-permute-start.17) | collective-permute-done | bytes 131104 | tf_op jit(solution)/shard_map/ppermute | solution.py:237
  255.5 1.5 collective-permute-start.21
  257.0 1.9 collective-permute-start.19
  258.9 7.7 %shard_map.70 = (f32[256,3072]{1,0:T(8,128)S(1)}, f32[256,3072]{1,0:T(8,128)S(1)}) custom-call(bf16[512,512]{1,0:T(8,128)(2,1)S(1)} %copy-done.5, bf16[512,128]{1,0:T(8,128)(2,1)S(1)} %get-tuple-element.117.refs_1_, bf16[512,128]{1,0:T(8,128)(2,1)S(1)} %collective-permute-done.13.refs_2_, bf16[512,128]{1,0:T(8,128)(2,1)S(1)} %copy-done.7, ...), custom_call_target="tpu_custom_call" | custom-call | flops 1 | bytes 1 | tf_op jit(solution)/shard_map/pallas_call | solution.py:192
  266.7 1.5 shard_map.72
  268.2 0.2 convert_element_type.9
  268.5 1.5 shard_map.71
  270.1 1.9 collective-permute-done.24
  271.9 1.6 fusion
  (80 shorter events, 0.5 us)
Async XLA Ops:
  0.0 76.0 %copy-start = (s32[1,32,16,8]{1,3,2,0:T(8,128)S(1)}, s32[1,32,16,8]{1,3,2,0:T(8,128)}, u32[]{:S(2)}) copy-start(s32[1,32,16,8]{1,3,2,0:T(8,128)} %param.10) | copy-start | bytes 49156
  4.1 6.5 %copy-start.28 = (bf16[128,3072]{1,0:T(8,128)(2,1)S(1)}, bf16[128,3072]{1,0:T(8,128)(2,1)}, u32[]{:S(2)}) copy-start(bf16[128,3072]{1,0:T(8,128)(2,1)} %param.9) | copy-start | bytes 2359300
  4.1 51.9 %all-to-all-start = ((bf16[8,256,384]{2,1,0:T(8,128)(2,1)}), bf16[8,256,384]{2,1,0:T(8,128)(2,1)S(1)}, u32[]{:S(2)}, u32[]{:S(2)}) async-start(bf16[8,256,384]{2,1,0:T(8,128)(2,1)} %shard_map.64.refs_3_), calls=%async_computation | async-start | bytes 3145728 | tf_op jit(solution)/shard_map/all_to_all | solution.py:225
  10.6 43.3 %collective-permute-start = (bf16[128,3072]{1,0:T(8,128)(2,1)S(1)}, bf16[128,3072]{1,0:T(8,128)(2,1)}, u32[]{:S(2)}, u32[]{:S(2)}) collective-permute-start(bf16[128,3072]{1,0:T(8,128)(2,1)S(1)} %copy-done.28), channel_id=1, source_target_pairs={{0,8},{4,12},{8,16},{12,20},{16,24},{20,28},{1,9},{5,13},{9,17},{1... | collective-permute-start | bytes 2359304 | tf_op jit(solution)/shard_map/ppermute | solution.py:237
  15.4 40.6 %collective-permute-start.1 = (bf16[128,3072]{1,0:T(8,128)(2,1)S(1)}, bf16[128,3072]{1,0:T(8,128)(2,1)}, u32[]{:S(2)}, u32[]{:S(2)}) collective-permute-start(bf16[128,3072]{1,0:T(8,128)(2,1)S(1)} %copy-done.28), channel_id=1, source_target_pairs={{8,0},{12,4},{16,8},{20,12},{24,16},{28,20},{9,1},{13,5},{17,9},{2... | collective-permute-start | bytes 2359304 | tf_op jit(solution)/shard_map/ppermute | solution.py:237
  56.1 56.7 %all-to-all-start.1 = ((bf16[8,256,384]{2,1,0:T(8,128)(2,1)}), bf16[8,256,384]{2,1,0:T(8,128)(2,1)S(1)}, u32[]{:S(2)}, u32[]{:S(2)}) async-start(bf16[8,256,384]{2,1,0:T(8,128)(2,1)} %get-tuple-element.73), calls=%async_computation.1 | async-start | bytes 3145728 | tf_op jit(solution)/shard_map/all_to_all | solution.py:225
  67.3 1.4 copy-start.29
  68.7 7.2 %copy-start.30 = (s32[1,32,16]{1,2,0:T(8,128)S(1)}, s32[1,32,16]{1,2,0:T(8,128)}, u32[]{:S(2)}) copy-start(s32[1,32,16]{1,2,0:T(8,128)} %param.11) | copy-start | bytes 6148
  68.7 7.5 %copy-start.14 = (s32[2]{0:T(128)S(1)}, s32[2]{0:T(128)}, u32[]{:S(2)}) copy-start(s32[2]{0:T(128)} %pad_add_fusion.place_ref) | copy-start | bytes 28
  69.9 42.8 %collective-permute-start.5 = (bf16[256,3072]{1,0:T(8,128)(2,1)}, bf16[256,3072]{1,0:T(8,128)(2,1)}, u32[]{:S(2)}, u32[]{:S(2)}) collective-permute-start(bf16[256,3072]{1,0:T(8,128)(2,1)} %pad_maximum_fusion.refs_9_), channel_id=1, source_target_pairs={{0,2},{1,3},{2,0},{3,1},{4,6},{5,7},{6,4},{7,5},{8,10},{9,11},{10,... | collective-permute-start | bytes 4718600 | tf_op jit(solution)/shard_map/ppermute | solution.py:237
  71.4 41.3 %collective-permute-start.4 = (bf16[256,3072]{1,0:T(8,128)(2,1)}, bf16[256,3072]{1,0:T(8,128)(2,1)}, u32[]{:S(2)}, u32[]{:S(2)}) collective-permute-start(bf16[256,3072]{1,0:T(8,128)(2,1)} %pad_maximum_fusion.refs_9_), channel_id=1, source_target_pairs={{0,1},{1,0},{2,3},{3,2},{4,5},{5,4},{6,7},{7,6},{8,9},{9,8},{10,11... | collective-permute-start | bytes 4718600 | tf_op jit(solution)/shard_map/ppermute | solution.py:237
  72.9 10.6 %collective-permute-start.2 = (bf16[128,3072]{1,0:T(8,128)(2,1)}, bf16[128,3072]{1,0:T(8,128)(2,1)}, u32[]{:S(2)}, u32[]{:S(2)}) collective-permute-start(bf16[128,3072]{1,0:T(8,128)(2,1)} %collective-permute-done), channel_id=1, source_target_pairs={{8,16},{12,20},{16,24},{20,28},{9,17},{13,21},{17,25},{21,29},{10,... | collective-permute-start | bytes 2359304 | tf_op jit(solution)/shard_map/ppermute | solution.py:237
  74.5 38.2 %collective-permute-start.3 = (bf16[128,3072]{1,0:T(8,128)(2,1)}, bf16[128,3072]{1,0:T(8,128)(2,1)}, u32[]{:S(2)}, u32[]{:S(2)}) collective-permute-start(bf16[128,3072]{1,0:T(8,128)(2,1)} %collective-permute-done.1), channel_id=1, source_target_pairs={{8,0},{12,4},{16,8},{20,12},{9,1},{13,5},{17,9},{21,13},{10,2},{14... | collective-permute-start | bytes 2359304 | tf_op jit(solution)/shard_map/ppermute | solution.py:237
  82.9 0.7 copy-start.12
  112.8 65.5 %all-to-all-start.2 = ((bf16[8,256,384]{2,1,0:T(8,128)(2,1)}), bf16[8,256,384]{2,1,0:T(8,128)(2,1)}, u32[]{:S(2)}, u32[]{:S(2)}) async-start(bf16[8,256,384]{2,1,0:T(8,128)(2,1)} %get-tuple-element.83), calls=%async_computation.2 | async-start | bytes 3145728 | tf_op jit(solution)/shard_map/all_to_all | solution.py:225
  124.0 37.9 %collective-permute-start.10 = (bf16[256,3072]{1,0:T(8,128)(2,1)}, bf16[256,3072]{1,0:T(8,128)(2,1)S(1)}, u32[]{:S(2)}, u32[]{:S(2)}) collective-permute-start(bf16[256,3072]{1,0:T(8,128)(2,1)} %pad_maximum_fusion.refs_9_), channel_id=1, source_target_pairs={{0,3},{1,2},{2,1},{3,0},{4,7},{5,6},{6,5},{7,4},{8,11},{9,10},{10,... | collective-permute-start | bytes 4718600 | tf_op jit(solution)/shard_map/ppermute | solution.py:237
  128.8 49.5 %collective-permute-start.6 = (bf16[128,3072]{1,0:T(8,128)(2,1)S(1)}, bf16[128,3072]{1,0:T(8,128)(2,1)}, u32[]{:S(2)}, u32[]{:S(2)}) collective-permute-start(bf16[128,3072]{1,0:T(8,128)(2,1)S(1)} %get-tuple-element.130), channel_id=1, source_target_pairs={{8,0},{12,4},{16,24},{20,28},{9,1},{13,5},{17,25},{21,29},{10,2},{... | collective-permute-start | bytes 2359304 | tf_op jit(solution)/shard_map/ppermute | solution.py:237
  130.1 48.2 %collective-permute-start.7 = (bf16[512,128]{1,0:T(8,128)(2,1)}, bf16[512,128]{1,0:T(8,128)(2,1)}, u32[]{:S(2)}, u32[]{:S(2)}) collective-permute-start(bf16[512,128]{1,0:T(8,128)(2,1)} %get-tuple-element.85), channel_id=1, source_target_pairs={{0,8},{4,12},{8,0},{12,4},{16,24},{20,28},{24,16},{28,20},{1,9},{5... | collective-permute-start | bytes 393224 | tf_op jit(solution)/shard_map/ppermute | solution.py:237
  134.1 44.2 %collective-permute-start.8 = (bf16[512,128]{1,0:T(8,128)(2,1)}, bf16[512,128]{1,0:T(8,128)(2,1)}, u32[]{:S(2)}, u32[]{:S(2)}) collective-permute-start(bf16[512,128]{1,0:T(8,128)(2,1)} %get-tuple-element.86), channel_id=1, source_target_pairs={{0,16},{4,20},{8,24},{12,28},{16,0},{20,4},{24,8},{28,12},{1,17},{... | collective-permute-start | bytes 393224 | tf_op jit(solution)/shard_map/ppermute | solution.py:237
  136.0 42.3 %collective-permute-start.9 = (bf16[512,128]{1,0:T(8,128)(2,1)}, bf16[512,128]{1,0:T(8,128)(2,1)}, u32[]{:S(2)}, u32[]{:S(2)}) collective-permute-start(bf16[512,128]{1,0:T(8,128)(2,1)} %get-tuple-element.87), channel_id=1, source_target_pairs={{0,24},{4,28},{8,16},{12,20},{16,8},{20,12},{24,0},{28,4},{1,25},{... | collective-permute-start | bytes 393224 | tf_op jit(solution)/shard_map/ppermute | solution.py:237
  142.9 0.7 copy-start.15
  143.5 0.7 copy-start.19
  144.2 34.1 %copy-start.17 = (bf16[512,128]{1,0:T(8,128)(2,1)}, bf16[512,128]{1,0:T(8,128)(2,1)S(1)}, u32[]{:S(2)}) copy-start(bf16[512,128]{1,0:T(8,128)(2,1)S(1)} %get-tuple-element.91) | copy-start | bytes 393220
  178.3 52.9 %all-to-all-start.3 = ((bf16[8,256,384]{2,1,0:T(8,128)(2,1)}), bf16[8,256,384]{2,1,0:T(8,128)(2,1)S(1)}, u32[]{:S(2)}, u32[]{:S(2)}) async-start(bf16[8,256,384]{2,1,0:T(8,128)(2,1)} %get-tuple-element.93), calls=%async_computation.3 | async-start | bytes 3145728 | tf_op jit(solution)/shard_map/all_to_all | solution.py:225
  182.1 1.6 copy-start.27
  183.7 3.2 %copy-start.20 = (bf16[512,128]{1,0:T(8,128)(2,1)S(1)}, bf16[512,128]{1,0:T(8,128)(2,1)}, u32[]{:S(2)}) copy-start(bf16[512,128]{1,0:T(8,128)(2,1)} %copy-done.19) | copy-start | bytes 393220
  183.7 4.9 %copy-start.18 = (bf16[512,128]{1,0:T(8,128)(2,1)S(1)}, bf16[512,128]{1,0:T(8,128)(2,1)}, u32[]{:S(2)}) copy-start(bf16[512,128]{1,0:T(8,128)(2,1)} %copy-done.17) | copy-start | bytes 393220
  183.7 7.5 %copy-start.16 = (bf16[512,128]{1,0:T(8,128)(2,1)S(1)}, bf16[512,128]{1,0:T(8,128)(2,1)}, u32[]{:S(2)}) copy-start(bf16[512,128]{1,0:T(8,128)(2,1)} %copy-done.15) | copy-start | bytes 393220
  183.8 46.3 %copy-start.1 = (bf16[256,3072]{1,0:T(8,128)(2,1)}, bf16[256,3072]{1,0:T(8,128)(2,1)S(1)}, u32[]{:S(2)}) copy-start(bf16[256,3072]{1,0:T(8,128)(2,1)S(1)} %pad_maximum_fusion.1.refs_12_) | copy-start | bytes 4718596
  183.8 13.5 %copy-start.13 = (bf16[512,128]{1,0:T(8,128)(2,1)S(1)}, bf16[512,128]{1,0:T(8,128)(2,1)}, u32[]{:S(2)}) copy-start(bf16[512,128]{1,0:T(8,128)(2,1)} %copy-done.12) | copy-start | bytes 393220
  183.8 46.2 %collective-permute-start.12 = (bf16[256,3072]{1,0:T(8,128)(2,1)S(1)}, bf16[256,3072]{1,0:T(8,128)(2,1)S(1)}, u32[]{:S(2)}, u32[]{:S(2)}) collective-permute-start(bf16[256,3072]{1,0:T(8,128)(2,1)S(1)} %pad_maximum_fusion.1.refs_12_), channel_id=1, source_target_pairs={{0,2},{1,3},{2,0},{3,1},{4,6},{5,7},{6,4},{7,5},{8,10},{9,11},{10,... | collective-permute-start | bytes 4718600 | tf_op jit(solution)/shard_map/ppermute | solution.py:237
  185.4 45.8 %collective-permute-start.11 = (bf16[256,3072]{1,0:T(8,128)(2,1)S(1)}, bf16[256,3072]{1,0:T(8,128)(2,1)}, u32[]{:S(2)}, u32[]{:S(2)}) collective-permute-start(bf16[256,3072]{1,0:T(8,128)(2,1)S(1)} %pad_maximum_fusion.1.refs_12_), channel_id=1, source_target_pairs={{0,1},{1,0},{2,3},{3,2},{4,5},{5,4},{6,7},{7,6},{8,9},{9,8},{10,11... | collective-permute-start | bytes 4718600 | tf_op jit(solution)/shard_map/ppermute | solution.py:237
  186.9 24.6 %collective-permute-start.13 = (bf16[512,128]{1,0:T(8,128)(2,1)S(1)}, bf16[512,128]{1,0:T(8,128)(2,1)S(1)}, u32[]{:S(2)}, u32[]{:S(2)}) collective-permute-start(bf16[512,128]{1,0:T(8,128)(2,1)S(1)} %copy-done.20), channel_id=1, source_target_pairs={{0,8},{4,12},{8,0},{12,4},{16,24},{20,28},{24,16},{28,20},{1,9},{5... | collective-permute-start | bytes 393224 | tf_op jit(solution)/shard_map/ppermute | solution.py:237
  188.6 40.1 %collective-permute-start.14 = (bf16[512,128]{1,0:T(8,128)(2,1)S(1)}, bf16[512,128]{1,0:T(8,128)(2,1)S(1)}, u32[]{:S(2)}, u32[]{:S(2)}) collective-permute-start(bf16[512,128]{1,0:T(8,128)(2,1)S(1)} %copy-done.18), channel_id=1, source_target_pairs={{0,16},{4,20},{8,24},{12,28},{16,0},{20,4},{24,8},{28,12},{1,17},{... | collective-permute-start | bytes 393224 | tf_op jit(solution)/shard_map/ppermute | solution.py:237
  191.2 38.2 %collective-permute-start.15 = (bf16[512,128]{1,0:T(8,128)(2,1)S(1)}, bf16[512,128]{1,0:T(8,128)(2,1)S(1)}, u32[]{:S(2)}, u32[]{:S(2)}) collective-permute-start(bf16[512,128]{1,0:T(8,128)(2,1)S(1)} %copy-done.16), channel_id=1, source_target_pairs={{0,24},{4,28},{8,16},{12,20},{16,8},{20,12},{24,0},{28,4},{1,25},{... | collective-permute-start | bytes 393224 | tf_op jit(solution)/shard_map/ppermute | solution.py:237
  197.3 32.8 %copy-start.10 = (bf16[512,128]{1,0:T(8,128)(2,1)}, bf16[512,128]{1,0:T(8,128)(2,1)S(1)}, u32[]{:S(2)}) copy-start(bf16[512,128]{1,0:T(8,128)(2,1)S(1)} %get-tuple-element.121.refs_5_) | copy-start | bytes 393220
  197.3 32.7 %copy-start.21 = (bf16[512,128]{1,0:T(8,128)(2,1)}, bf16[512,128]{1,0:T(8,128)(2,1)S(1)}, u32[]{:S(2)}) copy-start(bf16[512,128]{1,0:T(8,128)(2,1)S(1)} %get-tuple-element.108) | copy-start | bytes 393220
  197.3 32.7 %copy-start.23 = (bf16[512,128]{1,0:T(8,128)(2,1)}, bf16[512,128]{1,0:T(8,128)(2,1)S(1)}, u32[]{:S(2)}) copy-start(bf16[512,128]{1,0:T(8,128)(2,1)S(1)} %get-tuple-element.107) | copy-start | bytes 393220
  197.3 32.7 %copy-start.25 = (bf16[512,128]{1,0:T(8,128)(2,1)}, bf16[512,128]{1,0:T(8,128)(2,1)S(1)}, u32[]{:S(2)}) copy-start(bf16[512,128]{1,0:T(8,128)(2,1)S(1)} %get-tuple-element.106) | copy-start | bytes 393220
  228.7 0.7 copy-start.6
  229.4 0.7 copy-start.8
  230.1 1.1 copy-start.3
  231.2 5.8 %copy-start.26 = (bf16[512,128]{1,0:T(8,128)(2,1)S(1)}, bf16[512,128]{1,0:T(8,128)(2,1)}, u32[]{:S(2)}) copy-start(bf16[512,128]{1,0:T(8,128)(2,1)} %copy-done.25) | copy-start | bytes 393220
  231.3 8.0 %copy-start.24 = (bf16[512,128]{1,0:T(8,128)(2,1)S(1)}, bf16[512,128]{1,0:T(8,128)(2,1)}, u32[]{:S(2)}) copy-start(bf16[512,128]{1,0:T(8,128)(2,1)} %copy-done.23) | copy-start | bytes 393220
  231.3 8.0 %copy-start.22 = (bf16[512,128]{1,0:T(8,128)(2,1)S(1)}, bf16[512,128]{1,0:T(8,128)(2,1)}, u32[]{:S(2)}) copy-start(bf16[512,128]{1,0:T(8,128)(2,1)} %copy-done.21) | copy-start | bytes 393220
  231.3 27.6 %copy-start.5 = (bf16[512,512]{1,0:T(8,128)(2,1)S(1)}, bf16[512,512]{1,0:T(8,128)(2,1)}, u32[]{:S(2)}) copy-start(bf16[512,512]{1,0:T(8,128)(2,1)} %pad_maximum_fusion.2.refs_0_) | copy-start | bytes 1572868
  231.3 27.6 %copy-start.7 = (bf16[512,128]{1,0:T(8,128)(2,1)S(1)}, bf16[512,128]{1,0:T(8,128)(2,1)}, u32[]{:S(2)}) copy-start(bf16[512,128]{1,0:T(8,128)(2,1)} %copy-done.6) | copy-start | bytes 393220
  231.3 27.6 %copy-start.9 = (bf16[512,128]{1,0:T(8,128)(2,1)S(1)}, bf16[512,128]{1,0:T(8,128)(2,1)}, u32[]{:S(2)}) copy-start(bf16[512,128]{1,0:T(8,128)(2,1)} %copy-done.8) | copy-start | bytes 393220
  231.3 27.6 %copy-start.11 = (bf16[512,128]{1,0:T(8,128)(2,1)S(1)}, bf16[512,128]{1,0:T(8,128)(2,1)}, u32[]{:S(2)}) copy-start(bf16[512,128]{1,0:T(8,128)(2,1)} %copy-done.10) | copy-start | bytes 393220
  232.6 26.3 %copy-start.2 = (bf16[256,3072]{1,0:T(8,128)(2,1)S(1)}, bf16[256,3072]{1,0:T(8,128)(2,1)}, u32[]{:S(2)}) copy-start(bf16[256,3072]{1,0:T(8,128)(2,1)} %copy-done.1) | copy-start | bytes 4718596
  232.6 26.3 %copy-start.4 = (bf16[256,3072]{1,0:T(8,128)(2,1)S(1)}, bf16[256,3072]{1,0:T(8,128)(2,1)}, u32[]{:S(2)}) copy-start(bf16[256,3072]{1,0:T(8,128)(2,1)} %copy-done.3) | copy-start | bytes 4718596
  234.0 32.7 %collective-permute-start.22 = (bf16[128,3072]{1,0:T(8,128)(2,1)S(1)}, bf16[128,3072]{1,0:T(8,128)(2,1)S(1)}, u32[]{:S(2)}, u32[]{:S(2)}) collective-permute-start(bf16[128,3072]{1,0:T(8,128)(2,1)S(1)} %slice.6), channel_id=1, source_target_pairs={{0,2},{1,3},{2,0},{3,1},{4,6},{5,7},{6,4},{7,5},{8,10},{9,11},{10,... | collective-permute-start | bytes 2359304 | tf_op jit(solution)/shard_map/ppermute | solution.py:237
  235.5 31.1 %collective-permute-start.23 = (bf16[128,3072]{1,0:T(8,128)(2,1)S(1)}, bf16[128,3072]{1,0:T(8,128)(2,1)S(1)}, u32[]{:S(2)}, u32[]{:S(2)}) collective-permute-start(bf16[128,3072]{1,0:T(8,128)(2,1)S(1)} %slice.7), channel_id=1, source_target_pairs={{0,1},{1,0},{2,3},{3,2},{4,5},{5,4},{6,7},{7,6},{8,9},{9,8},{10,11... | collective-permute-start | bytes 2359304 | tf_op jit(solution)/shard_map/ppermute | solution.py:237
  237.0 10.4 %collective-permute-start.16 = (bf16[512,128]{1,0:T(8,128)(2,1)S(1)}, bf16[512,128]{1,0:T(8,128)(2,1)S(1)}, u32[]{:S(2)}, u32[]{:S(2)}) collective-permute-start(bf16[512,128]{1,0:T(8,128)(2,1)S(1)} %copy-done.26), channel_id=1, source_target_pairs={{0,8},{4,12},{8,0},{12,4},{16,24},{20,28},{24,16},{28,20},{1,9},{5... | collective-permute-start | bytes 393224 | tf_op jit(solution)/shard_map/ppermute | solution.py:237
  239.3 16.2 %collective-permute-start.17 = (bf16[512,128]{1,0:T(8,128)(2,1)S(1)}, bf16[512,128]{1,0:T(8,128)(2,1)S(1)}, u32[]{:S(2)}, u32[]{:S(2)}) collective-permute-start(bf16[512,128]{1,0:T(8,128)(2,1)S(1)} %copy-done.24), channel_id=1, source_target_pairs={{0,16},{4,20},{8,24},{12,28},{16,0},{20,4},{24,8},{28,12},{1,17},{... | collective-permute-start | bytes 393224 | tf_op jit(solution)/shard_map/ppermute | solution.py:237
  239.3 17.7 %collective-permute-start.18 = (bf16[512,128]{1,0:T(8,128)(2,1)S(1)}, bf16[512,128]{1,0:T(8,128)(2,1)S(1)}, u32[]{:S(2)}, u32[]{:S(2)}) collective-permute-start(bf16[512,128]{1,0:T(8,128)(2,1)S(1)} %copy-done.22), channel_id=1, source_target_pairs={{0,24},{4,28},{8,16},{12,20},{16,8},{20,12},{24,0},{28,4},{1,25},{... | collective-permute-start | bytes 393224 | tf_op jit(solution)/shard_map/ppermute | solution.py:237
  247.4 19.2 %collective-permute-start.20 = (bf16[512,128]{1,0:T(8,128)(2,1)S(1)}, bf16[512,128]{1,0:T(8,128)(2,1)S(1)}, u32[]{:S(2)}, u32[]{:S(2)}) collective-permute-start(bf16[512,128]{1,0:T(8,128)(2,1)S(1)} %get-tuple-element.111), channel_id=1, source_target_pairs={{0,16},{4,20},{8,24},{12,28},{16,0},{20,4},{24,8},{28,12},{1,17},{... | collective-permute-start | bytes 393224 | tf_op jit(solution)/shard_map/ppermute | solution.py:237
  255.5 11.2 %collective-permute-start.21 = (bf16[512,128]{1,0:T(8,128)(2,1)S(1)}, bf16[512,128]{1,0:T(8,128)(2,1)S(1)}, u32[]{:S(2)}, u32[]{:S(2)}) collective-permute-start(bf16[512,128]{1,0:T(8,128)(2,1)S(1)} %get-tuple-element.112), channel_id=1, source_target_pairs={{0,24},{4,28},{8,16},{12,20},{16,8},{20,12},{24,0},{28,4},{1,25},{... | collective-permute-start | bytes 393224 | tf_op jit(solution)/shard_map/ppermute | solution.py:237
  257.0 9.7 %collective-permute-start.19 = (bf16[512,128]{1,0:T(8,128)(2,1)S(1)}, bf16[512,128]{1,0:T(8,128)(2,1)S(1)}, u32[]{:S(2)}, u32[]{:S(2)}) collective-permute-start(bf16[512,128]{1,0:T(8,128)(2,1)S(1)} %get-tuple-element.110), channel_id=1, source_target_pairs={{0,8},{4,12},{8,0},{12,4},{16,24},{20,28},{24,16},{28,20},{1,9},{5... | collective-permute-start | bytes 393224 | tf_op jit(solution)/shard_map/ppermute | solution.py:237
  268.5 3.5 %collective-permute-start.24 = (bf16[256,3072]{1,0:T(8,128)(2,1)S(1)}, bf16[256,3072]{1,0:T(8,128)(2,1)S(1)}, u32[]{:S(2)}, u32[]{:S(2)}) collective-permute-start(bf16[256,3072]{1,0:T(8,128)(2,1)S(1)} %convert_element_type.9), channel_id=1, source_target_pairs={{0,4},{4,0},{8,12},{12,8},{16,20},{20,16},{24,28},{28,24},{1,5},{5... | collective-permute-start | bytes 4718600 | tf_op jit(solution)/shard_map/ppermute | solution.py:237

commit v5 on v4

--- a/solution.py
+++ b/solution.py
@@ -245,9 +245,6 @@
     def sides(block):
         return [along(block, "fsdp", xor(1, 4)), along(block, "fsdp", xor(2, 4))]
 
-    def corner(x, y):
-        return [along(x[:n], "fsdp", xor(2, 4)), along(y[n:], "fsdp", xor(1, 4))]
-
     def fence(*values):
         return lax.optimization_barrier(values)
 
@@ -277,21 +274,20 @@
     back1 = send_back(out1)
     out2 = attend_step(qkv2, 2)
     joined = jnp.concatenate(back0, axis=1)
-    qkv3, far_sides, back1, out2, joined = fence(qkv3, far_sides, back1, out2, joined)
+    halves = [far_sides[0][:n], far_sides[1][n:]]
+    qkv3, far_sides, halves, back1, out2, joined = fence(qkv3, far_sides, halves, back1, out2, joined)
+    joined1 = jnp.concatenate(back1, axis=1)
     back2 = send_back(out2)
     out3 = attend_step(qkv3, 3)
-    far_corner = corner(*far_sides)
-    back3 = [out3[0], None] + [along(out3[p], "seq", xor(2 * p, groups)) for p in (2, 3)]
-    back2, side = fence(back2, out3[1])
-    back3[1] = along(side, "seq", xor(2, groups))
+    far_corner = [along(halves[0], "fsdp", xor(2, 4)), along(halves[1], "fsdp", xor(1, 4))]
+    back2, out3 = fence(back2, out3)
+    back3 = send_back(out3)
 
     sides_all = [near] + near_sides + [far] + far_sides
-    rows = [joined] + back1 + back2
+    rows = [joined, joined1] + back2
     early = [((0,), ((0, 0),), both), ((3,), ((0, 2 * width),), both)]
-    for m in (1, 2):
-        for h in (0, 1):
-            at = 4 * m - 3 + 2 * h
-            early.append(((m + 3 * h,), ((at, 0), (at + 1, 0)), both))
+    early += [((1,), ((1, 0),), both), ((4,), ((1, 2 * width),), both)]
+    early += [((2,), ((2, 0), (3, 0)), both), ((5,), ((4, 0), (5, 0)), both)]
     mine, theirs = project(rows, sides_all, early, [], 2)
 
     def finish(cut, before):

time: 274 us -> 272 us (level)
  waiting for transfers between devices: 135 us -> 132 us
    ppermute x25, waiting for transfers between devices: 135 us -> 132 us  [along(): return lax.ppermute(value, axis, pairs)]
    unnamed x62 -> x52, local copies, waits for them, and re-layouts: 4.63 us -> 5.6 us
  transfers between devices with their start and end apart: 29 -> 29, of which waited for: 9 -> 10; matrix products, arithmetic and copies ran while one was open for 3% -> 4% of each run, Pallas kernels for 14% -> 15%
where the time goes in v5:
time: 272 us; the launch traced here: 271 us
  waiting for transfers between devices  132 us (49%)
  starting transfers between devices  75.4 us (28%)
  Pallas kernels  44.8 us (16%)
  other arithmetic  11 us (4%)
  local copies, waits for them, and re-layouts  7.89 us (3%)
    ppermute x25, waiting for transfers between devices, along(): return lax.ppermute(value, axis, pairs)  132 us
    ppermute x25, starting transfers between devices, along(): return lax.ppermute(value, axis, pairs)  42.7 us
    all_to_all x4, starting transfers between devices, exchange(): return lax.all_to_all(x, 'seq', split_axis=0, concat_axis=0, tiled=True)  32.7 us
    pallas_call x4, Pallas kernels, attend(): pl.pallas_call(functools.partial(attend_kernel, step, at_lane, width, slo...  24.6 us
    pallas_call x3, Pallas kernels, project(): pl.pallas_call(functools.partial(project_kernel, terms, len(rows), len(bl...  10.7 us
    pallas_call x2, Pallas kernels, lay_out(): pl.pallas_call(functools.partial(layout_kernel, steps, here, width), out_...  9.52 us
    unnamed x52, local copies, waits for them, and re-layouts  5.6 us
  transfers between devices with their start and end apart: 29, of which 10 were waited for; matrix products, arithmetic and copies ran while one was open for 4% of the time, Pallas kernels for 15%

profile of v5, /device:TPU:0, one launch (start us, length us, event | category | flops | bytes accessed | tf_op | source)
XLA Modules:
  0.0 271.1 jit_solution(4870794928029218695)
XLA Ops:
  0.0 0.6 pad_add_fusion.place_ref
  0.6 3.5 %shard_map.64.refs_3_ = bf16[8,256,384]{2,1,0:T(8,128)(2,1)} custom-call(s32[2]{0:T(128)} %pad_add_fusion.place_ref, bf16[256,4096]{1,0:T(8,128)(2,1)} %bitcast.14, bf16[256,4096]{1,0:T(8,128)(2,1)} %bitcast.16, bf16[256,4096]{1,0:T(8,128)(2,1)} %bitcast.18), custom_call_target="tpu_custom_call" | custom-call | flops 1 | bytes 1 | tf_op jit(solution)/shard_map/pallas_call | solution.py:48
  4.1 6.5 %all-to-all-start = ((bf16[8,256,384]{2,1,0:T(8,128)(2,1)}), bf16[8,256,384]{2,1,0:T(8,128)(2,1)S(1)}, u32[]{:S(2)}, u32[]{:S(2)}) async-start(bf16[8,256,384]{2,1,0:T(8,128)(2,1)} %shard_map.64.refs_3_), calls=%async_computation | async-start | bytes 3145728 | tf_op jit(solution)/shard_map/all_to_all | solution.py:225
  10.6 4.8 %collective-permute-start = (bf16[128,3072]{1,0:T(8,128)(2,1)S(1)}, bf16[128,3072]{1,0:T(8,128)(2,1)}, u32[]{:S(2)}, u32[]{:S(2)}) collective-permute-start(bf16[128,3072]{1,0:T(8,128)(2,1)S(1)} %copy-done.15), channel_id=1, source_target_pairs={{0,8},{4,12},{8,16},{12,20},{16,24},{20,28},{1,9},{5,13},{9,17},{1... | collective-permute-start | bytes 2359304 | tf_op jit(solution)/shard_map/ppermute | solution.py:237
  15.4 1.3 collective-permute-start.1
  16.7 6.1 %shard_map.65 = (bf16[8,256,384]{2,1,0:T(8,128)(2,1)}, bf16[8,256,384]{2,1,0:T(8,128)(2,1)}, bf16[8,256,384]{2,1,0:T(8,128)(2,1)}) custom-call(s32[2]{0:T(128)} %pad_add_fusion.place_ref, bf16[256,4096]{1,0:T(8,128)(2,1)} %bitcast.15, bf16[256,4096]{1,0:T(8,128)(2,1)} %bitcast.17, bf16[256,4096]{1,0:T(8,128)(2,1)} %bitcast.19, ...), custom_call_target="tpu_custom_call" | custom-call | flops 1 | bytes 1 | tf_op jit(solution)/shard_map/pallas_call | solution.py:48
  22.7 31.1 %collective-permute-done = bf16[128,3072]{1,0:T(8,128)(2,1)} collective-permute-done((bf16[128,3072]{1,0:T(8,128)(2,1)S(1)}, bf16[128,3072]{1,0:T(8,128)(2,1)}, u32[]{:S(2)}, u32[]{:S(2)}) %collective-permute-start) | collective-permute-done | bytes 786464 | tf_op jit(solution)/shard_map/ppermute | solution.py:237
  53.9 2.2 collective-permute-done.1
  56.0 11.2 %all-to-all-start.1 = ((bf16[8,256,384]{2,1,0:T(8,128)(2,1)}), bf16[8,256,384]{2,1,0:T(8,128)(2,1)S(1)}, u32[]{:S(2)}, u32[]{:S(2)}) async-start(bf16[8,256,384]{2,1,0:T(8,128)(2,1)} %get-tuple-element.78), calls=%async_computation.1 | async-start | bytes 3145728 | tf_op jit(solution)/shard_map/all_to_all | solution.py:225
  67.3 1.3 broadcast_select_fusion.1
  68.6 1.2 pad_maximum_fusion.refs_6_
  69.9 1.5 collective-permute-start.5
  71.4 1.5 collective-permute-start.4
  72.9 1.5 collective-permute-start.2
  74.4 1.3 collective-permute-start.3
  76.0 5.9 %shard_map.66 = (bf16[512,128]{1,0:T(8,128)(2,1)S(1)}, bf16[512,128]{1,0:T(8,128)(2,1)}, bf16[512,128]{1,0:T(8,128)(2,1)}, bf16[512,128]{1,0:T(8,128)(2,1)S(1)}) custom-call(s32[2]{0:T(128)S(1)} %copy-done.10, s32[4,128]{1,0:T(4,128)S(1)} %copy.11.lists_ref, s32[4,16]{1,0:T(4,128)S(1)} %bitcast.10, bf16[8,256,384]{2,1,0:T(8,128)(2,1)S(1)} %all-to-all-done.refs_0_), custom_call_target="tpu_custom_call" | custom-call | flops 1 | bytes 1 | tf_op jit(solution)/shard_map/pallas_call | solution.py:128
  81.9 0.7 copy-done.8
  82.6 30.2 %collective-permute-done.3 = bf16[128,3072]{1,0:T(8,128)(2,1)} collective-permute-done((bf16[128,3072]{1,0:T(8,128)(2,1)}, bf16[128,3072]{1,0:T(8,128)(2,1)}, u32[]{:S(2)}, u32[]{:S(2)}) %collective-permute-start.3) | collective-permute-done | bytes 786464 | tf_op jit(solution)/shard_map/ppermute | solution.py:237
  112.7 11.2 %all-to-all-start.2 = ((bf16[8,256,384]{2,1,0:T(8,128)(2,1)}), bf16[8,256,384]{2,1,0:T(8,128)(2,1)}, u32[]{:S(2)}, u32[]{:S(2)}) async-start(bf16[8,256,384]{2,1,0:T(8,128)(2,1)} %get-tuple-element.88), calls=%async_computation.2 | async-start | bytes 3145728 | tf_op jit(solution)/shard_map/all_to_all | solution.py:225
  123.9 2.4 collective-permute-start.10
  126.4 2.4 broadcast_select_fusion
  128.8 1.3 collective-permute-start.6
  130.0 3.9 %collective-permute-start.7 = (bf16[512,128]{1,0:T(8,128)(2,1)}, bf16[512,128]{1,0:T(8,128)(2,1)S(1)}, u32[]{:S(2)}, u32[]{:S(2)}) collective-permute-start(bf16[512,128]{1,0:T(8,128)(2,1)} %get-tuple-element.90), channel_id=1, source_target_pairs={{0,8},{4,12},{8,0},{12,4},{16,24},{20,28},{24,16},{28,20},{1,9},{5... | collective-permute-start | bytes 393224 | tf_op jit(solution)/shard_map/ppermute | solution.py:237
  133.9 2.0 collective-permute-start.8
  135.9 1.5 collective-permute-start.9
  137.4 6.3 %shard_map.67 = (bf16[512,128]{1,0:T(8,128)(2,1)S(1)}, bf16[512,128]{1,0:T(8,128)(2,1)}, bf16[512,128]{1,0:T(8,128)(2,1)}, bf16[512,128]{1,0:T(8,128)(2,1)}) custom-call(s32[2]{0:T(128)S(1)} %copy-done.10, s32[4,128]{1,0:T(4,128)S(1)} %copy.11.lists_ref, s32[4,16]{1,0:T(4,128)S(1)} %bitcast.11, bf16[8,256,384]{2,1,0:T(8,128)(2,1)S(1)} %all-to-all-done.1.refs_0_), custom_call_target="tpu_custom_call" | custom-call | flops 1 | bytes 1 | tf_op jit(solution)/shard_map/pallas_call | solution.py:128
  143.6 18.2 %collective-permute-done.10.refs_4_ = bf16[256,3072]{1,0:T(8,128)(2,1)S(1)} collective-permute-done((bf16[256,3072]{1,0:T(8,128)(2,1)}, bf16[256,3072]{1,0:T(8,128)(2,1)S(1)}, u32[]{:S(2)}, u32[]{:S(2)}) %collective-permute-start.10) | collective-permute-done | bytes 1572896 | tf_op jit(solution)/shard_map/ppermute | solution.py:237
  161.9 16.3 %collective-permute-done.7 = bf16[512,128]{1,0:T(8,128)(2,1)S(1)} collective-permute-done((bf16[512,128]{1,0:T(8,128)(2,1)}, bf16[512,128]{1,0:T(8,128)(2,1)S(1)}, u32[]{:S(2)}, u32[]{:S(2)}) %collective-permute-start.7) | collective-permute-done | bytes 131104 | tf_op jit(solution)/shard_map/ppermute | solution.py:237
  178.1 0.6 copy-done.19
  178.8 0.6 copy-done.23
  179.5 3.8 %all-to-all-start.3 = ((bf16[8,256,384]{2,1,0:T(8,128)(2,1)}), bf16[8,256,384]{2,1,0:T(8,128)(2,1)S(1)}, u32[]{:S(2)}, u32[]{:S(2)}) async-start(bf16[8,256,384]{2,1,0:T(8,128)(2,1)} %get-tuple-element.98), calls=%async_computation.3 | async-start | bytes 3145728 | tf_op jit(solution)/shard_map/all_to_all | solution.py:225
  183.3 1.6 select_select_fusion
  184.9 0.1 pad_maximum_fusion.1.refs_9_
  185.0 1.6 collective-permute-start.12
  186.6 1.5 collective-permute-start.11
  188.1 1.6 collective-permute-start.13
  189.8 2.6 collective-permute-start.14
  192.4 0.1 collective-permute-start.15
  192.5 6.8 %shard_map.68 = (bf16[512,128]{1,0:T(8,128)(2,1)S(1)}, bf16[512,128]{1,0:T(8,128)(2,1)S(1)}, bf16[512,128]{1,0:T(8,128)(2,1)S(1)}, bf16[512,128]{1,0:T(8,128)(2,1)S(1)}) custom-call(s32[2]{0:T(128)S(1)} %copy-done.10, s32[4,128]{1,0:T(4,128)S(1)} %copy.11.lists_ref, s32[4,16]{1,0:T(4,128)S(1)} %bitcast.12, bf16[8,256,384]{2,1,0:T(8,128)(2,1)} %all-to-all-done.2.refs_0_), custom_call_target="tpu_custom_call" | custom-call | flops 1 | bytes 1 | tf_op jit(solution)/shard_map/pallas_call | solution.py:128
  199.4 0.9 pad_maximum_fusion.2.refs_0_
  200.3 21.4 %collective-permute-done.12.refs_11_ = bf16[256,3072]{1,0:T(8,128)(2,1)S(1)} collective-permute-done((bf16[256,3072]{1,0:T(8,128)(2,1)S(1)}, bf16[256,3072]{1,0:T(8,128)(2,1)S(1)}, u32[]{:S(2)}, u32[]{:S(2)}) %collective-permute-start.12) | collective-permute-done | bytes 1572896 | tf_op jit(solution)/shard_map/ppermute | solution.py:237
  221.8 1.0 slice.9
  222.8 0.2 collective-permute-done.11.refs_10_
  223.0 1.0 slice.8
  224.0 5.9 %collective-permute-done.14 = bf16[512,128]{1,0:T(8,128)(2,1)S(1)} collective-permute-done((bf16[512,128]{1,0:T(8,128)(2,1)}, bf16[512,128]{1,0:T(8,128)(2,1)S(1)}, u32[]{:S(2)}, u32[]{:S(2)}) %collective-permute-start.14) | collective-permute-done | bytes 131104 | tf_op jit(solution)/shard_map/ppermute | solution.py:237
  229.9 0.6 copy-done.18
  230.6 1.6 collective-permute-start.22
  232.2 1.5 collective-permute-start.23
  233.7 2.3 collective-permute-start.16
  236.0 2.4 collective-permute-start.18
  238.3 5.7 %shard_map.69 = (bf16[512,128]{1,0:T(8,128)(2,1)S(1)}, bf16[512,128]{1,0:T(8,128)(2,1)S(1)}, bf16[512,128]{1,0:T(8,128)(2,1)S(1)}, bf16[512,128]{1,0:T(8,128)(2,1)S(1)}) custom-call(s32[2]{0:T(128)S(1)} %copy-done.10, s32[4,128]{1,0:T(4,128)S(1)} %copy.11.lists_ref, s32[4,16]{1,0:T(4,128)S(1)} %bitcast.13, bf16[8,256,384]{2,1,0:T(8,128)(2,1)S(1)} %all-to-all-done.3.refs_0_), custom_call_target="tpu_custom_call" | custom-call | flops 1 | bytes 1 | tf_op jit(solution)/shard_map/pallas_call | solution.py:128
  244.0 4.2 %collective-permute-done.17.refs_4_ = bf16[512,128]{1,0:T(8,128)(2,1)S(1)} collective-permute-done((bf16[512,128]{1,0:T(8,128)(2,1)}, bf16[512,128]{1,0:T(8,128)(2,1)S(1)}, u32[]{:S(2)}, u32[]{:S(2)}) %collective-permute-start.17) | collective-permute-done | bytes 131104 | tf_op jit(solution)/shard_map/ppermute | solution.py:237
  248.2 2.1 collective-permute-start.19
  250.3 0.2 collective-permute-start.20
  250.5 2.2 collective-permute-start.21
  252.6 1.1 pad_maximum_fusion.3.refs_1_
  253.8 1.4 copy-done.4
  255.2 1.4 copy-done.6
  256.6 7.7 %shard_map.70 = (f32[256,3072]{1,0:T(8,128)S(1)}, f32[256,3072]{1,0:T(8,128)S(1)}) custom-call(bf16[512,512]{1,0:T(8,128)(2,1)S(1)} %copy-done.7, bf16[512,512]{1,0:T(8,128)(2,1)S(1)} %pad_maximum_fusion.3.refs_1_, bf16[512,128]{1,0:T(8,128)(2,1)S(1)} %get-tuple-element.129.refs_2_, bf16[512,128]{1,0:T(8,128)(2,1)S(1)} %collective-permute-done.16.refs_3_, ...), custom_call_target="tpu_custom_call" | custom-call | flops 1 | bytes 1 | tf_op jit(solution)/shard_map/pallas_call | solution.py:192
  264.3 1.5 shard_map.72
  265.8 0.2 convert_element_type.9
  266.1 1.5 shard_map.71
  267.7 1.9 collective-permute-done.24
  269.5 1.6 fusion
  (71 shorter events, 0.7 us)
Async XLA Ops:
  0.0 75.9 %copy-start = (s32[1,32,16,8]{1,3,2,0:T(8,128)S(1)}, s32[1,32,16,8]{1,3,2,0:T(8,128)}, u32[]{:S(2)}) copy-start(s32[1,32,16,8]{1,3,2,0:T(8,128)} %param.10) | copy-start | bytes 49156
  4.1 6.5 %copy-start.15 = (bf16[128,3072]{1,0:T(8,128)(2,1)S(1)}, bf16[128,3072]{1,0:T(8,128)(2,1)}, u32[]{:S(2)}) copy-start(bf16[128,3072]{1,0:T(8,128)(2,1)} %param.9) | copy-start | bytes 2359300
  4.1 51.9 %all-to-all-start = ((bf16[8,256,384]{2,1,0:T(8,128)(2,1)}), bf16[8,256,384]{2,1,0:T(8,128)(2,1)S(1)}, u32[]{:S(2)}, u32[]{:S(2)}) async-start(bf16[8,256,384]{2,1,0:T(8,128)(2,1)} %shard_map.64.refs_3_), calls=%async_computation | async-start | bytes 3145728 | tf_op jit(solution)/shard_map/all_to_all | solution.py:225
  10.6 43.3 %collective-permute-start = (bf16[128,3072]{1,0:T(8,128)(2,1)S(1)}, bf16[128,3072]{1,0:T(8,128)(2,1)}, u32[]{:S(2)}, u32[]{:S(2)}) collective-permute-start(bf16[128,3072]{1,0:T(8,128)(2,1)S(1)} %copy-done.15), channel_id=1, source_target_pairs={{0,8},{4,12},{8,16},{12,20},{16,24},{20,28},{1,9},{5,13},{9,17},{1... | collective-permute-start | bytes 2359304 | tf_op jit(solution)/shard_map/ppermute | solution.py:237
  15.4 40.6 %collective-permute-start.1 = (bf16[128,3072]{1,0:T(8,128)(2,1)S(1)}, bf16[128,3072]{1,0:T(8,128)(2,1)}, u32[]{:S(2)}, u32[]{:S(2)}) collective-permute-start(bf16[128,3072]{1,0:T(8,128)(2,1)S(1)} %copy-done.15), channel_id=1, source_target_pairs={{8,0},{12,4},{16,8},{20,12},{24,16},{28,20},{9,1},{13,5},{17,9},{2... | collective-permute-start | bytes 2359304 | tf_op jit(solution)/shard_map/ppermute | solution.py:237
  56.0 56.7 %all-to-all-start.1 = ((bf16[8,256,384]{2,1,0:T(8,128)(2,1)}), bf16[8,256,384]{2,1,0:T(8,128)(2,1)S(1)}, u32[]{:S(2)}, u32[]{:S(2)}) async-start(bf16[8,256,384]{2,1,0:T(8,128)(2,1)} %get-tuple-element.78), calls=%async_computation.1 | async-start | bytes 3145728 | tf_op jit(solution)/shard_map/all_to_all | solution.py:225
  67.2 1.4 copy-start.16
  68.6 7.1 %copy-start.25 = (s32[1,32,16]{1,2,0:T(8,128)S(1)}, s32[1,32,16]{1,2,0:T(8,128)}, u32[]{:S(2)}) copy-start(s32[1,32,16]{1,2,0:T(8,128)} %param.11) | copy-start | bytes 6148
  68.6 7.4 %copy-start.10 = (s32[2]{0:T(128)S(1)}, s32[2]{0:T(128)}, u32[]{:S(2)}) copy-start(s32[2]{0:T(128)} %pad_add_fusion.place_ref) | copy-start | bytes 28
  69.9 42.8 %collective-permute-start.5 = (bf16[256,3072]{1,0:T(8,128)(2,1)}, bf16[256,3072]{1,0:T(8,128)(2,1)}, u32[]{:S(2)}, u32[]{:S(2)}) collective-permute-start(bf16[256,3072]{1,0:T(8,128)(2,1)} %pad_maximum_fusion.refs_6_), channel_id=1, source_target_pairs={{0,2},{1,3},{2,0},{3,1},{4,6},{5,7},{6,4},{7,5},{8,10},{9,11},{10,... | collective-permute-start | bytes 4718600 | tf_op jit(solution)/shard_map/ppermute | solution.py:237
  71.4 41.3 %collective-permute-start.4 = (bf16[256,3072]{1,0:T(8,128)(2,1)}, bf16[256,3072]{1,0:T(8,128)(2,1)}, u32[]{:S(2)}, u32[]{:S(2)}) collective-permute-start(bf16[256,3072]{1,0:T(8,128)(2,1)} %pad_maximum_fusion.refs_6_), channel_id=1, source_target_pairs={{0,1},{1,0},{2,3},{3,2},{4,5},{5,4},{6,7},{7,6},{8,9},{9,8},{10,11... | collective-permute-start | bytes 4718600 | tf_op jit(solution)/shard_map/ppermute | solution.py:237
  72.9 9.7 %collective-permute-start.2 = (bf16[128,3072]{1,0:T(8,128)(2,1)}, bf16[128,3072]{1,0:T(8,128)(2,1)}, u32[]{:S(2)}, u32[]{:S(2)}) collective-permute-start(bf16[128,3072]{1,0:T(8,128)(2,1)} %collective-permute-done), channel_id=1, source_target_pairs={{8,16},{12,20},{16,24},{20,28},{9,17},{13,21},{17,25},{21,29},{10,... | collective-permute-start | bytes 2359304 | tf_op jit(solution)/shard_map/ppermute | solution.py:237
  74.4 38.3 %collective-permute-start.3 = (bf16[128,3072]{1,0:T(8,128)(2,1)}, bf16[128,3072]{1,0:T(8,128)(2,1)}, u32[]{:S(2)}, u32[]{:S(2)}) collective-permute-start(bf16[128,3072]{1,0:T(8,128)(2,1)} %collective-permute-done.1), channel_id=1, source_target_pairs={{8,0},{12,4},{16,8},{20,12},{9,1},{13,5},{17,9},{21,13},{10,2},{14... | collective-permute-start | bytes 2359304 | tf_op jit(solution)/shard_map/ppermute | solution.py:237
  81.9 0.7 copy-start.8
  112.7 66.7 %all-to-all-start.2 = ((bf16[8,256,384]{2,1,0:T(8,128)(2,1)}), bf16[8,256,384]{2,1,0:T(8,128)(2,1)}, u32[]{:S(2)}, u32[]{:S(2)}) async-start(bf16[8,256,384]{2,1,0:T(8,128)(2,1)} %get-tuple-element.88), calls=%async_computation.2 | async-start | bytes 3145728 | tf_op jit(solution)/shard_map/all_to_all | solution.py:225
  123.9 37.9 %collective-permute-start.10 = (bf16[256,3072]{1,0:T(8,128)(2,1)}, bf16[256,3072]{1,0:T(8,128)(2,1)S(1)}, u32[]{:S(2)}, u32[]{:S(2)}) collective-permute-start(bf16[256,3072]{1,0:T(8,128)(2,1)} %pad_maximum_fusion.refs_6_), channel_id=1, source_target_pairs={{0,3},{1,2},{2,1},{3,0},{4,7},{5,6},{6,5},{7,4},{8,11},{9,10},{10,... | collective-permute-start | bytes 4718600 | tf_op jit(solution)/shard_map/ppermute | solution.py:237
  128.8 50.7 %collective-permute-start.6 = (bf16[128,3072]{1,0:T(8,128)(2,1)S(1)}, bf16[128,3072]{1,0:T(8,128)(2,1)}, u32[]{:S(2)}, u32[]{:S(2)}) collective-permute-start(bf16[128,3072]{1,0:T(8,128)(2,1)S(1)} %get-tuple-element.140), channel_id=1, source_target_pairs={{8,0},{12,4},{16,24},{20,28},{9,1},{13,5},{17,25},{21,29},{10,2},{... | collective-permute-start | bytes 2359304 | tf_op jit(solution)/shard_map/ppermute | solution.py:237
  130.0 48.1 %collective-permute-start.7 = (bf16[512,128]{1,0:T(8,128)(2,1)}, bf16[512,128]{1,0:T(8,128)(2,1)S(1)}, u32[]{:S(2)}, u32[]{:S(2)}) collective-permute-start(bf16[512,128]{1,0:T(8,128)(2,1)} %get-tuple-element.90), channel_id=1, source_target_pairs={{0,8},{4,12},{8,0},{12,4},{16,24},{20,28},{24,16},{28,20},{1,9},{5... | collective-permute-start | bytes 393224 | tf_op jit(solution)/shard_map/ppermute | solution.py:237
  133.9 44.2 %collective-permute-start.8 = (bf16[512,128]{1,0:T(8,128)(2,1)}, bf16[512,128]{1,0:T(8,128)(2,1)S(1)}, u32[]{:S(2)}, u32[]{:S(2)}) collective-permute-start(bf16[512,128]{1,0:T(8,128)(2,1)} %get-tuple-element.91), channel_id=1, source_target_pairs={{0,16},{4,20},{8,24},{12,28},{16,0},{20,4},{24,8},{28,12},{1,17},{... | collective-permute-start | bytes 393224 | tf_op jit(solution)/shard_map/ppermute | solution.py:237
  135.9 42.2 %collective-permute-start.9 = (bf16[512,128]{1,0:T(8,128)(2,1)S(1)}, bf16[512,128]{1,0:T(8,128)(2,1)S(1)}, u32[]{:S(2)}, u32[]{:S(2)}) collective-permute-start(bf16[512,128]{1,0:T(8,128)(2,1)S(1)} %get-tuple-element.92), channel_id=1, source_target_pairs={{0,24},{4,28},{8,16},{12,20},{16,8},{20,12},{24,0},{28,4},{1,25},{... | collective-permute-start | bytes 393224 | tf_op jit(solution)/shard_map/ppermute | solution.py:237
  178.1 0.6 copy-start.19
  178.1 0.7 copy-start.21
  178.8 0.6 copy-start.23
  179.5 51.1 %all-to-all-start.3 = ((bf16[8,256,384]{2,1,0:T(8,128)(2,1)}), bf16[8,256,384]{2,1,0:T(8,128)(2,1)S(1)}, u32[]{:S(2)}, u32[]{:S(2)}) async-start(bf16[8,256,384]{2,1,0:T(8,128)(2,1)} %get-tuple-element.98), calls=%async_computation.3 | async-start | bytes 3145728 | tf_op jit(solution)/shard_map/all_to_all | solution.py:225
  183.2 1.6 copy-start.14
  185.0 37.8 %copy-start.1 = (bf16[256,3072]{1,0:T(8,128)(2,1)}, bf16[256,3072]{1,0:T(8,128)(2,1)S(1)}, u32[]{:S(2)}) copy-start(bf16[256,3072]{1,0:T(8,128)(2,1)S(1)} %pad_maximum_fusion.1.refs_9_) | copy-start | bytes 4718596
  185.0 14.3 %copy-start.9 = (bf16[512,128]{1,0:T(8,128)(2,1)S(1)}, bf16[512,128]{1,0:T(8,128)(2,1)}, u32[]{:S(2)}) copy-start(bf16[512,128]{1,0:T(8,128)(2,1)} %copy-done.8) | copy-start | bytes 393220
  185.0 14.3 %copy-start.20 = (bf16[512,128]{1,0:T(8,128)(2,1)S(1)}, bf16[512,128]{1,0:T(8,128)(2,1)}, u32[]{:S(2)}) copy-start(bf16[512,128]{1,0:T(8,128)(2,1)} %copy-done.19) | copy-start | bytes 393220
  185.0 14.3 %copy-start.22 = (bf16[512,128]{1,0:T(8,128)(2,1)S(1)}, bf16[512,128]{1,0:T(8,128)(2,1)}, u32[]{:S(2)}) copy-start(bf16[512,128]{1,0:T(8,128)(2,1)} %copy-done.21) | copy-start | bytes 393220
  185.0 14.3 %copy-start.24 = (bf16[512,128]{1,0:T(8,128)(2,1)S(1)}, bf16[512,128]{1,0:T(8,128)(2,1)}, u32[]{:S(2)}) copy-start(bf16[512,128]{1,0:T(8,128)(2,1)} %copy-done.23) | copy-start | bytes 393220
  185.0 36.8 %collective-permute-start.12 = (bf16[256,3072]{1,0:T(8,128)(2,1)S(1)}, bf16[256,3072]{1,0:T(8,128)(2,1)S(1)}, u32[]{:S(2)}, u32[]{:S(2)}) collective-permute-start(bf16[256,3072]{1,0:T(8,128)(2,1)S(1)} %pad_maximum_fusion.1.refs_9_), channel_id=1, source_target_pairs={{0,2},{1,3},{2,0},{3,1},{4,6},{5,7},{6,4},{7,5},{8,10},{9,11},{10,... | collective-permute-start | bytes 4718600 | tf_op jit(solution)/shard_map/ppermute | solution.py:237
  186.6 36.4 %collective-permute-start.11 = (bf16[256,3072]{1,0:T(8,128)(2,1)S(1)}, bf16[256,3072]{1,0:T(8,128)(2,1)S(1)}, u32[]{:S(2)}, u32[]{:S(2)}) collective-permute-start(bf16[256,3072]{1,0:T(8,128)(2,1)S(1)} %pad_maximum_fusion.1.refs_9_), channel_id=1, source_target_pairs={{0,1},{1,0},{2,3},{3,2},{4,5},{5,4},{6,7},{7,6},{8,9},{9,8},{10,11... | collective-permute-start | bytes 4718600 | tf_op jit(solution)/shard_map/ppermute | solution.py:237
  188.1 35.9 %collective-permute-start.13 = (bf16[512,128]{1,0:T(8,128)(2,1)}, bf16[512,128]{1,0:T(8,128)(2,1)S(1)}, u32[]{:S(2)}, u32[]{:S(2)}) collective-permute-start(bf16[512,128]{1,0:T(8,128)(2,1)} %get-tuple-element.95), channel_id=1, source_target_pairs={{0,8},{4,12},{8,0},{12,4},{16,24},{20,28},{24,16},{28,20},{1,9},{5... | collective-permute-start | bytes 393224 | tf_op jit(solution)/shard_map/ppermute | solution.py:237
  189.8 40.1 %collective-permute-start.14 = (bf16[512,128]{1,0:T(8,128)(2,1)}, bf16[512,128]{1,0:T(8,128)(2,1)S(1)}, u32[]{:S(2)}, u32[]{:S(2)}) collective-permute-start(bf16[512,128]{1,0:T(8,128)(2,1)} %get-tuple-element.96), channel_id=1, source_target_pairs={{0,16},{4,20},{8,24},{12,28},{16,0},{20,4},{24,8},{28,12},{1,17},{... | collective-permute-start | bytes 393224 | tf_op jit(solution)/shard_map/ppermute | solution.py:237
  192.4 38.2 %collective-permute-start.15 = (bf16[512,128]{1,0:T(8,128)(2,1)}, bf16[512,128]{1,0:T(8,128)(2,1)}, u32[]{:S(2)}, u32[]{:S(2)}) collective-permute-start(bf16[512,128]{1,0:T(8,128)(2,1)} %get-tuple-element.97), channel_id=1, source_target_pairs={{0,24},{4,28},{8,16},{12,20},{16,8},{20,12},{24,0},{28,4},{1,25},{... | collective-permute-start | bytes 393224 | tf_op jit(solution)/shard_map/ppermute | solution.py:237
  199.3 30.5 %copy-start.11 = (bf16[512,128]{1,0:T(8,128)(2,1)}, bf16[512,128]{1,0:T(8,128)(2,1)S(1)}, u32[]{:S(2)}) copy-start(bf16[512,128]{1,0:T(8,128)(2,1)S(1)} %get-tuple-element.111) | copy-start | bytes 393220
  199.4 30.5 %copy-start.12 = (bf16[512,128]{1,0:T(8,128)(2,1)}, bf16[512,128]{1,0:T(8,128)(2,1)S(1)}, u32[]{:S(2)}) copy-start(bf16[512,128]{1,0:T(8,128)(2,1)S(1)} %get-tuple-element.110) | copy-start | bytes 393220
  199.4 30.5 %copy-start.13 = (bf16[512,128]{1,0:T(8,128)(2,1)}, bf16[512,128]{1,0:T(8,128)(2,1)S(1)}, u32[]{:S(2)}) copy-start(bf16[512,128]{1,0:T(8,128)(2,1)S(1)} %get-tuple-element.109) | copy-start | bytes 393220
  221.8 2.2 copy-start.3
  223.0 6.9 %copy-start.5 = (bf16[256,3072]{1,0:T(8,128)(2,1)}, bf16[256,3072]{1,0:T(8,128)(2,1)S(1)}, u32[]{:S(2)}) copy-start(bf16[256,3072]{1,0:T(8,128)(2,1)S(1)} %collective-permute-done.11.refs_10_) | copy-start | bytes 4718596
  224.0 5.9 %copy-start.17 = (bf16[512,128]{1,0:T(8,128)(2,1)}, bf16[512,128]{1,0:T(8,128)(2,1)S(1)}, u32[]{:S(2)}) copy-start(bf16[512,128]{1,0:T(8,128)(2,1)S(1)} %collective-permute-done.13) | copy-start | bytes 393220
  229.9 0.6 copy-start.18
  230.6 23.2 %copy-start.2 = (bf16[256,3072]{1,0:T(8,128)(2,1)S(1)}, bf16[256,3072]{1,0:T(8,128)(2,1)}, u32[]{:S(2)}) copy-start(bf16[256,3072]{1,0:T(8,128)(2,1)} %copy-done.1) | copy-start | bytes 4718596
  230.6 23.2 %copy-start.7 = (bf16[512,512]{1,0:T(8,128)(2,1)S(1)}, bf16[512,512]{1,0:T(8,128)(2,1)}, u32[]{:S(2)}) copy-start(bf16[512,512]{1,0:T(8,128)(2,1)} %pad_maximum_fusion.2.refs_0_) | copy-start | bytes 1572868
  230.6 33.7 %collective-permute-start.22 = (bf16[128,3072]{1,0:T(8,128)(2,1)}, bf16[128,3072]{1,0:T(8,128)(2,1)S(1)}, u32[]{:S(2)}, u32[]{:S(2)}) collective-permute-start(bf16[128,3072]{1,0:T(8,128)(2,1)} %slice.8), channel_id=1, source_target_pairs={{0,2},{1,3},{2,0},{3,1},{4,6},{5,7},{6,4},{7,5},{8,10},{9,11},{10,... | collective-permute-start | bytes 2359304 | tf_op jit(solution)/shard_map/ppermute | solution.py:237
  232.2 32.1 %collective-permute-start.23 = (bf16[128,3072]{1,0:T(8,128)(2,1)}, bf16[128,3072]{1,0:T(8,128)(2,1)S(1)}, u32[]{:S(2)}, u32[]{:S(2)}) collective-permute-start(bf16[128,3072]{1,0:T(8,128)(2,1)} %slice.9), channel_id=1, source_target_pairs={{0,1},{1,0},{2,3},{3,2},{4,5},{5,4},{6,7},{7,6},{8,9},{9,8},{10,11... | collective-permute-start | bytes 2359304 | tf_op jit(solution)/shard_map/ppermute | solution.py:237
  233.7 10.3 %collective-permute-start.16 = (bf16[512,128]{1,0:T(8,128)(2,1)}, bf16[512,128]{1,0:T(8,128)(2,1)S(1)}, u32[]{:S(2)}, u32[]{:S(2)}) collective-permute-start(bf16[512,128]{1,0:T(8,128)(2,1)} %copy-done.13), channel_id=1, source_target_pairs={{0,8},{4,12},{8,0},{12,4},{16,24},{20,28},{24,16},{28,20},{1,9},{5... | collective-permute-start | bytes 393224 | tf_op jit(solution)/shard_map/ppermute | solution.py:237
  236.0 12.2 %collective-permute-start.17 = (bf16[512,128]{1,0:T(8,128)(2,1)}, bf16[512,128]{1,0:T(8,128)(2,1)S(1)}, u32[]{:S(2)}, u32[]{:S(2)}) collective-permute-start(bf16[512,128]{1,0:T(8,128)(2,1)} %copy-done.12), channel_id=1, source_target_pairs={{0,16},{4,20},{8,24},{12,28},{16,0},{20,4},{24,8},{28,12},{1,17},{... | collective-permute-start | bytes 393224 | tf_op jit(solution)/shard_map/ppermute | solution.py:237
  236.0 12.2 %collective-permute-start.18 = (bf16[512,128]{1,0:T(8,128)(2,1)}, bf16[512,128]{1,0:T(8,128)(2,1)S(1)}, u32[]{:S(2)}, u32[]{:S(2)}) collective-permute-start(bf16[512,128]{1,0:T(8,128)(2,1)} %copy-done.11), channel_id=1, source_target_pairs={{0,24},{4,28},{8,16},{12,20},{16,8},{20,12},{24,0},{28,4},{1,25},{... | collective-permute-start | bytes 393224 | tf_op jit(solution)/shard_map/ppermute | solution.py:237
  248.2 16.0 %collective-permute-start.19 = (bf16[512,128]{1,0:T(8,128)(2,1)S(1)}, bf16[512,128]{1,0:T(8,128)(2,1)S(1)}, u32[]{:S(2)}, u32[]{:S(2)}) collective-permute-start(bf16[512,128]{1,0:T(8,128)(2,1)S(1)} %get-tuple-element.118), channel_id=1, source_target_pairs={{0,8},{4,12},{8,0},{12,4},{16,24},{20,28},{24,16},{28,20},{1,9},{5... | collective-permute-start | bytes 393224 | tf_op jit(solution)/shard_map/ppermute | solution.py:237
  250.3 14.0 %collective-permute-start.20 = (bf16[512,128]{1,0:T(8,128)(2,1)S(1)}, bf16[512,128]{1,0:T(8,128)(2,1)S(1)}, u32[]{:S(2)}, u32[]{:S(2)}) collective-permute-start(bf16[512,128]{1,0:T(8,128)(2,1)S(1)} %get-tuple-element.119), channel_id=1, source_target_pairs={{0,16},{4,20},{8,24},{12,28},{16,0},{20,4},{24,8},{28,12},{1,17},{... | collective-permute-start | bytes 393224 | tf_op jit(solution)/shard_map/ppermute | solution.py:237
  250.5 13.8 %collective-permute-start.21 = (bf16[512,128]{1,0:T(8,128)(2,1)S(1)}, bf16[512,128]{1,0:T(8,128)(2,1)S(1)}, u32[]{:S(2)}, u32[]{:S(2)}) collective-permute-start(bf16[512,128]{1,0:T(8,128)(2,1)S(1)} %get-tuple-element.120), channel_id=1, source_target_pairs={{0,24},{4,28},{8,16},{12,20},{16,8},{20,12},{24,0},{28,4},{1,25},{... | collective-permute-start | bytes 393224 | tf_op jit(solution)/shard_map/ppermute | solution.py:237
  253.7 1.4 copy-start.4
  255.2 1.4 copy-start.6
  266.0 3.5 %collective-permute-start.24 = (bf16[256,3072]{1,0:T(8,128)(2,1)S(1)}, bf16[256,3072]{1,0:T(8,128)(2,1)S(1)}, u32[]{:S(2)}, u32[]{:S(2)}) collective-permute-start(bf16[256,3072]{1,0:T(8,128)(2,1)S(1)} %convert_element_type.9), channel_id=1, source_target_pairs={{0,4},{4,0},{8,12},{12,8},{16,20},{20,16},{24,28},{28,24},{1,5},{5... | collective-permute-start | bytes 4718600 | tf_op jit(solution)/shard_map/ppermute | solution.py:237

commit v6 on v5

--- a/solution.py
+++ b/solution.py
@@ -280,7 +280,7 @@
     back2 = send_back(out2)
     out3 = attend_step(qkv3, 3)
     far_corner = [along(halves[0], "fsdp", xor(2, 4)), along(halves[1], "fsdp", xor(1, 4))]
-    back2, out3 = fence(back2, out3)
+    back2, out3, joined1 = fence(back2, out3, joined1)
     back3 = send_back(out3)
 
     sides_all = [near] + near_sides + [far] + far_sides

time: 272 us -> 271 us (level)
  no operation moved by 1% of the time
where the time goes in v6:
time: 271 us; the launch traced here: 270 us
  waiting for transfers between devices  130 us (48%)
  starting transfers between devices  75.4 us (28%)
  Pallas kernels  45.7 us (17%)
  other arithmetic  11 us (4%)
  local copies, waits for them, and re-layouts  7.91 us (3%)
    ppermute x25, waiting for transfers between devices, along(): return lax.ppermute(value, axis, pairs)  130 us
    ppermute x25, starting transfers between devices, along(): return lax.ppermute(value, axis, pairs)  42.7 us
    all_to_all x4, starting transfers between devices, exchange(): return lax.all_to_all(x, 'seq', split_axis=0, concat_axis=0, tiled=True)  32.7 us
    pallas_call x4, Pallas kernels, attend(): pl.pallas_call(functools.partial(attend_kernel, step, at_lane, width, slo...  25.4 us
    pallas_call x3, Pallas kernels, project(): pl.pallas_call(functools.partial(project_kernel, terms, len(rows), len(bl...  10.7 us
    pallas_call x2, Pallas kernels, lay_out(): pl.pallas_call(functools.partial(layout_kernel, steps, here, width), out_...  9.52 us
    unnamed x52, local copies, waits for them, and re-layouts  5.6 us
  transfers between devices with their start and end apart: 29, of which 10 were waited for; matrix products, arithmetic and copies ran while one was open for 4% of the time, Pallas kernels for 15%

profile of v6, /device:TPU:0, one launch (start us, length us, event | category | flops | bytes accessed | tf_op | source)
XLA Modules:
  0.0 270.0 jit_solution(6580676958336024143)
XLA Ops:
  0.0 0.6 pad_add_fusion.place_ref
  0.6 3.5 %shard_map.64.refs_3_ = bf16[8,256,384]{2,1,0:T(8,128)(2,1)} custom-call(s32[2]{0:T(128)} %pad_add_fusion.place_ref, bf16[256,4096]{1,0:T(8,128)(2,1)} %bitcast.14, bf16[256,4096]{1,0:T(8,128)(2,1)} %bitcast.16, bf16[256,4096]{1,0:T(8,128)(2,1)} %bitcast.18), custom_call_target="tpu_custom_call" | custom-call | flops 1 | bytes 1 | tf_op jit(solution)/shard_map/pallas_call | solution.py:48
  4.1 6.5 %all-to-all-start = ((bf16[8,256,384]{2,1,0:T(8,128)(2,1)}), bf16[8,256,384]{2,1,0:T(8,128)(2,1)S(1)}, u32[]{:S(2)}, u32[]{:S(2)}) async-start(bf16[8,256,384]{2,1,0:T(8,128)(2,1)} %shard_map.64.refs_3_), calls=%async_computation | async-start | bytes 3145728 | tf_op jit(solution)/shard_map/all_to_all | solution.py:225
  10.6 4.8 %collective-permute-start = (bf16[128,3072]{1,0:T(8,128)(2,1)S(1)}, bf16[128,3072]{1,0:T(8,128)(2,1)}, u32[]{:S(2)}, u32[]{:S(2)}) collective-permute-start(bf16[128,3072]{1,0:T(8,128)(2,1)S(1)} %copy-done.15), channel_id=1, source_target_pairs={{0,8},{4,12},{8,16},{12,20},{16,24},{20,28},{1,9},{5,13},{9,17},{1... | collective-permute-start | bytes 2359304 | tf_op jit(solution)/shard_map/ppermute | solution.py:237
  15.4 1.3 collective-permute-start.1
  16.7 6.1 %shard_map.65 = (bf16[8,256,384]{2,1,0:T(8,128)(2,1)}, bf16[8,256,384]{2,1,0:T(8,128)(2,1)}, bf16[8,256,384]{2,1,0:T(8,128)(2,1)}) custom-call(s32[2]{0:T(128)} %pad_add_fusion.place_ref, bf16[256,4096]{1,0:T(8,128)(2,1)} %bitcast.15, bf16[256,4096]{1,0:T(8,128)(2,1)} %bitcast.17, bf16[256,4096]{1,0:T(8,128)(2,1)} %bitcast.19, ...), custom_call_target="tpu_custom_call" | custom-call | flops 1 | bytes 1 | tf_op jit(solution)/shard_map/pallas_call | solution.py:48
  22.7 31.1 %collective-permute-done = bf16[128,3072]{1,0:T(8,128)(2,1)} collective-permute-done((bf16[128,3072]{1,0:T(8,128)(2,1)S(1)}, bf16[128,3072]{1,0:T(8,128)(2,1)}, u32[]{:S(2)}, u32[]{:S(2)}) %collective-permute-start) | collective-permute-done | bytes 786464 | tf_op jit(solution)/shard_map/ppermute | solution.py:237
  53.9 2.2 collective-permute-done.1
  56.0 11.2 %all-to-all-start.1 = ((bf16[8,256,384]{2,1,0:T(8,128)(2,1)}), bf16[8,256,384]{2,1,0:T(8,128)(2,1)S(1)}, u32[]{:S(2)}, u32[]{:S(2)}) async-start(bf16[8,256,384]{2,1,0:T(8,128)(2,1)} %get-tuple-element.79), calls=%async_computation.1 | async-start | bytes 3145728 | tf_op jit(solution)/shard_map/all_to_all | solution.py:225
  67.3 1.3 broadcast_select_fusion.1
  68.6 1.2 pad_maximum_fusion.refs_6_
  69.9 1.5 collective-permute-start.4
  71.4 1.5 collective-permute-start.5
  72.9 1.5 collective-permute-start.2
  74.4 1.3 collective-permute-start.3
  76.0 6.6 %shard_map.66 = (bf16[512,128]{1,0:T(8,128)(2,1)S(1)}, bf16[512,128]{1,0:T(8,128)(2,1)}, bf16[512,128]{1,0:T(8,128)(2,1)}, bf16[512,128]{1,0:T(8,128)(2,1)S(1)}) custom-call(s32[2]{0:T(128)S(1)} %copy-done.10, s32[4,128]{1,0:T(4,128)S(1)} %copy.11.lists_ref, s32[4,16]{1,0:T(4,128)S(1)} %bitcast.10, bf16[8,256,384]{2,1,0:T(8,128)(2,1)S(1)} %all-to-all-done.refs_0_), custom_call_target="tpu_custom_call" | custom-call | flops 1 | bytes 1 | tf_op jit(solution)/shard_map/pallas_call | solution.py:128
  82.7 0.7 copy-done.8
  83.3 29.4 %collective-permute-done.3 = bf16[128,3072]{1,0:T(8,128)(2,1)} collective-permute-done((bf16[128,3072]{1,0:T(8,128)(2,1)}, bf16[128,3072]{1,0:T(8,128)(2,1)}, u32[]{:S(2)}, u32[]{:S(2)}) %collective-permute-start.3) | collective-permute-done | bytes 786464 | tf_op jit(solution)/shard_map/ppermute | solution.py:237
  112.7 11.2 %all-to-all-start.2 = ((bf16[8,256,384]{2,1,0:T(8,128)(2,1)}), bf16[8,256,384]{2,1,0:T(8,128)(2,1)}, u32[]{:S(2)}, u32[]{:S(2)}) async-start(bf16[8,256,384]{2,1,0:T(8,128)(2,1)} %get-tuple-element.89), calls=%async_computation.2 | async-start | bytes 3145728 | tf_op jit(solution)/shard_map/all_to_all | solution.py:225
  123.9 2.4 collective-permute-start.10
  126.4 2.4 broadcast_select_fusion
  128.8 1.3 collective-permute-start.6
  130.0 3.9 %collective-permute-start.7 = (bf16[512,128]{1,0:T(8,128)(2,1)}, bf16[512,128]{1,0:T(8,128)(2,1)S(1)}, u32[]{:S(2)}, u32[]{:S(2)}) collective-permute-start(bf16[512,128]{1,0:T(8,128)(2,1)} %get-tuple-element.91), channel_id=1, source_target_pairs={{0,8},{4,12},{8,0},{12,4},{16,24},{20,28},{24,16},{28,20},{1,9},{5... | collective-permute-start | bytes 393224 | tf_op jit(solution)/shard_map/ppermute | solution.py:237
  133.9 2.0 collective-permute-start.8
  135.9 1.5 collective-permute-start.9
  137.4 6.0 %shard_map.67 = (bf16[512,128]{1,0:T(8,128)(2,1)S(1)}, bf16[512,128]{1,0:T(8,128)(2,1)}, bf16[512,128]{1,0:T(8,128)(2,1)}, bf16[512,128]{1,0:T(8,128)(2,1)}) custom-call(s32[2]{0:T(128)S(1)} %copy-done.10, s32[4,128]{1,0:T(4,128)S(1)} %copy.11.lists_ref, s32[4,16]{1,0:T(4,128)S(1)} %bitcast.11, bf16[8,256,384]{2,1,0:T(8,128)(2,1)S(1)} %all-to-all-done.1.refs_0_), custom_call_target="tpu_custom_call" | custom-call | flops 1 | bytes 1 | tf_op jit(solution)/shard_map/pallas_call | solution.py:128
  143.4 18.5 %collective-permute-done.10.refs_4_ = bf16[256,3072]{1,0:T(8,128)(2,1)S(1)} collective-permute-done((bf16[256,3072]{1,0:T(8,128)(2,1)}, bf16[256,3072]{1,0:T(8,128)(2,1)S(1)}, u32[]{:S(2)}, u32[]{:S(2)}) %collective-permute-start.10) | collective-permute-done | bytes 1572896 | tf_op jit(solution)/shard_map/ppermute | solution.py:237
  161.9 16.3 %collective-permute-done.7 = bf16[512,128]{1,0:T(8,128)(2,1)S(1)} collective-permute-done((bf16[512,128]{1,0:T(8,128)(2,1)}, bf16[512,128]{1,0:T(8,128)(2,1)S(1)}, u32[]{:S(2)}, u32[]{:S(2)}) %collective-permute-start.7) | collective-permute-done | bytes 131104 | tf_op jit(solution)/shard_map/ppermute | solution.py:237
  178.1 0.6 copy-done.17
  178.8 0.6 copy-done.21
  179.5 3.8 %all-to-all-start.3 = ((bf16[8,256,384]{2,1,0:T(8,128)(2,1)}), bf16[8,256,384]{2,1,0:T(8,128)(2,1)S(1)}, u32[]{:S(2)}, u32[]{:S(2)}) async-start(bf16[8,256,384]{2,1,0:T(8,128)(2,1)} %get-tuple-element.99), calls=%async_computation.3 | async-start | bytes 3145728 | tf_op jit(solution)/shard_map/all_to_all | solution.py:225
  183.3 1.6 select_select_fusion
  184.8 0.1 pad_maximum_fusion.1.refs_9_
  185.0 1.6 collective-permute-start.11
  186.6 1.5 collective-permute-start.12
  188.1 1.6 collective-permute-start.13
  189.8 2.6 collective-permute-start.14
  192.4 0.1 collective-permute-start.15
  192.5 6.4 %shard_map.68 = (bf16[512,128]{1,0:T(8,128)(2,1)S(1)}, bf16[512,128]{1,0:T(8,128)(2,1)S(1)}, bf16[512,128]{1,0:T(8,128)(2,1)S(1)}, bf16[512,128]{1,0:T(8,128)(2,1)S(1)}) custom-call(s32[2]{0:T(128)S(1)} %copy-done.10, s32[4,128]{1,0:T(4,128)S(1)} %copy.11.lists_ref, s32[4,16]{1,0:T(4,128)S(1)} %bitcast.12, bf16[8,256,384]{2,1,0:T(8,128)(2,1)} %all-to-all-done.2.refs_0_), custom_call_target="tpu_custom_call" | custom-call | flops 1 | bytes 1 | tf_op jit(solution)/shard_map/pallas_call | solution.py:128
  199.0 0.9 pad_maximum_fusion.2.refs_0_
  199.9 21.9 %collective-permute-done.11.refs_10_ = bf16[256,3072]{1,0:T(8,128)(2,1)S(1)} collective-permute-done((bf16[256,3072]{1,0:T(8,128)(2,1)S(1)}, bf16[256,3072]{1,0:T(8,128)(2,1)S(1)}, u32[]{:S(2)}, u32[]{:S(2)}) %collective-permute-start.11) | collective-permute-done | bytes 1572896 | tf_op jit(solution)/shard_map/ppermute | solution.py:237
  221.8 1.0 slice.8
  222.8 0.2 collective-permute-done.12.refs_11_
  223.0 1.0 slice.9
  224.0 5.9 %collective-permute-done.14 = bf16[512,128]{1,0:T(8,128)(2,1)S(1)} collective-permute-done((bf16[512,128]{1,0:T(8,128)(2,1)}, bf16[512,128]{1,0:T(8,128)(2,1)S(1)}, u32[]{:S(2)}, u32[]{:S(2)}) %collective-permute-start.14) | collective-permute-done | bytes 131104 | tf_op jit(solution)/shard_map/ppermute | solution.py:237
  229.9 0.6 copy-done.24
  230.6 1.6 collective-permute-start.22
  232.2 1.5 collective-permute-start.23
  233.7 2.3 collective-permute-start.16
  236.0 2.4 collective-permute-start.18
  238.3 6.4 %shard_map.69 = (bf16[512,128]{1,0:T(8,128)(2,1)S(1)}, bf16[512,128]{1,0:T(8,128)(2,1)S(1)}, bf16[512,128]{1,0:T(8,128)(2,1)S(1)}, bf16[512,128]{1,0:T(8,128)(2,1)S(1)}) custom-call(s32[2]{0:T(128)S(1)} %copy-done.10, s32[4,128]{1,0:T(4,128)S(1)} %copy.11.lists_ref, s32[4,16]{1,0:T(4,128)S(1)} %bitcast.13, bf16[8,256,384]{2,1,0:T(8,128)(2,1)S(1)} %all-to-all-done.3.refs_0_), custom_call_target="tpu_custom_call" | custom-call | flops 1 | bytes 1 | tf_op jit(solution)/shard_map/pallas_call | solution.py:128
  244.7 1.1 pad_maximum_fusion.3.refs_1_
  245.8 2.4 collective-permute-done.17.refs_4_
  248.2 2.1 collective-permute-start.19
  250.3 0.2 collective-permute-start.20
  250.5 2.2 collective-permute-start.21
  252.6 1.4 copy-done.4
  254.1 1.4 copy-done.6
  255.5 7.7 %shard_map.70 = (f32[256,3072]{1,0:T(8,128)S(1)}, f32[256,3072]{1,0:T(8,128)S(1)}) custom-call(bf16[512,512]{1,0:T(8,128)(2,1)S(1)} %copy-done.7, bf16[512,512]{1,0:T(8,128)(2,1)S(1)} %pad_maximum_fusion.3.refs_1_, bf16[512,128]{1,0:T(8,128)(2,1)S(1)} %get-tuple-element.131.refs_2_, bf16[512,128]{1,0:T(8,128)(2,1)S(1)} %collective-permute-done.16.refs_3_, ...), custom_call_target="tpu_custom_call" | custom-call | flops 1 | bytes 1 | tf_op jit(solution)/shard_map/pallas_call | solution.py:192
  263.2 1.5 shard_map.72
  264.7 0.2 convert_element_type.9
  265.0 1.5 shard_map.71
  266.6 1.9 collective-permute-done.24
  268.4 1.6 fusion
  (71 shorter events, 0.7 us)
Async XLA Ops:
  0.0 75.7 %copy-start = (s32[1,32,16,8]{1,3,2,0:T(8,128)S(1)}, s32[1,32,16,8]{1,3,2,0:T(8,128)}, u32[]{:S(2)}) copy-start(s32[1,32,16,8]{1,3,2,0:T(8,128)} %param.10) | copy-start | bytes 49156
  4.1 6.5 %copy-start.15 = (bf16[128,3072]{1,0:T(8,128)(2,1)S(1)}, bf16[128,3072]{1,0:T(8,128)(2,1)}, u32[]{:S(2)}) copy-start(bf16[128,3072]{1,0:T(8,128)(2,1)} %param.9) | copy-start | bytes 2359300
  4.1 51.9 %all-to-all-start = ((bf16[8,256,384]{2,1,0:T(8,128)(2,1)}), bf16[8,256,384]{2,1,0:T(8,128)(2,1)S(1)}, u32[]{:S(2)}, u32[]{:S(2)}) async-start(bf16[8,256,384]{2,1,0:T(8,128)(2,1)} %shard_map.64.refs_3_), calls=%async_computation | async-start | bytes 3145728 | tf_op jit(solution)/shard_map/all_to_all | solution.py:225
  10.6 43.3 %collective-permute-start = (bf16[128,3072]{1,0:T(8,128)(2,1)S(1)}, bf16[128,3072]{1,0:T(8,128)(2,1)}, u32[]{:S(2)}, u32[]{:S(2)}) collective-permute-start(bf16[128,3072]{1,0:T(8,128)(2,1)S(1)} %copy-done.15), channel_id=1, source_target_pairs={{0,8},{4,12},{8,16},{12,20},{16,24},{20,28},{1,9},{5,13},{9,17},{1... | collective-permute-start | bytes 2359304 | tf_op jit(solution)/shard_map/ppermute | solution.py:237
  15.4 40.6 %collective-permute-start.1 = (bf16[128,3072]{1,0:T(8,128)(2,1)S(1)}, bf16[128,3072]{1,0:T(8,128)(2,1)}, u32[]{:S(2)}, u32[]{:S(2)}) collective-permute-start(bf16[128,3072]{1,0:T(8,128)(2,1)S(1)} %copy-done.15), channel_id=1, source_target_pairs={{8,0},{12,4},{16,8},{20,12},{24,16},{28,20},{9,1},{13,5},{17,9},{2... | collective-permute-start | bytes 2359304 | tf_op jit(solution)/shard_map/ppermute | solution.py:237
  56.0 56.7 %all-to-all-start.1 = ((bf16[8,256,384]{2,1,0:T(8,128)(2,1)}), bf16[8,256,384]{2,1,0:T(8,128)(2,1)S(1)}, u32[]{:S(2)}, u32[]{:S(2)}) async-start(bf16[8,256,384]{2,1,0:T(8,128)(2,1)} %get-tuple-element.79), calls=%async_computation.1 | async-start | bytes 3145728 | tf_op jit(solution)/shard_map/all_to_all | solution.py:225
  67.2 1.4 copy-start.16
  68.6 7.2 %copy-start.25 = (s32[1,32,16]{1,2,0:T(8,128)S(1)}, s32[1,32,16]{1,2,0:T(8,128)}, u32[]{:S(2)}) copy-start(s32[1,32,16]{1,2,0:T(8,128)} %param.11) | copy-start | bytes 6148
  68.6 7.4 %copy-start.10 = (s32[2]{0:T(128)S(1)}, s32[2]{0:T(128)}, u32[]{:S(2)}) copy-start(s32[2]{0:T(128)} %pad_add_fusion.place_ref) | copy-start | bytes 28
  69.9 42.8 %collective-permute-start.4 = (bf16[256,3072]{1,0:T(8,128)(2,1)}, bf16[256,3072]{1,0:T(8,128)(2,1)}, u32[]{:S(2)}, u32[]{:S(2)}) collective-permute-start(bf16[256,3072]{1,0:T(8,128)(2,1)} %pad_maximum_fusion.refs_6_), channel_id=1, source_target_pairs={{0,1},{1,0},{2,3},{3,2},{4,5},{5,4},{6,7},{7,6},{8,9},{9,8},{10,11... | collective-permute-start | bytes 4718600 | tf_op jit(solution)/shard_map/ppermute | solution.py:237
  71.4 41.4 %collective-permute-start.5 = (bf16[256,3072]{1,0:T(8,128)(2,1)}, bf16[256,3072]{1,0:T(8,128)(2,1)}, u32[]{:S(2)}, u32[]{:S(2)}) collective-permute-start(bf16[256,3072]{1,0:T(8,128)(2,1)} %pad_maximum_fusion.refs_6_), channel_id=1, source_target_pairs={{0,2},{1,3},{2,0},{3,1},{4,6},{5,7},{6,4},{7,5},{8,10},{9,11},{10,... | collective-permute-start | bytes 4718600 | tf_op jit(solution)/shard_map/ppermute | solution.py:237
  72.9 10.5 %collective-permute-start.2 = (bf16[128,3072]{1,0:T(8,128)(2,1)}, bf16[128,3072]{1,0:T(8,128)(2,1)}, u32[]{:S(2)}, u32[]{:S(2)}) collective-permute-start(bf16[128,3072]{1,0:T(8,128)(2,1)} %collective-permute-done), channel_id=1, source_target_pairs={{8,16},{12,20},{16,24},{20,28},{9,17},{13,21},{17,25},{21,29},{10,... | collective-permute-start | bytes 2359304 | tf_op jit(solution)/shard_map/ppermute | solution.py:237
  74.4 38.3 %collective-permute-start.3 = (bf16[128,3072]{1,0:T(8,128)(2,1)}, bf16[128,3072]{1,0:T(8,128)(2,1)}, u32[]{:S(2)}, u32[]{:S(2)}) collective-permute-start(bf16[128,3072]{1,0:T(8,128)(2,1)} %collective-permute-done.1), channel_id=1, source_target_pairs={{8,0},{12,4},{16,8},{20,12},{9,1},{13,5},{17,9},{21,13},{10,2},{14... | collective-permute-start | bytes 2359304 | tf_op jit(solution)/shard_map/ppermute | solution.py:237
  82.7 0.7 copy-start.8
  112.7 66.7 %all-to-all-start.2 = ((bf16[8,256,384]{2,1,0:T(8,128)(2,1)}), bf16[8,256,384]{2,1,0:T(8,128)(2,1)}, u32[]{:S(2)}, u32[]{:S(2)}) async-start(bf16[8,256,384]{2,1,0:T(8,128)(2,1)} %get-tuple-element.89), calls=%async_computation.2 | async-start | bytes 3145728 | tf_op jit(solution)/shard_map/all_to_all | solution.py:225
  123.9 37.9 %collective-permute-start.10 = (bf16[256,3072]{1,0:T(8,128)(2,1)}, bf16[256,3072]{1,0:T(8,128)(2,1)S(1)}, u32[]{:S(2)}, u32[]{:S(2)}) collective-permute-start(bf16[256,3072]{1,0:T(8,128)(2,1)} %pad_maximum_fusion.refs_6_), channel_id=1, source_target_pairs={{0,3},{1,2},{2,1},{3,0},{4,7},{5,6},{6,5},{7,4},{8,11},{9,10},{10,... | collective-permute-start | bytes 4718600 | tf_op jit(solution)/shard_map/ppermute | solution.py:237
  128.8 50.7 %collective-permute-start.6 = (bf16[128,3072]{1,0:T(8,128)(2,1)S(1)}, bf16[128,3072]{1,0:T(8,128)(2,1)}, u32[]{:S(2)}, u32[]{:S(2)}) collective-permute-start(bf16[128,3072]{1,0:T(8,128)(2,1)S(1)} %get-tuple-element.142), channel_id=1, source_target_pairs={{8,0},{12,4},{16,24},{20,28},{9,1},{13,5},{17,25},{21,29},{10,2},{... | collective-permute-start | bytes 2359304 | tf_op jit(solution)/shard_map/ppermute | solution.py:237
  130.0 48.1 %collective-permute-start.7 = (bf16[512,128]{1,0:T(8,128)(2,1)}, bf16[512,128]{1,0:T(8,128)(2,1)S(1)}, u32[]{:S(2)}, u32[]{:S(2)}) collective-permute-start(bf16[512,128]{1,0:T(8,128)(2,1)} %get-tuple-element.91), channel_id=1, source_target_pairs={{0,8},{4,12},{8,0},{12,4},{16,24},{20,28},{24,16},{28,20},{1,9},{5... | collective-permute-start | bytes 393224 | tf_op jit(solution)/shard_map/ppermute | solution.py:237
  133.9 44.2 %collective-permute-start.8 = (bf16[512,128]{1,0:T(8,128)(2,1)}, bf16[512,128]{1,0:T(8,128)(2,1)S(1)}, u32[]{:S(2)}, u32[]{:S(2)}) collective-permute-start(bf16[512,128]{1,0:T(8,128)(2,1)} %get-tuple-element.92), channel_id=1, source_target_pairs={{0,16},{4,20},{8,24},{12,28},{16,0},{20,4},{24,8},{28,12},{1,17},{... | collective-permute-start | bytes 393224 | tf_op jit(solution)/shard_map/ppermute | solution.py:237
  135.9 42.2 %collective-permute-start.9 = (bf16[512,128]{1,0:T(8,128)(2,1)S(1)}, bf16[512,128]{1,0:T(8,128)(2,1)S(1)}, u32[]{:S(2)}, u32[]{:S(2)}) collective-permute-start(bf16[512,128]{1,0:T(8,128)(2,1)S(1)} %get-tuple-element.93), channel_id=1, source_target_pairs={{0,24},{4,28},{8,16},{12,20},{16,8},{20,12},{24,0},{28,4},{1,25},{... | collective-permute-start | bytes 393224 | tf_op jit(solution)/shard_map/ppermute | solution.py:237
  178.1 0.6 copy-start.17
  178.1 0.7 copy-start.19
  178.8 0.6 copy-start.21
  179.5 51.1 %all-to-all-start.3 = ((bf16[8,256,384]{2,1,0:T(8,128)(2,1)}), bf16[8,256,384]{2,1,0:T(8,128)(2,1)S(1)}, u32[]{:S(2)}, u32[]{:S(2)}) async-start(bf16[8,256,384]{2,1,0:T(8,128)(2,1)} %get-tuple-element.99), calls=%async_computation.3 | async-start | bytes 3145728 | tf_op jit(solution)/shard_map/all_to_all | solution.py:225
  183.2 1.6 copy-start.14
  185.0 37.8 %copy-start.1 = (bf16[256,3072]{1,0:T(8,128)(2,1)}, bf16[256,3072]{1,0:T(8,128)(2,1)S(1)}, u32[]{:S(2)}) copy-start(bf16[256,3072]{1,0:T(8,128)(2,1)S(1)} %pad_maximum_fusion.1.refs_9_) | copy-start | bytes 4718596
  185.0 13.9 %copy-start.9 = (bf16[512,128]{1,0:T(8,128)(2,1)S(1)}, bf16[512,128]{1,0:T(8,128)(2,1)}, u32[]{:S(2)}) copy-start(bf16[512,128]{1,0:T(8,128)(2,1)} %copy-done.8) | copy-start | bytes 393220
  185.0 13.9 %copy-start.18 = (bf16[512,128]{1,0:T(8,128)(2,1)S(1)}, bf16[512,128]{1,0:T(8,128)(2,1)}, u32[]{:S(2)}) copy-start(bf16[512,128]{1,0:T(8,128)(2,1)} %copy-done.17) | copy-start | bytes 393220
  185.0 13.9 %copy-start.20 = (bf16[512,128]{1,0:T(8,128)(2,1)S(1)}, bf16[512,128]{1,0:T(8,128)(2,1)}, u32[]{:S(2)}) copy-start(bf16[512,128]{1,0:T(8,128)(2,1)} %copy-done.19) | copy-start | bytes 393220
  185.0 13.9 %copy-start.22 = (bf16[512,128]{1,0:T(8,128)(2,1)S(1)}, bf16[512,128]{1,0:T(8,128)(2,1)}, u32[]{:S(2)}) copy-start(bf16[512,128]{1,0:T(8,128)(2,1)} %copy-done.21) | copy-start | bytes 393220
  185.0 36.8 %collective-permute-start.11 = (bf16[256,3072]{1,0:T(8,128)(2,1)S(1)}, bf16[256,3072]{1,0:T(8,128)(2,1)S(1)}, u32[]{:S(2)}, u32[]{:S(2)}) collective-permute-start(bf16[256,3072]{1,0:T(8,128)(2,1)S(1)} %pad_maximum_fusion.1.refs_9_), channel_id=1, source_target_pairs={{0,1},{1,0},{2,3},{3,2},{4,5},{5,4},{6,7},{7,6},{8,9},{9,8},{10,11... | collective-permute-start | bytes 4718600 | tf_op jit(solution)/shard_map/ppermute | solution.py:237
  186.6 36.4 %collective-permute-start.12 = (bf16[256,3072]{1,0:T(8,128)(2,1)S(1)}, bf16[256,3072]{1,0:T(8,128)(2,1)S(1)}, u32[]{:S(2)}, u32[]{:S(2)}) collective-permute-start(bf16[256,3072]{1,0:T(8,128)(2,1)S(1)} %pad_maximum_fusion.1.refs_9_), channel_id=1, source_target_pairs={{0,2},{1,3},{2,0},{3,1},{4,6},{5,7},{6,4},{7,5},{8,10},{9,11},{10,... | collective-permute-start | bytes 4718600 | tf_op jit(solution)/shard_map/ppermute | solution.py:237
  188.1 35.9 %collective-permute-start.13 = (bf16[512,128]{1,0:T(8,128)(2,1)}, bf16[512,128]{1,0:T(8,128)(2,1)S(1)}, u32[]{:S(2)}, u32[]{:S(2)}) collective-permute-start(bf16[512,128]{1,0:T(8,128)(2,1)} %get-tuple-element.96), channel_id=1, source_target_pairs={{0,8},{4,12},{8,0},{12,4},{16,24},{20,28},{24,16},{28,20},{1,9},{5... | collective-permute-start | bytes 393224 | tf_op jit(solution)/shard_map/ppermute | solution.py:237
  189.8 40.1 %collective-permute-start.14 = (bf16[512,128]{1,0:T(8,128)(2,1)}, bf16[512,128]{1,0:T(8,128)(2,1)S(1)}, u32[]{:S(2)}, u32[]{:S(2)}) collective-permute-start(bf16[512,128]{1,0:T(8,128)(2,1)} %get-tuple-element.97), channel_id=1, source_target_pairs={{0,16},{4,20},{8,24},{12,28},{16,0},{20,4},{24,8},{28,12},{1,17},{... | collective-permute-start | bytes 393224 | tf_op jit(solution)/shard_map/ppermute | solution.py:237
  192.4 38.2 %collective-permute-start.15 = (bf16[512,128]{1,0:T(8,128)(2,1)}, bf16[512,128]{1,0:T(8,128)(2,1)}, u32[]{:S(2)}, u32[]{:S(2)}) collective-permute-start(bf16[512,128]{1,0:T(8,128)(2,1)} %get-tuple-element.98), channel_id=1, source_target_pairs={{0,24},{4,28},{8,16},{12,20},{16,8},{20,12},{24,0},{28,4},{1,25},{... | collective-permute-start | bytes 393224 | tf_op jit(solution)/shard_map/ppermute | solution.py:237
  198.9 31.0 %copy-start.11 = (bf16[512,128]{1,0:T(8,128)(2,1)}, bf16[512,128]{1,0:T(8,128)(2,1)S(1)}, u32[]{:S(2)}) copy-start(bf16[512,128]{1,0:T(8,128)(2,1)S(1)} %get-tuple-element.112) | copy-start | bytes 393220
  198.9 30.9 %copy-start.12 = (bf16[512,128]{1,0:T(8,128)(2,1)}, bf16[512,128]{1,0:T(8,128)(2,1)S(1)}, u32[]{:S(2)}) copy-start(bf16[512,128]{1,0:T(8,128)(2,1)S(1)} %get-tuple-element.111) | copy-start | bytes 393220
  199.0 30.9 %copy-start.13 = (bf16[512,128]{1,0:T(8,128)(2,1)}, bf16[512,128]{1,0:T(8,128)(2,1)S(1)}, u32[]{:S(2)}) copy-start(bf16[512,128]{1,0:T(8,128)(2,1)S(1)} %get-tuple-element.110) | copy-start | bytes 393220
  221.8 2.2 copy-start.3
  223.0 6.9 %copy-start.5 = (bf16[256,3072]{1,0:T(8,128)(2,1)}, bf16[256,3072]{1,0:T(8,128)(2,1)S(1)}, u32[]{:S(2)}) copy-start(bf16[256,3072]{1,0:T(8,128)(2,1)S(1)} %collective-permute-done.12.refs_11_) | copy-start | bytes 4718596
  224.0 5.9 %copy-start.23 = (bf16[512,128]{1,0:T(8,128)(2,1)}, bf16[512,128]{1,0:T(8,128)(2,1)S(1)}, u32[]{:S(2)}) copy-start(bf16[512,128]{1,0:T(8,128)(2,1)S(1)} %collective-permute-done.13) | copy-start | bytes 393220
  229.9 0.6 copy-start.24
  230.6 22.1 %copy-start.2 = (bf16[256,3072]{1,0:T(8,128)(2,1)S(1)}, bf16[256,3072]{1,0:T(8,128)(2,1)}, u32[]{:S(2)}) copy-start(bf16[256,3072]{1,0:T(8,128)(2,1)} %copy-done.1) | copy-start | bytes 4718596
  230.6 22.1 %copy-start.7 = (bf16[512,512]{1,0:T(8,128)(2,1)S(1)}, bf16[512,512]{1,0:T(8,128)(2,1)}, u32[]{:S(2)}) copy-start(bf16[512,512]{1,0:T(8,128)(2,1)} %pad_maximum_fusion.2.refs_0_) | copy-start | bytes 1572868
  230.6 32.6 %collective-permute-start.22 = (bf16[128,3072]{1,0:T(8,128)(2,1)}, bf16[128,3072]{1,0:T(8,128)(2,1)S(1)}, u32[]{:S(2)}, u32[]{:S(2)}) collective-permute-start(bf16[128,3072]{1,0:T(8,128)(2,1)} %slice.8), channel_id=1, source_target_pairs={{0,2},{1,3},{2,0},{3,1},{4,6},{5,7},{6,4},{7,5},{8,10},{9,11},{10,... | collective-permute-start | bytes 2359304 | tf_op jit(solution)/shard_map/ppermute | solution.py:237
  232.2 31.0 %collective-permute-start.23 = (bf16[128,3072]{1,0:T(8,128)(2,1)}, bf16[128,3072]{1,0:T(8,128)(2,1)S(1)}, u32[]{:S(2)}, u32[]{:S(2)}) collective-permute-start(bf16[128,3072]{1,0:T(8,128)(2,1)} %slice.9), channel_id=1, source_target_pairs={{0,1},{1,0},{2,3},{3,2},{4,5},{5,4},{6,7},{7,6},{8,9},{9,8},{10,11... | collective-permute-start | bytes 2359304 | tf_op jit(solution)/shard_map/ppermute | solution.py:237
  233.7 12.2 %collective-permute-start.16 = (bf16[512,128]{1,0:T(8,128)(2,1)}, bf16[512,128]{1,0:T(8,128)(2,1)S(1)}, u32[]{:S(2)}, u32[]{:S(2)}) collective-permute-start(bf16[512,128]{1,0:T(8,128)(2,1)} %copy-done.13), channel_id=1, source_target_pairs={{0,8},{4,12},{8,0},{12,4},{16,24},{20,28},{24,16},{28,20},{1,9},{5... | collective-permute-start | bytes 393224 | tf_op jit(solution)/shard_map/ppermute | solution.py:237
  236.0 12.2 %collective-permute-start.17 = (bf16[512,128]{1,0:T(8,128)(2,1)}, bf16[512,128]{1,0:T(8,128)(2,1)S(1)}, u32[]{:S(2)}, u32[]{:S(2)}) collective-permute-start(bf16[512,128]{1,0:T(8,128)(2,1)} %copy-done.12), channel_id=1, source_target_pairs={{0,16},{4,20},{8,24},{12,28},{16,0},{20,4},{24,8},{28,12},{1,17},{... | collective-permute-start | bytes 393224 | tf_op jit(solution)/shard_map/ppermute | solution.py:237
  236.0 12.2 %collective-permute-start.18 = (bf16[512,128]{1,0:T(8,128)(2,1)}, bf16[512,128]{1,0:T(8,128)(2,1)S(1)}, u32[]{:S(2)}, u32[]{:S(2)}) collective-permute-start(bf16[512,128]{1,0:T(8,128)(2,1)} %copy-done.11), channel_id=1, source_target_pairs={{0,24},{4,28},{8,16},{12,20},{16,8},{20,12},{24,0},{28,4},{1,25},{... | collective-permute-start | bytes 393224 | tf_op jit(solution)/shard_map/ppermute | solution.py:237
  248.2 14.9 %collective-permute-start.19 = (bf16[512,128]{1,0:T(8,128)(2,1)S(1)}, bf16[512,128]{1,0:T(8,128)(2,1)S(1)}, u32[]{:S(2)}, u32[]{:S(2)}) collective-permute-start(bf16[512,128]{1,0:T(8,128)(2,1)S(1)} %get-tuple-element.123), channel_id=1, source_target_pairs={{0,8},{4,12},{8,0},{12,4},{16,24},{20,28},{24,16},{28,20},{1,9},{5... | collective-permute-start | bytes 393224 | tf_op jit(solution)/shard_map/ppermute | solution.py:237
  250.3 12.9 %collective-permute-start.20 = (bf16[512,128]{1,0:T(8,128)(2,1)S(1)}, bf16[512,128]{1,0:T(8,128)(2,1)S(1)}, u32[]{:S(2)}, u32[]{:S(2)}) collective-permute-start(bf16[512,128]{1,0:T(8,128)(2,1)S(1)} %get-tuple-element.124), channel_id=1, source_target_pairs={{0,16},{4,20},{8,24},{12,28},{16,0},{20,4},{24,8},{28,12},{1,17},{... | collective-permute-start | bytes 393224 | tf_op jit(solution)/shard_map/ppermute | solution.py:237
  250.5 12.7 %collective-permute-start.21 = (bf16[512,128]{1,0:T(8,128)(2,1)S(1)}, bf16[512,128]{1,0:T(8,128)(2,1)S(1)}, u32[]{:S(2)}, u32[]{:S(2)}) collective-permute-start(bf16[512,128]{1,0:T(8,128)(2,1)S(1)} %get-tuple-element.125), channel_id=1, source_target_pairs={{0,24},{4,28},{8,16},{12,20},{16,8},{20,12},{24,0},{28,4},{1,25},{... | collective-permute-start | bytes 393224 | tf_op jit(solution)/shard_map/ppermute | solution.py:237
  252.6 1.4 copy-start.4
  254.0 1.4 copy-start.6
  264.9 3.5 %collective-permute-start.24 = (bf16[256,3072]{1,0:T(8,128)(2,1)S(1)}, bf16[256,3072]{1,0:T(8,128)(2,1)S(1)}, u32[]{:S(2)}, u32[]{:S(2)}) collective-permute-start(bf16[256,3072]{1,0:T(8,128)(2,1)S(1)} %convert_element_type.9), channel_id=1, source_target_pairs={{0,4},{4,0},{8,12},{12,8},{16,20},{20,16},{24,28},{28,24},{1,5},{5... | collective-permute-start | bytes 4718600 | tf_op jit(solution)/shard_map/ppermute | solution.py:237
